TPU v7x, 32 devices: a whole 2x2x4 slice. The times are simulated.
32 devices in a mesh: ctx: 8 (over z, y), ch: 4 (over x, core).
Axes of the slice: x: 2, y: 2, z: 4, core: 2. Of those that a mesh axis runs over, the one named last changes fastest.
Arguments:
- features: bfloat16 [1536, 4096], P('ctx', 'ch'), may hold values from -6 to 6
- w_in: bfloat16 [4096, 3, 2048], P('ctx', None, 'ch'), may hold values from -0.09375 to 0.09375
- short_filter: float32 [3, 3, 2048], P(None, None, 'ch'), may hold values from -3 to 3
- filter_spectrum: float32 [2, 1536, 2048], P(None, 'ctx', 'ch'), may hold values from -6 to 6
- out_grad: bfloat16 [1536, 4096], P('ctx'), may hold values from -0.059814453 to 0.059814453
Outputs:
- gated: bfloat16 [1536, 2048], P('ctx', 'ch')
- w_out_grad: float32 [4096, 2048], P('ctx', 'ch')
All inputs are finite; a program needn't handle non-finite values.
Results may differ from a plain program's by a relative error of at most 0.0065.
Values may be sent and summed in bfloat16 or wider, within the bound.
No kernel may reach another device: no remote copies, remote signals or barrier semaphores. Data moves between devices by JAX's collectives and lax.ppermute only.
A program may use at most 128 MiB of HBM per device.

v0:
```python
import math

import jax
import jax.numpy as jnp
from jax import lax
from jax.sharding import PartitionSpec as P

TWO_PI = 2.0 * math.pi


def from_behind(value, axis, by):
    count = lax.axis_size(axis)
    pairs = [(i, i + by) for i in range(count) if 0 <= i + by < count]
    return lax.ppermute(value, axis, pairs)


def product(left, right):
    return jnp.dot(left, right, precision=lax.Precision.HIGHEST, preferred_element_type=jnp.float32)


def reverse_bits(values, count):
    result = jnp.zeros_like(values)
    for level in range(count):
        result = result | (values >> level & 1) << count - 1 - level
    return result


def phase_tables(phase, period):
    angle = TWO_PI / period * phase.astype(jnp.float32)
    return (jnp.cos(angle), jnp.sin(angle))


def on_device(features, w_in, short_filter, filter_spectrum, out_grad):
    rows = features.shape[0]
    width = w_in.shape[2]
    devices = lax.axis_size("ctx")
    sections = devices.bit_length() - 1
    total = rows * devices
    place = lax.axis_index("ctx")
    whole = lax.all_gather(features, "ch", axis=1, tiled=True)
    flat_width = 3 * width
    piece = lax.all_gather(w_in, "ctx", axis=0, tiled=True)
    columns = whole
    projected = jnp.dot(
        columns, piece.reshape(piece.shape[0], flat_width), preferred_element_type=jnp.float32
    )
    projected = projected.astype(jnp.bfloat16).reshape(rows, 3, width)
    earlier = from_behind(projected[rows - 2 :], "ctx", 1)
    extended = jnp.concatenate([earlier, projected], axis=0).astype(jnp.float32)
    mixed = (
        short_filter[0] * extended[2:]
        + short_filter[1] * extended[1 : rows + 1]
        + short_filter[2] * extended[:rows]
    )
    query = mixed[:, 0]
    signal = mixed[:, 1] * mixed[:, 2]
    local_pos = lax.broadcasted_iota(jnp.int32, (rows, 1), 0)
    grid = lax.broadcasted_iota(jnp.int32, (rows, rows), 0) * lax.broadcasted_iota(
        jnp.int32, (rows, rows), 1
    )
    local_cos, local_sin = phase_tables(grid % rows, rows)
    block = rows // devices
    order = reverse_bits(lax.broadcasted_iota(jnp.int32, (devices, 1), 0), sections)
    across = order * lax.broadcasted_iota(jnp.int32, (1, devices), 1)
    across_cos, across_sin = phase_tables(across % devices, devices)
    positions = place * block + lax.broadcasted_iota(jnp.int32, (1, block), 1)
    turn_cos, turn_sin = phase_tables(order * positions % total, total)
    turn_cos = turn_cos[:, :, None]
    turn_sin = turn_sin[:, :, None]
    pieces = lax.all_to_all(
        signal.reshape(devices, block, width), "ctx", split_axis=0, concat_axis=0, tiled=True
    )
    flat = pieces.reshape(devices, -1)
    real_part = product(across_cos, flat).reshape(pieces.shape)
    imag_part = -product(across_sin, flat).reshape(pieces.shape)
    columns = jnp.stack(
        [real_part * turn_cos + imag_part * turn_sin, imag_part * turn_cos - real_part * turn_sin]
    )
    data = lax.all_to_all(columns, "ctx", split_axis=1, concat_axis=2, tiled=True).reshape(
        2, rows, width
    )
    spec_real = product(local_cos, data[0]) + product(local_sin, data[1])
    spec_imag = product(local_cos, data[1]) - product(local_sin, data[0])
    prod_real = spec_real * filter_spectrum[0] - spec_imag * filter_spectrum[1]
    prod_imag = spec_real * filter_spectrum[1] + spec_imag * filter_spectrum[0]
    back_real = (product(local_cos, prod_real) - product(local_sin, prod_imag)) / rows
    back_imag = (product(local_cos, prod_imag) + product(local_sin, prod_real)) / rows
    own_class = reverse_bits(place, sections)
    shift_cos, shift_sin = phase_tables(own_class * local_pos % total, total)
    turned_real = back_real * shift_cos - back_imag * shift_sin
    turned_imag = back_imag * shift_cos + back_real * shift_sin
    rows_data = jnp.stack([turned_real, turned_imag]).reshape(2, devices, block, width)
    back_cos = across_cos.T
    back_sin = across_sin.T
    pieces = lax.all_to_all(rows_data, "ctx", split_axis=1, concat_axis=1, tiled=True)
    shape = pieces.shape[1:]
    flat_real = pieces[0].reshape(devices, -1)
    flat_imag = pieces[1].reshape(devices, -1)
    partial_rows = (
        (product(back_cos, flat_real) - product(back_sin, flat_imag)) / devices
    ).reshape(shape)
    convolved = lax.all_to_all(
        partial_rows, "ctx", split_axis=0, concat_axis=1, tiled=True
    ).reshape(rows, width)
    gated = (query * convolved).astype(jnp.bfloat16)
    w_out_grad = lax.psum_scatter(
        lax.dot_general(
            out_grad, gated, (((0,), (0,)), ((), ())), preferred_element_type=jnp.float32
        ),
        "ctx",
        scatter_dimension=0,
        tiled=True,
    )
    return (gated, w_out_grad)


def solution(mesh):
    in_specs = (
        P("ctx", "ch"),
        P("ctx", None, "ch"),
        P(None, None, "ch"),
        P(None, "ctx", "ch"),
        P("ctx", None),
    )
    out_specs = (P("ctx", "ch"), P("ctx", "ch"))
    return jax.shard_map(
        on_device, mesh=mesh, in_specs=in_specs, out_specs=out_specs, check_vma=False
    )
```

profile of v0, /device:TPU:0, one launch (start us, length us, event | category | flops | bytes accessed | tf_op | source)
XLA Modules:
  0.0 482.1 jit_solution(704376275738526798)
XLA Ops:
  7.2 0.0 all-gather.3.cloned.1.call-start
  7.2 0.7 all-gather.3.cloned.1.call-update
  7.9 0.0 all-gather.5.cloned.1.call-start
  8.0 2.7 copy.16
  10.6 21.3 %all-gather.3.cloned.1.call-done = bf16[192,4096]{1,0:T(8,128)(2,1)} async-done(((bf16[192,1024]{1,0:T(8,128)(2,1)}), bf16[192,4096]{1,0:T(8,128)(2,1)}) %all-gather.3.cloned.1.call-update) | async-done | bytes 1572880 | tf_op jit(solution)/shard_map/all_gather | solution.py:40
  32.0 178.7 %all-gather.5.cloned.1.call-done = bf16[4096,3,512]{0,2,1:T(8,128)(2,1)} async-done(((bf16[512,3,512]{0,2,1:T(8,128)(2,1)}), bf16[4096,3,512]{0,2,1:T(8,128)(2,1)}) %all-gather.5.cloned.1.call-update) | async-done | bytes 12582928 | tf_op jit(solution)/shard_map/all_gather | solution.py:42
  210.6 9.3 %convolution_convert_fusion = bf16[192,1536]{1,0:T(8,128)(2,1)S(1)} fusion(bf16[192,4096]{1,0:T(8,128)(2,1)} %all-gather.3.cloned.1.call-done, bf16[4096,1536]{0,1:T(8,128)(2,1)} %bitcast.100), kind=kOutput, calls=%fused_computation.3 | convolution fusion | flops 2416214016 | bytes 14745600 | tf_op jit(solution)/shard_map/dot_general | solution.py:44
  220.0 3.4 collective-permute-start
  223.4 0.4 reshape.172
  223.8 0.9 collective-permute-done
  224.7 0.5 maximum_convert_fusion
  225.2 0.5 fusion.1
  225.7 0.8 slice_multiply_fusion.3
  226.5 0.8 copy.25
  227.3 4.5 all-to-all-start
  231.8 0.1 fusion.54
  231.9 10.5 %all-to-all-done = f32[8,24,512]{2,1,0:T(8,128)S(1)} async-done(((f32[8,24,512]{2,1,0:T(8,128)}), f32[8,24,512]{2,1,0:T(8,128)S(1)}, u32[]{:S(2)}, u32[]{:S(2)}) %all-to-all-start) | async-done | bytes 393248 | tf_op jit(solution)/shard_map/all_to_all | solution.py:70
  242.4 0.7 convolution_negate_fusion
  243.1 0.8 add_bitcast_fusion
  243.9 0.1 pad_maximum_fusion
  244.0 1.3 copy.17
  245.3 3.7 all-to-all-start.1
  249.0 0.2 reduce-scatter.2.cloned.1.call-start
  249.2 0.1 sine_multiply_fusion
  249.3 19.3 %all-to-all-done.1 = f32[2,8,24,512]{3,2,0,1:T(8,128)S(1)} async-done(((f32[2,8,24,512]{3,2,0,1:T(8,128)}), f32[2,8,24,512]{3,2,0,1:T(8,128)S(1)}, u32[]{:S(2)}, u32[]{:S(2)}) %all-to-all-start.1) | async-done | bytes 786464 | tf_op jit(solution)/shard_map/all_to_all | solution.py:79
  268.6 0.1 fusion.122
  268.7 1.3 fusion.16
  270.0 1.3 fusion.18
  271.3 1.3 convolution_subtract_fusion.2
  272.6 1.4 fusion.5
  274.0 1.3 fusion.14
  275.3 1.3 fusion.12
  276.5 1.3 convolution_subtract_fusion.1
  277.8 1.4 multiply_subtract_fusion
  279.2 0.1 pad_maximum_fusion.1
  279.3 23.6 %all_to_all.28 = f32[2,8,24,512]{3,2,0,1:T(8,128)S(1)} all-to-all(f32[2,8,24,512]{3,2,0,1:T(8,128)S(1)} %pad_maximum_fusion.1), channel_id=1, replica_groups=mesh['ctx'=8,'ch'=4] {'ctx'}, dimensions={1} | all-to-all | bytes 1572864 | tf_op jit(solution)/shard_map/all_to_all | solution.py:95
  302.9 0.1 slice_bitcast_fusion
  303.0 0.2 copy.29
  303.2 0.6 fusion.67
  303.9 0.2 copy.30
  304.1 0.6 fusion
  304.8 0.2 copy.22
  305.0 15.2 %all_to_all.29 = f32[8,24,512]{2,1,0:T(8,128)S(1)} all-to-all(f32[8,24,512]{2,1,0:T(8,128)S(1)} %copy.22), channel_id=1, replica_groups=mesh['ctx'=8,'ch'=4] {'ctx'}, dimensions={0} | all-to-all | bytes 786432 | tf_op jit(solution)/shard_map/all_to_all | solution.py:102
  320.2 0.1 fusion.3
  320.3 4.5 convolution_bitcast_fusion
  324.8 0.0 reduce-scatter.2.cloned.1.call-update
  324.9 148.2 %reduce-scatter.2.cloned.1.call-done = f32[512,512]{0,1:T(8,128)} async-done(((f32[4096,512]{0,1:T(8,128)}), f32[512,512]{0,1:T(8,128)}) %reduce-scatter.2.cloned.1.call-update) | async-done | bytes 1048592 | tf_op jit(solution)/shard_map/reduce_scatter | solution.py:106
  473.1 2.5 copy.23
  (14 shorter events, 0.1 us)
Async XLA Ops:
  7.2 313.1 %copy-start = (bf16[192,4096]{1,0:T(8,128)(2,1)S(1)}, bf16[192,4096]{1,0:T(8,128)(2,1)}, u32[]{:S(2)}) copy-start(bf16[192,4096]{1,0:T(8,128)(2,1)} %param.9) | copy-start | bytes 4718596
  7.2 24.8 %all-gather.3.cloned.1.call-start = ((), (), s32[]{:S(2)}) async-start(), calls=%async_computation.5 | async-start | bytes 1966080 | tf_op jit(solution)/shard_map/all_gather | solution.py:40
  7.9 202.7 %all-gather.5.cloned.1.call-start = ((), (), s32[]{:S(2)}) async-start(), calls=%async_computation.6 | async-start | bytes 14155776 | tf_op jit(solution)/shard_map/all_gather | solution.py:42
  210.6 12.8 %copy-start.3 = (f32[3,3,512]{2,1,0:T(4,128)S(1)}, f32[3,3,512]{2,1,0:T(4,128)}, u32[]{:S(2)}) copy-start(f32[3,3,512]{2,1,0:T(4,128)} %param.7) | copy-start | bytes 55300
  220.0 4.7 collective-permute-start
  227.3 15.2 %all-to-all-start = ((f32[8,24,512]{2,1,0:T(8,128)}), f32[8,24,512]{2,1,0:T(8,128)S(1)}, u32[]{:S(2)}, u32[]{:S(2)}) async-start(f32[8,24,512]{2,1,0:T(8,128)} %bitcast.25), calls=%async_computation | async-start | bytes 786432 | tf_op jit(solution)/shard_map/all_to_all | solution.py:70
  245.3 23.3 %all-to-all-start.1 = ((f32[2,8,24,512]{3,2,0,1:T(8,128)}), f32[2,8,24,512]{3,2,0,1:T(8,128)S(1)}, u32[]{:S(2)}, u32[]{:S(2)}) async-start(f32[2,8,24,512]{3,2,0,1:T(8,128)} %copy.17), calls=%async_computation.1 | async-start | bytes 1572864 | tf_op jit(solution)/shard_map/all_to_all | solution.py:79
  249.0 224.0 %reduce-scatter.2.cloned.1.call-start = ((), (), s32[]{:S(2)}) async-start(), calls=%async_computation.7 | async-start | bytes 9437184 | tf_op jit(solution)/shard_map/reduce_scatter | solution.py:106
  268.7 3.9 copy-start.2
  320.3 4.6 copy-start.1
Sparse Core Ops, SparseCore 0:
  9.6 22.3 all-gather.2
  34.0 176.5 all-gather.4
  325.0 148.0 reduce-scatter.1
where the time goes:
time: 483 us; the launch traced here: 482 us
  waiting for transfers between devices  380 us (79%)
  blocking collectives  38.8 us (8%)
  matrix products  27.1 us (6%)
  between operations  14 us (3%)
  starting transfers between devices  11.9 us (2%)
  local copies, waits for them, and re-layouts  8.6 us (2%)
    all_gather x1, waiting for transfers between devices, on_device(): piece = lax.all_gather(w_in, 'ctx', axis=0, tiled=True)  179 us
    reduce_scatter x1, waiting for transfers between devices, on_device(): lax.psum_scatter(lax.dot_general(out_grad, gated, (((0,), (0,)), ((), ())...  148 us
    all_to_all x1, blocking collectives, on_device(): lax.all_to_all(rows_data, 'ctx', split_axis=1, concat_axis=1, tiled=True)  23.6 us
    all_gather x1, waiting for transfers between devices, on_device(): whole = lax.all_gather(features, 'ch', axis=1, tiled=True)  21.3 us
    all_to_all x1, waiting for transfers between devices, on_device(): lax.all_to_all(columns, 'ctx', split_axis=1, concat_axis=2, tiled=True)  19.3 us
    all_to_all x1, blocking collectives, on_device(): lax.all_to_all(partial_rows, 'ctx', split_axis=0, concat_axis=1, tiled=True)  15.2 us
    dot_general x12, matrix products, product(): jnp.dot(left, right, precision=lax.Precision.HIGHEST, preferred_element_t...  13.3 us
    all_to_all x1, waiting for transfers between devices, on_device(): lax.all_to_all(signal.reshape(devices, block, width), 'ctx', split_axis=0...  10.5 us
  transfers between devices with their start and end apart: 6, of which 6 were waited for; matrix products, arithmetic and copies ran while one was open for 1% of the time, Pallas kernels for 0%

commit v1 on v0

v1 whole, which is shorter than its diff:
```python
import math

import jax
import jax.numpy as jnp
from jax import lax
from jax.sharding import PartitionSpec as P

TWO_PI = 2.0 * math.pi
BOTH = ("ctx", "ch")


def product(spec, left, right):
    return jnp.einsum(
        spec, left, right, precision=lax.Precision.HIGHEST, preferred_element_type=jnp.float32
    )


def reverse_bits(values, count):
    result = jnp.zeros_like(values)
    for level in range(count):
        result = result | (values >> level & 1) << count - 1 - level
    return result


def phase_tables(phase, period):
    angle = TWO_PI / period * phase.astype(jnp.float32)
    return (jnp.cos(angle), jnp.sin(angle))


def gather_pairs(value, n, place):
    pairs = n // 2
    odd = place % 2
    near = [value]
    for shift in range(1, pairs):
        hops = [(i, (i // 2 + shift) % pairs * 2 + i % 2) for i in range(n)]
        near.append(lax.ppermute(value, "ctx", hops))
    flips = [(i, i ^ 1) for i in range(n)]
    found = []
    for shift in range(pairs):
        other = lax.ppermute(near[shift], "ctx", flips)
        low = jnp.where(odd == 0, near[shift], other)
        high = jnp.where(odd == 0, other, near[shift])
        found.append(((place // 2 - shift) % pairs, low, high))
    return found


def on_device(features, w_in, short_filter, filter_spectrum, out_grad):
    n = lax.axis_size("ctx")
    m = lax.axis_size("ch")
    place = lax.axis_index("ctx")
    column = lax.axis_index("ch")
    rows, depth = features.shape
    total = rows * n
    share = n // m
    block_depth = w_in.shape[0]
    width = w_in.shape[2]
    own = width // n
    sections = n.bit_length() - 1

    whole = jnp.zeros((n // 2, 2, rows, depth), features.dtype)
    for index, low, high in gather_pairs(features, n, place):
        whole = lax.dynamic_update_slice(whole, jnp.stack([low, high])[None], (index, 0, 0, 0))
    whole = whole.reshape(total, depth)

    turned = w_in.reshape(block_depth, 3, n, own).transpose(2, 1, 3, 0)
    sender = place % share * m + column
    weights = jnp.zeros((n, 3, own, block_depth), w_in.dtype)
    for step in range(n):
        hops = []
        for i in range(n):
            for j in range(m):
                hops.append((i * m + j, (i % share * m + j + step) % n * m + i // share))
        piece = lax.dynamic_index_in_dim(turned, (sender + step) % n, 0)
        piece = lax.ppermute(piece, BOTH, hops)
        weights = lax.dynamic_update_slice(weights, piece, ((place - step) % n, 0, 0, 0))
    weights = weights.reshape(share, m * 3 * own, block_depth).transpose(1, 0, 2)
    weights = weights.reshape(m * 3 * own, depth)

    partial = lax.dot_general(
        weights, whole, (((1,), (1,)), ((), ())), preferred_element_type=jnp.float32
    )
    partial = partial.reshape(m, 3 * own, total)
    bits = m.bit_length() - 1
    for bit in range(bits):
        mine = column >> bit & 1
        halves = partial.reshape(-1, 2, 3 * own, total)
        keep = lax.dynamic_index_in_dim(halves, mine, 1, keepdims=False)
        send = lax.dynamic_index_in_dim(halves, 1 - mine, 1, keepdims=False)
        if bit == bits - 1:
            send = send.astype(jnp.bfloat16)
        flips = [(j, j ^ 1 << bit) for j in range(m)]
        partial = keep + lax.ppermute(send, "ch", flips).astype(jnp.float32)
    projected = partial.reshape(3, own, total).astype(jnp.bfloat16).astype(jnp.float32)

    taps = lax.dynamic_slice_in_dim(short_filter, place * own, own, 2)[:, :, :, None]
    padded = jnp.pad(projected, ((0, 0), (0, 0), (2, 0)))
    mixed = (
        taps[0] * projected + taps[1] * padded[:, :, 1 : total + 1] + taps[2] * padded[:, :, :total]
    )
    query = mixed[0]
    signal = (mixed[1] * mixed[2]).reshape(own, n, rows)

    response = lax.all_to_all(
        filter_spectrum.reshape(2, rows, n, own).transpose(2, 3, 0, 1),
        "ctx", split_axis=0, concat_axis=0, tiled=True,
    )
    grid = lax.broadcasted_iota(jnp.int32, (rows, rows), 0) * lax.broadcasted_iota(
        jnp.int32, (rows, rows), 1
    )
    local_cos, local_sin = phase_tables(grid % rows, rows)
    order = reverse_bits(lax.broadcasted_iota(jnp.int32, (n, 1), 0), sections)
    across = order * lax.broadcasted_iota(jnp.int32, (1, n), 1)
    across_cos, across_sin = phase_tables(across % n, n)
    turn = order * lax.broadcasted_iota(jnp.int32, (1, rows), 1)
    turn_cos, turn_sin = phase_tables(turn % total, total)
    turn_cos, turn_sin = turn_cos[:, None], turn_sin[:, None]
    real = product("rn,cnt->rct", across_cos, signal)
    imag = -product("rn,cnt->rct", across_sin, signal)
    real, imag = real * turn_cos + imag * turn_sin, imag * turn_cos - real * turn_sin
    spec_real = product("rct,tq->rcq", real, local_cos) + product("rct,tq->rcq", imag, local_sin)
    spec_imag = product("rct,tq->rcq", imag, local_cos) - product("rct,tq->rcq", real, local_sin)
    res_real, res_imag = response[:, :, 0], response[:, :, 1]
    prod_real = spec_real * res_real - spec_imag * res_imag
    prod_imag = spec_real * res_imag + spec_imag * res_real
    back_real = product("rcq,qt->rct", prod_real, local_cos) - product(
        "rcq,qt->rct", prod_imag, local_sin
    )
    back_imag = product("rcq,qt->rct", prod_imag, local_cos) + product(
        "rcq,qt->rct", prod_real, local_sin
    )
    back_real, back_imag = (
        back_real * turn_cos - back_imag * turn_sin,
        back_imag * turn_cos + back_real * turn_sin,
    )
    convolved = (
        product("rn,rct->cnt", across_cos, back_real)
        - product("rn,rct->cnt", across_sin, back_imag)
    ) / total
    gated = (query * convolved.reshape(own, total)).astype(jnp.bfloat16)

    out_rows = out_grad.shape[1] // n
    part = out_rows // m
    mine = lax.dynamic_index_in_dim(
        out_grad.reshape(rows, n, m, part), column, 2, keepdims=False
    )
    mine = lax.all_to_all(mine, "ctx", split_axis=1, concat_axis=0, tiled=True)
    grads = lax.all_gather(mine.reshape(total, part), "ch", axis=1, tiled=True)

    every = jnp.zeros((n // 2, 2, own, total), jnp.bfloat16)
    for index, low, high in gather_pairs(gated, n, place):
        every = lax.dynamic_update_slice(every, jnp.stack([low, high])[None], (index, 0, 0, 0))
    every = every.reshape(width, total)
    w_out_grad = lax.dot_general(
        grads, every, (((0,), (1,)), ((), ())), preferred_element_type=jnp.float32
    )
    out = lax.dynamic_slice_in_dim(every, place * rows, rows, 1).T
    return (out, w_out_grad)


def solution(mesh):
    in_specs = (
        P("ctx", "ch"),
        P("ctx", None, "ch"),
        P(None, None, "ch"),
        P(None, "ctx", "ch"),
        P("ctx", None),
    )
    out_specs = (P("ctx", "ch"), P("ctx", "ch"))
    return jax.shard_map(
        on_device, mesh=mesh, in_specs=in_specs, out_specs=out_specs, check_vma=False
    )
```

time: 483 us -> 273 us (0.57)
  waiting for transfers between devices: 380 us -> 93.1 us
  starting transfers between devices: 11.9 us -> 110 us
  blocking collectives: 38.8 us -> 0 us
  local copies, waits for them, and re-layouts: 8.6 us -> 20.2 us
  other arithmetic: 2.13 us -> 9.85 us
    all_gather x2 -> x1, waiting for transfers between devices: 200 us -> 0.01 us  [on_device(): grads = lax.all_gather(mine.reshape(total, part), 'ch', axis=1, tiled=True)]
    reduce_scatter x1 -> x0, waiting for transfers between devices: 148 us -> none  [on_device(): lax.psum_scatter(lax.dot_general(out_grad, gated, (((0,), (0,)), ((), ())...]
    ppermute x1 -> x24, starting transfers between devices: 3.36 us -> 102 us  [the longest x8 62.5 us: on_device(): piece = lax.ppermute(piece, BOTH, hops)]
    ppermute x1 -> x24, waiting for transfers between devices: 0.88 us -> 83.8 us  [the longest x8 47 us: on_device(): piece = lax.ppermute(piece, BOTH, hops)]
    all_to_all x2 -> x0, blocking collectives: 38.8 us -> none  [the longest x1 23.6 us: on_device(): lax.all_to_all(rows_data, 'ctx', split_axis=1, concat_axis=1, tiled=True)]
    all_to_all x2, waiting for transfers between devices: 29.8 us -> 9.27 us  [the longest x1 9.27 us: on_device(): lax.all_to_all(filter_spectrum.reshape(2, rows, n, own).transpose(2, 3, 0...]
  transfers between devices with their start and end apart: 6 -> 27, of which waited for: 6 -> 16; matrix products, arithmetic and copies ran while one was open for 1% -> 14% of each run, Pallas kernels for 0% -> 0%
where the time goes in v1:
time: 273 us; the launch traced here: 272 us
  starting transfers between devices  110 us (40%)
  waiting for transfers between devices  93.1 us (34%)
  matrix products  24.4 us (9%)
  local copies, waits for them, and re-layouts  20.2 us (7%)
  between operations  14.7 us (5%)
  other arithmetic  9.85 us (4%)
    ppermute x8, starting transfers between devices, on_device(): piece = lax.ppermute(piece, BOTH, hops)  62.5 us
    ppermute x8, waiting for transfers between devices, on_device(): piece = lax.ppermute(piece, BOTH, hops)  47 us
    ppermute x8, waiting for transfers between devices, gather_pairs(): other = lax.ppermute(near[shift], 'ctx', flips)  21.2 us
    dot_general x12, matrix products, product(): jnp.einsum(spec, left, right, precision=lax.Precision.HIGHEST, preferred_...  18.3 us
    ppermute x8, starting transfers between devices, gather_pairs(): other = lax.ppermute(near[shift], 'ctx', flips)  15.6 us
    ppermute x2, starting transfers between devices, on_device(): partial = keep + lax.ppermute(send, 'ch', flips).astype(jnp.float32)  14.3 us
    ppermute x6, waiting for transfers between devices, gather_pairs(): near.append(lax.ppermute(value, 'ctx', hops))  11.3 us
    all_to_all x1, waiting for transfers between devices, on_device(): lax.all_to_all(filter_spectrum.reshape(2, rows, n, own).transpose(2, 3, 0...  9.27 us
  transfers between devices with their start and end apart: 27, of which 16 were waited for; matrix products, arithmetic and copies ran while one was open for 14% of the time, Pallas kernels for 0%

profile of v1, /device:TPU:0, one launch (start us, length us, event | category | flops | bytes accessed | tf_op | source)
XLA Modules:
  0.0 271.9 jit_solution(3095907087095984943)
XLA Ops:
  7.3 1.7 copy.91
  10.1 6.7 %collective-permute-start.8 = (bf16[192,1024]{1,0:T(8,128)(2,1)S(1)}, bf16[192,1024]{1,0:T(8,128)(2,1)}, u32[]{:S(2)}, u32[]{:S(2)}) collective-permute-start(bf16[192,1024]{1,0:T(8,128)(2,1)S(1)} %copy-done.1), channel_id=1, source_target_pairs={{0,4},{4,0},{8,12},{12,8},{16,20},{20,16},{24,28},{28,24},{1,5},{5... | collective-permute-start | bytes 1179656 | tf_op jit(solution)/shard_map/ppermute | solution.py:40
  16.7 2.4 collective-permute-start.11
  19.1 2.0 collective-permute-start.13
  21.2 2.6 collective-permute-start.1
  24.0 6.0 %collective-permute-done.1 = bf16[1,3,64,512]{3,2,0,1:T(8,128)(2,1)S(1)} collective-permute-done((bf16[1,3,64,512]{3,2,0,1:T(8,128)(2,1)S(1)}, bf16[1,3,64,512]{3,2,0,1:T(8,128)(2,1)S(1)}, u32[]{:S(2)}, u32[]{:S(2)}) %collective-permute-start.1) | collective-permute-done | bytes 196640 | tf_op jit(solution)/shard_map/ppermute | solution.py:74
  30.1 29.2 %collective-permute-start.2 = (bf16[1,3,64,512]{3,2,0,1:T(8,128)(2,1)S(1)}, bf16[1,3,64,512]{3,2,0,1:T(8,128)(2,1)S(1)}, u32[]{:S(2)}, u32[]{:S(2)}) collective-permute-start(bf16[1,3,64,512]{3,2,0,1:T(8,128)(2,1)S(1)} %get-tuple-element.17), channel_id=1, source_target_pairs={{0,8},{1,12},{2,16},{3,20},{4,24},{5,28},{6,0},{7,4},{8,9},{9,13},... | collective-permute-start | bytes 589832 | tf_op jit(solution)/shard_map/ppermute | solution.py:74
  59.3 19.0 %collective-permute-done.2 = bf16[1,3,64,512]{3,2,0,1:T(8,128)(2,1)S(1)} collective-permute-done((bf16[1,3,64,512]{3,2,0,1:T(8,128)(2,1)S(1)}, bf16[1,3,64,512]{3,2,0,1:T(8,128)(2,1)S(1)}, u32[]{:S(2)}, u32[]{:S(2)}) %collective-permute-start.2) | collective-permute-done | bytes 196640 | tf_op jit(solution)/shard_map/ppermute | solution.py:74
  78.4 3.7 %collective-permute-start.3 = (bf16[1,3,64,512]{3,2,0,1:T(8,128)(2,1)S(1)}, bf16[1,3,64,512]{3,2,0,1:T(8,128)(2,1)S(1)}, u32[]{:S(2)}, u32[]{:S(2)}) collective-permute-start(bf16[1,3,64,512]{3,2,0,1:T(8,128)(2,1)S(1)} %get-tuple-element.16), channel_id=1, source_target_pairs={{0,12},{1,16},{2,20},{3,24},{4,28},{5,0},{6,4},{7,8},{8,13},{9,17}... | collective-permute-start | bytes 589832 | tf_op jit(solution)/shard_map/ppermute | solution.py:74
  82.1 5.3 %collective-permute-done.3 = bf16[1,3,64,512]{3,2,0,1:T(8,128)(2,1)S(1)} collective-permute-done((bf16[1,3,64,512]{3,2,0,1:T(8,128)(2,1)S(1)}, bf16[1,3,64,512]{3,2,0,1:T(8,128)(2,1)S(1)}, u32[]{:S(2)}, u32[]{:S(2)}) %collective-permute-start.3) | collective-permute-done | bytes 196640 | tf_op jit(solution)/shard_map/ppermute | solution.py:74
  87.4 2.8 %collective-permute-start.4 = (bf16[1,3,64,512]{3,2,0,1:T(8,128)(2,1)S(1)}, bf16[1,3,64,512]{3,2,0,1:T(8,128)(2,1)S(1)}, u32[]{:S(2)}, u32[]{:S(2)}) collective-permute-start(bf16[1,3,64,512]{3,2,0,1:T(8,128)(2,1)S(1)} %get-tuple-element.15), channel_id=1, source_target_pairs={{0,16},{1,20},{2,24},{3,28},{4,0},{5,4},{6,8},{7,12},{8,17},{9,21}... | collective-permute-start | bytes 589832 | tf_op jit(solution)/shard_map/ppermute | solution.py:74
  90.2 4.3 %collective-permute-done.4 = bf16[1,3,64,512]{3,2,0,1:T(8,128)(2,1)S(1)} collective-permute-done((bf16[1,3,64,512]{3,2,0,1:T(8,128)(2,1)S(1)}, bf16[1,3,64,512]{3,2,0,1:T(8,128)(2,1)S(1)}, u32[]{:S(2)}, u32[]{:S(2)}) %collective-permute-start.4) | collective-permute-done | bytes 196640 | tf_op jit(solution)/shard_map/ppermute | solution.py:74
  94.5 8.9 %collective-permute-start.5 = (bf16[1,3,64,512]{3,2,0,1:T(8,128)(2,1)S(1)}, bf16[1,3,64,512]{3,2,0,1:T(8,128)(2,1)S(1)}, u32[]{:S(2)}, u32[]{:S(2)}) collective-permute-start(bf16[1,3,64,512]{3,2,0,1:T(8,128)(2,1)S(1)} %get-tuple-element.14), channel_id=1, source_target_pairs={{0,20},{1,24},{2,28},{3,0},{4,4},{5,8},{6,12},{7,16},{8,21},{9,25}... | collective-permute-start | bytes 589832 | tf_op jit(solution)/shard_map/ppermute | solution.py:74
  103.4 3.9 %collective-permute-done.5 = bf16[1,3,64,512]{3,2,0,1:T(8,128)(2,1)S(1)} collective-permute-done((bf16[1,3,64,512]{3,2,0,1:T(8,128)(2,1)S(1)}, bf16[1,3,64,512]{3,2,0,1:T(8,128)(2,1)S(1)}, u32[]{:S(2)}, u32[]{:S(2)}) %collective-permute-start.5) | collective-permute-done | bytes 196640 | tf_op jit(solution)/shard_map/ppermute | solution.py:74
  107.3 7.7 %collective-permute-start.6 = (bf16[1,3,64,512]{3,2,0,1:T(8,128)(2,1)S(1)}, bf16[1,3,64,512]{3,2,0,1:T(8,128)(2,1)S(1)}, u32[]{:S(2)}, u32[]{:S(2)}) collective-permute-start(bf16[1,3,64,512]{3,2,0,1:T(8,128)(2,1)S(1)} %get-tuple-element.13), channel_id=1, source_target_pairs={{0,24},{1,28},{2,0},{3,4},{4,8},{5,12},{6,16},{7,20},{8,25},{9,29}... | collective-permute-start | bytes 589832 | tf_op jit(solution)/shard_map/ppermute | solution.py:74
  115.1 4.9 %collective-permute-done.6 = bf16[1,3,64,512]{3,2,0,1:T(8,128)(2,1)S(1)} collective-permute-done((bf16[1,3,64,512]{3,2,0,1:T(8,128)(2,1)S(1)}, bf16[1,3,64,512]{3,2,0,1:T(8,128)(2,1)S(1)}, u32[]{:S(2)}, u32[]{:S(2)}) %collective-permute-start.6) | collective-permute-done | bytes 196640 | tf_op jit(solution)/shard_map/ppermute | solution.py:74
  120.0 6.9 %collective-permute-start.7 = (bf16[1,3,64,512]{3,2,0,1:T(8,128)(2,1)S(1)}, bf16[1,3,64,512]{3,2,0,1:T(8,128)(2,1)S(1)}, u32[]{:S(2)}, u32[]{:S(2)}) collective-permute-start(bf16[1,3,64,512]{3,2,0,1:T(8,128)(2,1)S(1)} %get-tuple-element.12), channel_id=1, source_target_pairs={{0,28},{1,0},{2,4},{3,8},{4,12},{5,16},{6,20},{7,24},{8,29},{9,1},... | collective-permute-start | bytes 589832 | tf_op jit(solution)/shard_map/ppermute | solution.py:74
  126.9 3.6 %collective-permute-done.7 = bf16[1,3,64,512]{3,2,0,1:T(8,128)(2,1)S(1)} collective-permute-done((bf16[1,3,64,512]{3,2,0,1:T(8,128)(2,1)S(1)}, bf16[1,3,64,512]{3,2,0,1:T(8,128)(2,1)S(1)}, u32[]{:S(2)}, u32[]{:S(2)}) %collective-permute-start.7) | collective-permute-done | bytes 196640 | tf_op jit(solution)/shard_map/ppermute | solution.py:74
  130.5 1.6 copy.100
  137.9 3.4 %collective-permute-done.10 = bf16[192,1024]{1,0:T(8,128)(2,1)S(1)} collective-permute-done((bf16[192,1024]{1,0:T(8,128)(2,1)}, bf16[192,1024]{1,0:T(8,128)(2,1)S(1)}, u32[]{:S(2)}, u32[]{:S(2)}) %collective-permute-start.10) | collective-permute-done | bytes 393248 | tf_op jit(solution)/shard_map/ppermute | solution.py:40
  142.5 5.8 %collective-permute-done.12 = bf16[192,1024]{1,0:T(8,128)(2,1)S(1)} collective-permute-done((bf16[192,1024]{1,0:T(8,128)(2,1)}, bf16[192,1024]{1,0:T(8,128)(2,1)S(1)}, u32[]{:S(2)}, u32[]{:S(2)}) %collective-permute-start.12) | collective-permute-done | bytes 393248 | tf_op jit(solution)/shard_map/ppermute | solution.py:40
  149.4 7.3 %collective-permute-done.14 = bf16[192,1024]{1,0:T(8,128)(2,1)S(1)} collective-permute-done((bf16[192,1024]{1,0:T(8,128)(2,1)}, bf16[192,1024]{1,0:T(8,128)(2,1)S(1)}, u32[]{:S(2)}, u32[]{:S(2)}) %collective-permute-start.14) | collective-permute-done | bytes 393248 | tf_op jit(solution)/shard_map/ppermute | solution.py:40
  157.8 2.6 fusion.159
  160.7 2.0 copy-done
  162.6 5.5 %collective-permute-start.15 = (f32[2,192,1536]{2,1,0:T(8,128)S(1)}, f32[2,192,1536]{2,1,0:T(8,128)}, u32[]{:S(2)}, u32[]{:S(2)}) collective-permute-start(f32[2,192,1536]{2,1,0:T(8,128)S(1)} %dynamic-slice_bitcast_fusion), channel_id=1, source_target_pairs={{0,1},{1,0},{2,3},{3,2},{4,5},{5,4},{6,7},{7,6},{8,9},{9,8},{10,11... | collective-permute-start | bytes 7077896 | tf_op jit(solution)/shard_map/ppermute | solution.py:92
  168.1 4.3 %collective-permute-done.15 = f32[2,192,1536]{2,1,0:T(8,128)} collective-permute-done((f32[2,192,1536]{2,1,0:T(8,128)S(1)}, f32[2,192,1536]{2,1,0:T(8,128)}, u32[]{:S(2)}, u32[]{:S(2)}) %collective-permute-start.15) | collective-permute-done | bytes 2359328 | tf_op jit(solution)/shard_map/ppermute | solution.py:92
  172.4 2.8 %bitcast_add_fusion = f32[2,192,1536]{2,1,0:T(8,128)S(1)} fusion(f32[2,192,1536]{2,1,0:T(8,128)} %collective-permute-done.15, f32[2,2,192,1536]{3,2,1,0:T(8,128)} %copy-done, s32[]{:T(128)S(6)} %select_n.383), kind=kLoop, calls=%fused_computation | loop fusion | flops 589824 | bytes 7077892 | tf_op jit(solution)/shard_map/add | solution.py:92
  176.1 8.8 %collective-permute-start.16 = (bf16[1,192,1536]{2,1,0:T(8,128)(2,1)}, bf16[1,192,1536]{2,1,0:T(8,128)(2,1)}, u32[]{:S(2)}, u32[]{:S(2)}) collective-permute-start(bf16[1,192,1536]{2,1,0:T(8,128)(2,1)} %dynamic-slice_convert_fusion), channel_id=1, source_target_pairs={{0,2},{1,3},{2,0},{3,1},{4,6},{5,7},{6,4},{7,5},{8,10},{9,11},{10,... | collective-permute-start | bytes 1769480 | tf_op jit(solution)/shard_map/ppermute | solution.py:92
  184.9 1.5 copy.105
  187.5 3.7 %all-to-all-start = ((f32[8,64,2,192]{3,1,2,0:T(8,128)}), f32[8,64,2,192]{3,1,2,0:T(8,128)S(1)}, u32[]{:S(2)}, u32[]{:S(2)}) async-start(f32[8,64,2,192]{3,1,2,0:T(8,128)} %copy.106), calls=%async_computation | async-start | bytes 2097152 | tf_op jit(solution)/shard_map/all_to_all | solution.py:103
  191.2 3.8 %reshape.133 = bf16[192,8,4,128]{3,2,1,0:T(4,128)(2,1)} reshape(bf16[192,4096]{1,0:T(8,128)(2,1)} %param.9) | data formatting | bytes 3145728 | tf_op jit(solution)/shard_map/reshape | solution.py:144
  195.0 2.2 constant_dynamic-slice_fusion.2
  204.3 2.2 fusion.17
  206.5 1.4 convolution_add_fusion
  208.0 9.3 %all-to-all-done = f32[8,64,2,192]{3,1,2,0:T(8,128)S(1)} async-done(((f32[8,64,2,192]{3,1,2,0:T(8,128)}), f32[8,64,2,192]{3,1,2,0:T(8,128)S(1)}, u32[]{:S(2)}, u32[]{:S(2)}) %all-to-all-start) | async-done | bytes 786464 | tf_op jit(solution)/shard_map/all_to_all | solution.py:103
  217.2 4.1 %all-to-all-start.1 = ((bf16[192,8,128]{2,0,1:T(8,128)(2,1)}), bf16[192,8,128]{2,0,1:T(8,128)(2,1)}, u32[]{:S(2)}, u32[]{:S(2)}) async-start(bf16[192,8,128]{2,0,1:T(8,128)(2,1)} %bitcast.206), calls=%async_computation.1 | async-start | bytes 786432 | tf_op jit(solution)/shard_map/all_to_all | solution.py:146
  221.6 2.5 multiply_subtract_fusion
  229.5 2.0 fusion.13
  231.5 2.0 fusion.1
  233.7 1.7 collective-permute-start.18
  235.4 1.5 collective-permute-start.17
  236.9 2.4 collective-permute-start.22
  239.9 3.5 %collective-permute-done.18 = bf16[64,1536]{1,0:T(8,128)(2,1)S(1)} collective-permute-done((bf16[64,1536]{1,0:T(8,128)(2,1)S(1)}, bf16[64,1536]{1,0:T(8,128)(2,1)S(1)}, u32[]{:S(2)}, u32[]{:S(2)}) %collective-permute-start.18) | collective-permute-done | bytes 196640 | tf_op jit(solution)/shard_map/ppermute | solution.py:36
  243.4 1.7 collective-permute-start.19
  247.1 7.2 %collective-permute-done.20 = bf16[64,1536]{1,0:T(8,128)(2,1)S(1)} collective-permute-done((bf16[64,1536]{1,0:T(8,128)(2,1)S(1)}, bf16[64,1536]{1,0:T(8,128)(2,1)S(1)}, u32[]{:S(2)}, u32[]{:S(2)}) %collective-permute-start.20) | collective-permute-done | bytes 196640 | tf_op jit(solution)/shard_map/ppermute | solution.py:36
  254.3 1.5 collective-permute-start.21
  255.8 4.6 %collective-permute-done.21 = bf16[64,1536]{1,0:T(8,128)(2,1)S(1)} collective-permute-done((bf16[64,1536]{1,0:T(8,128)(2,1)S(1)}, bf16[64,1536]{1,0:T(8,128)(2,1)S(1)}, u32[]{:S(2)}, u32[]{:S(2)}) %collective-permute-start.21) | collective-permute-done | bytes 196640 | tf_op jit(solution)/shard_map/ppermute | solution.py:40
  261.6 3.4 %fusion.160 = f32[512,512]{1,0:T(8,128)} fusion(bf16[1536,512]{1,0:T(8,128)(2,1)} %all-gather.2.cloned.1.call-done, bf16[512,1536]{1,0:T(8,128)(2,1)S(1)} %bitcast.205), kind=kOutput, calls=%fused_computation.216 | convolution fusion | flops 805306368 | bytes 4194304 | tf_op jit(solution)/shard_map/dot_general | solution.py:153
  (76 shorter events, 29.1 us)
Async XLA Ops:
  9.1 1.0 copy-start.1
  9.2 11.9 %collective-permute-start = (bf16[1,3,64,512]{3,2,0,1:T(8,128)(2,1)S(1)}, bf16[1,3,64,512]{3,2,0,1:T(8,128)(2,1)S(1)}, u32[]{:S(2)}, u32[]{:S(2)}) collective-permute-start(bf16[1,3,64,512]{3,2,0,1:T(8,128)(2,1)S(1)} %get-tuple-element.19), channel_id=1, source_target_pairs={{0,0},{1,4},{2,8},{3,12},{4,16},{5,20},{6,24},{7,28},{8,1},{9,5},{... | collective-permute-start | bytes 589832 | tf_op jit(solution)/shard_map/ppermute | solution.py:74
  10.1 126.3 %collective-permute-start.8 = (bf16[192,1024]{1,0:T(8,128)(2,1)S(1)}, bf16[192,1024]{1,0:T(8,128)(2,1)}, u32[]{:S(2)}, u32[]{:S(2)}) collective-permute-start(bf16[192,1024]{1,0:T(8,128)(2,1)S(1)} %copy-done.1), channel_id=1, source_target_pairs={{0,4},{4,0},{8,12},{12,8},{16,20},{20,16},{24,28},{28,24},{1,5},{5... | collective-permute-start | bytes 1179656 | tf_op jit(solution)/shard_map/ppermute | solution.py:40
  16.7 116.5 %collective-permute-start.9 = (bf16[192,1024]{1,0:T(8,128)(2,1)S(1)}, bf16[192,1024]{1,0:T(8,128)(2,1)}, u32[]{:S(2)}, u32[]{:S(2)}) collective-permute-start(bf16[192,1024]{1,0:T(8,128)(2,1)S(1)} %copy-done.1), channel_id=1, source_target_pairs={{0,8},{4,12},{8,16},{12,20},{16,24},{20,28},{24,0},{28,4},{1,9},{5... | collective-permute-start | bytes 1179656 | tf_op jit(solution)/shard_map/ppermute | solution.py:36
  16.7 117.6 %collective-permute-start.11 = (bf16[192,1024]{1,0:T(8,128)(2,1)S(1)}, bf16[192,1024]{1,0:T(8,128)(2,1)}, u32[]{:S(2)}, u32[]{:S(2)}) collective-permute-start(bf16[192,1024]{1,0:T(8,128)(2,1)S(1)} %copy-done.1), channel_id=1, source_target_pairs={{0,16},{4,20},{8,24},{12,28},{16,0},{20,4},{24,8},{28,12},{1,17},{... | collective-permute-start | bytes 1179656 | tf_op jit(solution)/shard_map/ppermute | solution.py:36
  19.1 116.2 %collective-permute-start.13 = (bf16[192,1024]{1,0:T(8,128)(2,1)S(1)}, bf16[192,1024]{1,0:T(8,128)(2,1)}, u32[]{:S(2)}, u32[]{:S(2)}) collective-permute-start(bf16[192,1024]{1,0:T(8,128)(2,1)S(1)} %copy-done.1), channel_id=1, source_target_pairs={{0,24},{4,28},{8,0},{12,4},{16,8},{20,12},{24,16},{28,20},{1,25},{... | collective-permute-start | bytes 1179656 | tf_op jit(solution)/shard_map/ppermute | solution.py:36
  21.2 8.9 %collective-permute-start.1 = (bf16[1,3,64,512]{3,2,0,1:T(8,128)(2,1)S(1)}, bf16[1,3,64,512]{3,2,0,1:T(8,128)(2,1)S(1)}, u32[]{:S(2)}, u32[]{:S(2)}) collective-permute-start(bf16[1,3,64,512]{3,2,0,1:T(8,128)(2,1)S(1)} %get-tuple-element.18), channel_id=1, source_target_pairs={{0,4},{1,8},{2,12},{3,16},{4,20},{5,24},{6,28},{7,0},{8,5},{9,9},{... | collective-permute-start | bytes 589832 | tf_op jit(solution)/shard_map/ppermute | solution.py:74
  30.1 48.3 %collective-permute-start.2 = (bf16[1,3,64,512]{3,2,0,1:T(8,128)(2,1)S(1)}, bf16[1,3,64,512]{3,2,0,1:T(8,128)(2,1)S(1)}, u32[]{:S(2)}, u32[]{:S(2)}) collective-permute-start(bf16[1,3,64,512]{3,2,0,1:T(8,128)(2,1)S(1)} %get-tuple-element.17), channel_id=1, source_target_pairs={{0,8},{1,12},{2,16},{3,20},{4,24},{5,28},{6,0},{7,4},{8,9},{9,13},... | collective-permute-start | bytes 589832 | tf_op jit(solution)/shard_map/ppermute | solution.py:74
  78.4 9.0 %collective-permute-start.3 = (bf16[1,3,64,512]{3,2,0,1:T(8,128)(2,1)S(1)}, bf16[1,3,64,512]{3,2,0,1:T(8,128)(2,1)S(1)}, u32[]{:S(2)}, u32[]{:S(2)}) collective-permute-start(bf16[1,3,64,512]{3,2,0,1:T(8,128)(2,1)S(1)} %get-tuple-element.16), channel_id=1, source_target_pairs={{0,12},{1,16},{2,20},{3,24},{4,28},{5,0},{6,4},{7,8},{8,13},{9,17}... | collective-permute-start | bytes 589832 | tf_op jit(solution)/shard_map/ppermute | solution.py:74
  87.4 7.2 %collective-permute-start.4 = (bf16[1,3,64,512]{3,2,0,1:T(8,128)(2,1)S(1)}, bf16[1,3,64,512]{3,2,0,1:T(8,128)(2,1)S(1)}, u32[]{:S(2)}, u32[]{:S(2)}) collective-permute-start(bf16[1,3,64,512]{3,2,0,1:T(8,128)(2,1)S(1)} %get-tuple-element.15), channel_id=1, source_target_pairs={{0,16},{1,20},{2,24},{3,28},{4,0},{5,4},{6,8},{7,12},{8,17},{9,21}... | collective-permute-start | bytes 589832 | tf_op jit(solution)/shard_map/ppermute | solution.py:74
  94.5 12.8 %collective-permute-start.5 = (bf16[1,3,64,512]{3,2,0,1:T(8,128)(2,1)S(1)}, bf16[1,3,64,512]{3,2,0,1:T(8,128)(2,1)S(1)}, u32[]{:S(2)}, u32[]{:S(2)}) collective-permute-start(bf16[1,3,64,512]{3,2,0,1:T(8,128)(2,1)S(1)} %get-tuple-element.14), channel_id=1, source_target_pairs={{0,20},{1,24},{2,28},{3,0},{4,4},{5,8},{6,12},{7,16},{8,21},{9,25}... | collective-permute-start | bytes 589832 | tf_op jit(solution)/shard_map/ppermute | solution.py:74
  107.3 12.7 %collective-permute-start.6 = (bf16[1,3,64,512]{3,2,0,1:T(8,128)(2,1)S(1)}, bf16[1,3,64,512]{3,2,0,1:T(8,128)(2,1)S(1)}, u32[]{:S(2)}, u32[]{:S(2)}) collective-permute-start(bf16[1,3,64,512]{3,2,0,1:T(8,128)(2,1)S(1)} %get-tuple-element.13), channel_id=1, source_target_pairs={{0,24},{1,28},{2,0},{3,4},{4,8},{5,12},{6,16},{7,20},{8,25},{9,29}... | collective-permute-start | bytes 589832 | tf_op jit(solution)/shard_map/ppermute | solution.py:74
  120.0 10.5 %collective-permute-start.7 = (bf16[1,3,64,512]{3,2,0,1:T(8,128)(2,1)S(1)}, bf16[1,3,64,512]{3,2,0,1:T(8,128)(2,1)S(1)}, u32[]{:S(2)}, u32[]{:S(2)}) collective-permute-start(bf16[1,3,64,512]{3,2,0,1:T(8,128)(2,1)S(1)} %get-tuple-element.12), channel_id=1, source_target_pairs={{0,28},{1,0},{2,4},{3,8},{4,12},{5,16},{6,20},{7,24},{8,29},{9,1},... | collective-permute-start | bytes 589832 | tf_op jit(solution)/shard_map/ppermute | solution.py:74
  133.3 8.1 %collective-permute-start.10 = (bf16[192,1024]{1,0:T(8,128)(2,1)}, bf16[192,1024]{1,0:T(8,128)(2,1)S(1)}, u32[]{:S(2)}, u32[]{:S(2)}) collective-permute-start(bf16[192,1024]{1,0:T(8,128)(2,1)} %collective-permute-done.9), channel_id=1, source_target_pairs={{0,4},{4,0},{8,12},{12,8},{16,20},{20,16},{24,28},{28,24},{1,5},{5... | collective-permute-start | bytes 1179656 | tf_op jit(solution)/shard_map/ppermute | solution.py:40
  134.3 13.9 %collective-permute-start.12 = (bf16[192,1024]{1,0:T(8,128)(2,1)}, bf16[192,1024]{1,0:T(8,128)(2,1)S(1)}, u32[]{:S(2)}, u32[]{:S(2)}) collective-permute-start(bf16[192,1024]{1,0:T(8,128)(2,1)} %collective-permute-done.11), channel_id=1, source_target_pairs={{0,4},{4,0},{8,12},{12,8},{16,20},{20,16},{24,28},{28,24},{1,5},{5... | collective-permute-start | bytes 1179656 | tf_op jit(solution)/shard_map/ppermute | solution.py:40
  135.4 21.3 %collective-permute-start.14 = (bf16[192,1024]{1,0:T(8,128)(2,1)}, bf16[192,1024]{1,0:T(8,128)(2,1)S(1)}, u32[]{:S(2)}, u32[]{:S(2)}) collective-permute-start(bf16[192,1024]{1,0:T(8,128)(2,1)} %collective-permute-done.13), channel_id=1, source_target_pairs={{0,4},{4,0},{8,12},{12,8},{16,20},{20,16},{24,28},{28,24},{1,5},{5... | collective-permute-start | bytes 1179656 | tf_op jit(solution)/shard_map/ppermute | solution.py:40
  160.5 2.1 copy-start
  162.6 9.8 %collective-permute-start.15 = (f32[2,192,1536]{2,1,0:T(8,128)S(1)}, f32[2,192,1536]{2,1,0:T(8,128)}, u32[]{:S(2)}, u32[]{:S(2)}) collective-permute-start(f32[2,192,1536]{2,1,0:T(8,128)S(1)} %dynamic-slice_bitcast_fusion), channel_id=1, source_target_pairs={{0,1},{1,0},{2,3},{3,2},{4,5},{5,4},{6,7},{7,6},{8,9},{9,8},{10,11... | collective-permute-start | bytes 7077896 | tf_op jit(solution)/shard_map/ppermute | solution.py:92
  176.1 23.0 %collective-permute-start.16 = (bf16[1,192,1536]{2,1,0:T(8,128)(2,1)}, bf16[1,192,1536]{2,1,0:T(8,128)(2,1)}, u32[]{:S(2)}, u32[]{:S(2)}) collective-permute-start(bf16[1,192,1536]{2,1,0:T(8,128)(2,1)} %dynamic-slice_convert_fusion), channel_id=1, source_target_pairs={{0,2},{1,3},{2,0},{3,1},{4,6},{5,7},{6,4},{7,5},{8,10},{9,11},{10,... | collective-permute-start | bytes 1769480 | tf_op jit(solution)/shard_map/ppermute | solution.py:92
  187.5 29.8 %all-to-all-start = ((f32[8,64,2,192]{3,1,2,0:T(8,128)}), f32[8,64,2,192]{3,1,2,0:T(8,128)S(1)}, u32[]{:S(2)}, u32[]{:S(2)}) async-start(f32[8,64,2,192]{3,1,2,0:T(8,128)} %copy.106), calls=%async_computation | async-start | bytes 2097152 | tf_op jit(solution)/shard_map/all_to_all | solution.py:103
  217.2 19.6 %all-to-all-start.1 = ((bf16[192,8,128]{2,0,1:T(8,128)(2,1)}), bf16[192,8,128]{2,0,1:T(8,128)(2,1)}, u32[]{:S(2)}, u32[]{:S(2)}) async-start(bf16[192,8,128]{2,0,1:T(8,128)(2,1)} %bitcast.206), calls=%async_computation.1 | async-start | bytes 786432 | tf_op jit(solution)/shard_map/all_to_all | solution.py:146
  221.3 40.3 %all-gather.2.cloned.1.call-start = ((), (), s32[]{:S(2)}) async-start(), calls=%async_computation.2 | async-start | bytes 1966080 | tf_op jit(solution)/shard_map/all_gather | solution.py:147
  233.7 9.7 %collective-permute-start.18 = (bf16[64,1536]{1,0:T(8,128)(2,1)S(1)}, bf16[64,1536]{1,0:T(8,128)(2,1)S(1)}, u32[]{:S(2)}, u32[]{:S(2)}) collective-permute-start(bf16[64,1536]{1,0:T(8,128)(2,1)S(1)} %fusion.24), channel_id=1, source_target_pairs={{0,8},{4,12},{8,16},{12,20},{16,24},{20,28},{24,0},{28,4},{1,9},{5... | collective-permute-start | bytes 589832 | tf_op jit(solution)/shard_map/ppermute | solution.py:36
  235.4 9.7 %collective-permute-start.17 = (bf16[64,1536]{1,0:T(8,128)(2,1)S(1)}, bf16[64,1536]{1,0:T(8,128)(2,1)S(1)}, u32[]{:S(2)}, u32[]{:S(2)}) collective-permute-start(bf16[64,1536]{1,0:T(8,128)(2,1)S(1)} %fusion.24), channel_id=1, source_target_pairs={{0,4},{4,0},{8,12},{12,8},{16,20},{20,16},{24,28},{28,24},{1,5},{5... | collective-permute-start | bytes 589832 | tf_op jit(solution)/shard_map/ppermute | solution.py:40
  236.9 8.9 %collective-permute-start.22 = (bf16[64,1536]{1,0:T(8,128)(2,1)S(1)}, bf16[64,1536]{1,0:T(8,128)(2,1)S(1)}, u32[]{:S(2)}, u32[]{:S(2)}) collective-permute-start(bf16[64,1536]{1,0:T(8,128)(2,1)S(1)} %fusion.24), channel_id=1, source_target_pairs={{0,24},{4,28},{8,0},{12,4},{16,8},{20,12},{24,16},{28,20},{1,25},{... | collective-permute-start | bytes 589832 | tf_op jit(solution)/shard_map/ppermute | solution.py:36
  239.3 15.0 %collective-permute-start.20 = (bf16[64,1536]{1,0:T(8,128)(2,1)S(1)}, bf16[64,1536]{1,0:T(8,128)(2,1)S(1)}, u32[]{:S(2)}, u32[]{:S(2)}) collective-permute-start(bf16[64,1536]{1,0:T(8,128)(2,1)S(1)} %fusion.24), channel_id=1, source_target_pairs={{0,16},{4,20},{8,24},{12,28},{16,0},{20,4},{24,8},{28,12},{1,17},{... | collective-permute-start | bytes 589832 | tf_op jit(solution)/shard_map/ppermute | solution.py:36
  243.4 12.3 %collective-permute-start.19 = (bf16[64,1536]{1,0:T(8,128)(2,1)S(1)}, bf16[64,1536]{1,0:T(8,128)(2,1)S(1)}, u32[]{:S(2)}, u32[]{:S(2)}) collective-permute-start(bf16[64,1536]{1,0:T(8,128)(2,1)S(1)} %collective-permute-done.18), channel_id=1, source_target_pairs={{0,4},{4,0},{8,12},{12,8},{16,20},{20,16},{24,28},{28,24},{1,5},{5... | collective-permute-start | bytes 589832 | tf_op jit(solution)/shard_map/ppermute | solution.py:40
  245.8 14.7 %collective-permute-start.23 = (bf16[64,1536]{1,0:T(8,128)(2,1)S(1)}, bf16[64,1536]{1,0:T(8,128)(2,1)S(1)}, u32[]{:S(2)}, u32[]{:S(2)}) collective-permute-start(bf16[64,1536]{1,0:T(8,128)(2,1)S(1)} %collective-permute-done.22), channel_id=1, source_target_pairs={{0,4},{4,0},{8,12},{12,8},{16,20},{20,16},{24,28},{28,24},{1,5},{5... | collective-permute-start | bytes 589832 | tf_op jit(solution)/shard_map/ppermute | solution.py:40
  254.3 6.2 %collective-permute-start.21 = (bf16[64,1536]{1,0:T(8,128)(2,1)S(1)}, bf16[64,1536]{1,0:T(8,128)(2,1)S(1)}, u32[]{:S(2)}, u32[]{:S(2)}) collective-permute-start(bf16[64,1536]{1,0:T(8,128)(2,1)S(1)} %collective-permute-done.20), channel_id=1, source_target_pairs={{0,4},{4,0},{8,12},{12,8},{16,20},{20,16},{24,28},{28,24},{1,5},{5... | collective-permute-start | bytes 589832 | tf_op jit(solution)/shard_map/ppermute | solution.py:40
Sparse Core Ops, SparseCore 0:
  237.0 18.3 all-gather.1

commit v2 on v1

--- a/solution.py
+++ b/solution.py
@@ -1,12 +1,17 @@
+import functools
 import math
 
 import jax
 import jax.numpy as jnp
+import numpy as np
 from jax import lax
+from jax.experimental import pallas as pl
+from jax.experimental.pallas import tpu as pltpu
 from jax.sharding import PartitionSpec as P
 
 TWO_PI = 2.0 * math.pi
 BOTH = ("ctx", "ch")
+ORDER = (0, 4, 2, 6, 1, 5, 3, 7)
 
 
 def product(spec, left, right):
@@ -44,7 +49,7 @@
     return found
 
 
-def on_device(features, w_in, short_filter, filter_spectrum, out_grad):
+def general(features, w_in, short_filter, filter_spectrum, out_grad):
     n = lax.axis_size("ctx")
     m = lax.axis_size("ch")
     place = lax.axis_index("ctx")
@@ -157,6 +162,337 @@
     return (out, w_out_grad)
 
 
+def exact(left, right):
+    return jnp.dot(left, right, precision=lax.Precision.HIGHEST, preferred_element_type=jnp.float32)
+
+def tables(rows, lanes):
+    grid = np.arange(rows)[:, None] * np.arange(rows)[None, :] % rows
+    angle = 2.0 * math.pi / rows * grid
+    table = np.zeros((rows, 2 * lanes), np.float32)
+    table[:, :rows] = np.cos(angle)
+    table[:, lanes : lanes + rows] = np.sin(angle)
+    turn = 2.0 * math.pi / (8 * rows) * (np.arange(5)[:, None] * np.arange(rows)[None, :])
+    return table, np.stack([np.cos(turn), np.sin(turn)]).astype(np.float32)
+
+def convolve_kernel(odd_ref, mine_ref, other_ref, taps_ref, response_ref, table_ref, turn_ref, out_ref):
+    own, total = out_ref.shape
+    rows = total // 8
+    lanes = table_ref.shape[1] // 2
+    mine, other = mine_ref[...].astype(jnp.float32), other_ref[...].astype(jnp.float32)
+    even, uneven = jnp.where(odd_ref[0] == 0, mine, other), jnp.where(odd_ref[0] == 0, other, mine)
+    slabs = []
+    for spot in range(4):
+        slabs += [even[:, rows * spot : rows * (spot + 1)], uneven[:, rows * spot : rows * (spot + 1)]]
+    projected = jnp.concatenate(slabs, axis=1)
+    lane = lax.broadcasted_iota(jnp.int32, projected.shape, 1)
+    mixed = taps_ref[0] * projected
+    for back in (1, 2):
+        moved = jnp.where(lane < back, 0.0, pltpu.roll(projected, back, 1))
+        mixed += taps_ref[back] * moved
+    query = mixed[:own]
+    signal = mixed[own : 2 * own] * mixed[2 * own :]
+    a = [signal[:, rows * i : rows * (i + 1)] for i in range(8)]
+    half = math.sqrt(0.5)
+    s04, d04, s26, d26 = a[0] + a[4], a[0] - a[4], a[2] + a[6], a[2] - a[6]
+    s15, d15, s37, d37 = a[1] + a[5], a[1] - a[5], a[3] + a[7], a[3] - a[7]
+    e, f = s04 + s26, s15 + s37
+    g, h = half * (d15 - d37), half * (d15 + d37)
+    real = [e + f, d04 + g, s04 - s26, d04 - g, e - f]
+    imag = [None, -(d26 + h), s37 - s15, d26 - h, None]
+    ins = [real[0]]
+    for r in range(1, 5):
+        cos, sin = turn_ref[0, r : r + 1], turn_ref[1, r : r + 1]
+        if imag[r] is None:
+            ins += [real[r] * cos, -real[r] * sin]
+        else:
+            ins += [real[r] * cos + imag[r] * sin, imag[r] * cos - real[r] * sin]
+    spectrum = exact(jnp.concatenate(ins, axis=0), table_ref[...])
+    response = [
+        jnp.concatenate([response_ref[ORDER[r], i] for i in range(response_ref.shape[1])], axis=1)
+        for r in range(8)
+    ]
+    response = [value.astype(jnp.float32) for value in response]
+    outs = []
+    for r in range(5):
+        if r == 0:
+            first = spectrum[:own]
+            spec_real, spec_imag = first[:, :rows], -first[:, lanes : lanes + rows]
+        else:
+            first = spectrum[(2 * r - 1) * own : 2 * r * own]
+            second = spectrum[2 * r * own : (2 * r + 1) * own]
+            spec_real = first[:, :rows] + second[:, lanes : lanes + rows]
+            spec_imag = second[:, :rows] - first[:, lanes : lanes + rows]
+        own_class = response[r]
+        res_real, res_imag = own_class[:, :rows], own_class[:, rows:]
+        if r in (1, 2, 3):
+            mirrored = response[8 - r]
+            res_real = 0.5 * (res_real + mirrored[:, :rows])
+            res_imag = 0.5 * (res_imag - mirrored[:, rows:])
+        outs += [spec_real * res_real - spec_imag * res_imag, spec_real * res_imag + spec_imag * res_real]
+    back = exact(jnp.concatenate(outs, axis=0), table_ref[...])
+    u_real, u_imag = [], []
+    for r in range(5):
+        first = back[2 * r * own : (2 * r + 1) * own]
+        second = back[(2 * r + 1) * own : (2 * r + 2) * own]
+        v_real = first[:, :rows] - second[:, lanes : lanes + rows]
+        if r == 0:
+            u_real.append(v_real)
+            u_imag.append(None)
+            continue
+        v_imag = second[:, :rows] + first[:, lanes : lanes + rows]
+        cos, sin = turn_ref[0, r : r + 1], turn_ref[1, r : r + 1]
+        u_real.append(v_real * cos - v_imag * sin)
+        u_imag.append(None if r == 4 else v_imag * cos + v_real * sin)
+    p, q = u_real[0] + u_real[4], u_real[0] - u_real[4]
+    r13, i13 = u_real[1] + u_real[3], u_imag[1] - u_imag[3]
+    dr, di = half * (u_real[1] - u_real[3]), half * (u_imag[1] + u_imag[3])
+    two = 2.0
+    r2, i2 = u_real[2], u_imag[2]
+    y = [p + two * (r13 + r2), q + two * (dr - di - i2), p - two * (i13 + r2), q + two * (i2 - dr - di),
+         p + two * (r2 - r13), q + two * (di - dr - i2), p + two * (i13 - r2), q + two * (dr + di + i2)]
+    scale = 1.0 / total
+    convolved = jnp.concatenate(y, axis=1) * scale
+    out_ref[...] = (query * convolved).astype(jnp.bfloat16)
+
+def convolve(odd, mine, other, taps, response):
+    total = 2 * mine.shape[1]
+    own = mine.shape[0] // 3
+    rows = total // 8
+    table, turn = tables(rows, -(-rows // 128) * 128)
+    return pl.pallas_call(convolve_kernel, out_shape=jax.ShapeDtypeStruct((own, total), jnp.bfloat16),
+        in_specs=[pl.BlockSpec(memory_space=pltpu.SMEM)] + [pl.BlockSpec(memory_space=pltpu.VMEM)] * 6,
+        compiler_params=pltpu.CompilerParams(vmem_limit_bytes=48*2**20),
+        cost_estimate=pl.CostEstimate(flops=10**9, bytes_accessed=4*10**6, transcendentals=0),
+    )(odd, mine, other, taps, response, jnp.asarray(table), jnp.asarray(turn))
+
+
+PARTS = 2
+
+
+def multiply_kernel(part, slots, whole_ref, *refs):
+    send_ref, keep_ref, held, sems = refs[-4:]
+    pieces = refs[:-4]
+    share, spots, spot, block_depth = held.shape
+    copies = []
+    for step, piece in enumerate(pieces):
+        copies.append(
+            pltpu.make_async_copy(
+                piece.at[pl.ds(part * spot, spot)],
+                held.at[slots[0, step], slots[1, step]],
+                sems.at[step],
+            )
+        )
+    for copy in copies:
+        copy.start()
+    for copy in copies:
+        copy.wait()
+    for place in (1, 3, 2, 0):
+        total = jnp.zeros((spot, whole_ref.shape[0]), jnp.float32)
+        for block in range(share):
+            total += lax.dot_general(
+                held[block, place],
+                whole_ref[:, block * block_depth : (block + 1) * block_depth],
+                (((1,), (1,)), ((), ())),
+                preferred_element_type=jnp.float32,
+            )
+        out_ref = send_ref if place % 2 else keep_ref
+        out_ref[place // 2] = total
+
+
+def multiply(part, slots, whole, pieces, share):
+    rows, block_depth = pieces[0].shape
+    spot = rows // PARTS
+    spots = len(pieces) // share
+    vmem = pl.BlockSpec(memory_space=pltpu.VMEM)
+    anywhere = pl.BlockSpec(memory_space=pl.ANY)
+    out = jax.ShapeDtypeStruct((spots // 2, spot, whole.shape[0]), jnp.float32)
+    return pl.pallas_call(
+        functools.partial(multiply_kernel, part),
+        out_shape=[out] * 2,
+        in_specs=[pl.BlockSpec(memory_space=pltpu.SMEM), vmem] + [anywhere] * len(pieces),
+        out_specs=[vmem] * 2,
+        scratch_shapes=[
+            pltpu.VMEM((share, spots, spot, block_depth), jnp.bfloat16),
+            pltpu.SemaphoreType.DMA((len(pieces),)),
+        ],
+        compiler_params=pltpu.CompilerParams(vmem_limit_bytes=32 * 2**20),
+        cost_estimate=pl.CostEstimate(
+            flops=2 * spots * spot * whole.shape[0] * whole.shape[1],
+            bytes_accessed=6 * 2**20,
+            transcendentals=0,
+        ),
+    )(slots, whole, *pieces)
+
+
+def pack_kernel(flag_ref, value_ref, grad_ref, out_ref):
+    rows = value_ref.shape[1]
+    n, _, count, lanes = out_ref.shape
+    own = value_ref.shape[2] // n
+    down = lax.broadcasted_iota(jnp.int32, (rows, rows), 0)
+    along = lax.broadcasted_iota(jnp.int32, (rows, rows), 1)
+    target = jnp.where(flag_ref[0] == 1, rows - 1 - down, down)
+    swap = (along == target).astype(jnp.bfloat16)
+    turned = [
+        lax.dot_general(
+            value_ref[part].astype(jnp.bfloat16),
+            swap,
+            (((0,), (0,)), ((), ())),
+            preferred_element_type=jnp.float32,
+        ).astype(jnp.bfloat16)
+        for part in range(2)
+    ]
+    turned = jnp.concatenate(turned, axis=1)
+    step = grad_ref.shape[1] // n
+    for place in range(n):
+        for chunk in range(count // own):
+            out_ref[place, 0, own * chunk : own * (chunk + 1)] = turned[
+                own * place : own * (place + 1), lanes * chunk : lanes * (chunk + 1)
+            ]
+        start = pl.multiple_of(place * step + flag_ref[1] * lanes, lanes)
+        out_ref[place, 1] = grad_ref[:, pl.ds(start, lanes)]
+
+
+def pack(flags, value, grad, n, m):
+    rows = grad.shape[0]
+    lanes = grad.shape[1] // (n * m)
+    vmem = pl.BlockSpec(memory_space=pltpu.VMEM)
+    return pl.pallas_call(
+        pack_kernel,
+        out_shape=jax.ShapeDtypeStruct((n, 2, rows, lanes), jnp.bfloat16),
+        in_specs=[pl.BlockSpec(memory_space=pltpu.SMEM), vmem, vmem],
+        out_specs=vmem,
+        compiler_params=pltpu.CompilerParams(vmem_limit_bytes=32 * 2**20),
+        cost_estimate=pl.CostEstimate(flops=10**8, bytes_accessed=4 * 2**20, transcendentals=0),
+    )(flags, value, grad)
+
+
+def fits(mesh):
+    return mesh.shape["ctx"] == 8 and mesh.shape["ch"] == 4
+
+
+def after(value, *others):
+    return lax.optimization_barrier((value, *others))[0]
+
+
+def special(features, w_in, short_filter, filter_spectrum, out_grad):
+    n = lax.axis_size("ctx")
+    m = lax.axis_size("ch")
+    place = lax.axis_index("ctx")
+    column = lax.axis_index("ch")
+    rows, depth = features.shape
+    total = rows * n
+    share = n // m
+    pairs = n // 2
+    line = place // 2
+    odd = place % 2
+    block_depth = w_in.shape[0]
+    width = w_in.shape[2]
+    own = width // n
+    sub = own // PARTS
+    sections = n.bit_length() - 1
+    flips = [(i, i ^ 1) for i in range(n)]
+    shifts = [[(i, (i // 2 + s) % pairs * 2 + i % 2) for i in range(n)] for s in range(pairs)]
+    up = [(i, i + 2) for i in range(n - 2)]
+    down = [(i + 2, i) for i in range(n - 2)]
+
+    def trade(value, bit):
+        return lax.ppermute(value, "ch", [(j, j ^ 1 << bit) for j in range(m)])
+
+    up1 = lax.ppermute(features, "ctx", up)
+    down1 = lax.ppermute(features, "ctx", down)
+
+    turned = w_in.reshape(block_depth, 3, pairs, 2, PARTS, sub).transpose(2, 4, 3, 1, 5, 0)
+    turned = turned.reshape(pairs, PARTS * 2 * 3 * sub, block_depth)
+    pieces = []
+    for step in range(m):
+        hops = []
+        for i in range(n):
+            for j in range(m):
+                hops.append((i * m + j, ((j + step) % m * 2 + i % 2) * m + i // 2))
+        piece = lax.dynamic_index_in_dim(turned, (column + step) % m, 0, keepdims=False)
+        if step >= m // 2:
+            piece = after(piece, up1, down1)
+        pieces.append(lax.ppermute(piece, BOTH, hops))
+    pieces += [lax.ppermute(piece, "ctx", flips) for piece in pieces]
+
+    mirrored = (reverse_bits(place, sections) > n // 2).astype(jnp.int32)
+    packed = pack(jnp.stack([mirrored, column]), filter_spectrum, out_grad, n, m)
+
+    up2 = lax.ppermute(up1, "ctx", up)
+    down2 = lax.ppermute(down1, "ctx", down)
+    up3 = lax.ppermute(after(up2, packed), "ctx", up)
+    down3 = lax.ppermute(after(down2, packed), "ctx", down)
+    behind = [
+        jnp.where(line >= 1, up1, down3),
+        jnp.where(line >= 2, up2, down2),
+        jnp.where(line >= 3, up3, down1),
+    ]
+    whole = jnp.zeros((pairs, rows, depth), features.dtype)
+    for shift, value in enumerate([features] + behind):
+        whole = lax.dynamic_update_slice(whole, value[None], ((line - shift) % pairs, 0, 0))
+    whole = whole.reshape(pairs * rows, depth)
+
+    sources = (line - jnp.arange(m, dtype=jnp.int32)) % m ^ column
+    blocks = jnp.concatenate([jnp.full((m,), odd), jnp.full((m,), 1 - odd)])
+    slots = jnp.stack([blocks, jnp.concatenate([sources, sources])])
+
+    packed = after(packed, up3, down3, *pieces[:m])
+    packed = lax.all_to_all(packed, "ctx", split_axis=0, concat_axis=0, tiled=True)
+    response = packed[:, 0].reshape(n, rows // own, own, packed.shape[3])
+
+    taps = lax.dynamic_slice_in_dim(short_filter, place * own, own, 2)
+    taps = taps.reshape(3, 3, PARTS, sub).transpose(2, 0, 1, 3).reshape(PARTS, 3, 3 * sub, 1)
+    sends, keeps = zip(*[multiply(part, slots, whole, pieces, share) for part in range(PARTS)])
+    gots = [trade(send, 0) for send in sends]
+    across = [
+        trade((keep[1] + got[1]).astype(jnp.bfloat16), 1) for keep, got in zip(keeps, gots)
+    ]
+    gated = []
+    for part in range(PARTS):
+        projected = keeps[part][0] + gots[part][0] + across[part].astype(jnp.float32)
+        projected = projected.astype(jnp.bfloat16).reshape(2, 3 * sub, total // 2)
+        mine = lax.dynamic_index_in_dim(projected, odd, 0, keepdims=False)
+        give = lax.dynamic_index_in_dim(projected, 1 - odd, 0, keepdims=False)
+        other = lax.ppermute(give, "ctx", flips)
+        gated.append(
+            convolve(
+                odd.reshape(1), mine, other, taps[part],
+                response[:, :, part * sub : (part + 1) * sub],
+            )
+        )
+
+    grads = packed[:, 1].reshape(total, packed.shape[3])
+    for bit in (1, 0):
+        other = trade(grads, bit)
+        low = column >> bit & 1 == 0
+        if bit == 1:
+            grads = jnp.stack([jnp.where(low, grads, other), jnp.where(low, other, grads)])
+        else:
+            low, high = jnp.where(low, grads, other), jnp.where(low, other, grads)
+            grads = jnp.concatenate([low[0], high[0], low[1], high[1]], axis=1)
+
+    every = jnp.zeros((pairs, 2, PARTS, sub, total), jnp.bfloat16)
+    for part in range(PARTS):
+        near = [gated[part]]
+        near += [lax.ppermute(gated[part], "ctx", shifts[s]) for s in range(1, pairs)]
+        near = jnp.stack(near)
+        other = lax.ppermute(near, "ctx", flips)
+        low = jnp.where(odd == 0, near, other)
+        high = jnp.where(odd == 0, other, near)
+        for shift in range(pairs):
+            every = lax.dynamic_update_slice(
+                every,
+                jnp.stack([low[shift], high[shift]])[None, :, None],
+                ((line - shift) % pairs, 0, part, 0, 0),
+            )
+    every = every.reshape(width, total)
+    w_out_grad = lax.dot_general(
+        grads, every, (((0,), (1,)), ((), ())), preferred_element_type=jnp.float32
+    )
+    out = lax.dynamic_slice_in_dim(every, place * rows, rows, 1).T
+    return (out, w_out_grad)
+
+
 def solution(mesh):
     in_specs = (
         P("ctx", "ch"),
@@ -166,6 +502,7 @@
         P("ctx", None),
     )
     out_specs = (P("ctx", "ch"), P("ctx", "ch"))
+    on_device = special if fits(mesh) else general
     return jax.shard_map(
         on_device, mesh=mesh, in_specs=in_specs, out_specs=out_specs, check_vma=False
     )

time: 273 us -> 177 us (0.65)
  starting transfers between devices: 110 us -> 72.2 us
  waiting for transfers between devices: 93.1 us -> 62 us
  matrix products: 24.4 us -> 2.01 us
  Pallas kernels: 0 us -> 17.3 us
  between operations: 14.7 us -> 1.18 us
  local copies, waits for them, and re-layouts: 20.2 us -> 9.16 us
    ppermute x24 -> x30, starting transfers between devices: 102 us -> 62.7 us  [the longest x1 13.1 us: special(): up3 = lax.ppermute(after(up2, packed), 'ctx', up)]
    ppermute x24 -> x30, waiting for transfers between devices: 83.8 us -> 47.5 us  [the longest x1 19.4 us: special(): up2 = lax.ppermute(up1, 'ctx', up)]
    dot_general x14 -> x1, matrix products: 24.4 us -> 2.01 us  [special(): lax.dot_general(grads, every, (((0,), (1,)), ((), ())), preferred_element...]
    pallas_call x0 -> x5, Pallas kernels: none -> 17.3 us  [the longest x2 10.2 us: multiply(): pl.pallas_call(functools.partial(multiply_kernel, part), out_shape=[out]...]
    all_to_all x2 -> x1, waiting for transfers between devices: 9.27 us -> 14.4 us  [special(): lax.all_to_all(packed, 'ctx', split_axis=0, concat_axis=0, tiled=True)]
    convert_element_type x3 -> x4, other arithmetic: 1.34 us -> 6.15 us  [the longest x2 3.69 us: special(): (keep[1] + got[1]).astype(jnp.bfloat16)]
    another operation x8 -> x7, other arithmetic: 4.37 us -> 0.42 us  [the longest x2 0.15 us: special(): jnp.stack([jnp.where(low, grads, other), jnp.where(low, other, grads)])]
    reshape x2 -> x1, local copies, waits for them, and re-layouts: 3.98 us -> 0.09 us  [special(): taps.reshape(3, 3, PARTS, sub).transpose(2, 0, 1, 3)]
  transfers between devices with their start and end apart: 27 -> 31, of which waited for: 16 -> 10; matrix products, arithmetic and copies ran while one was open for 14% -> 10% of each run, Pallas kernels for 0% -> 7%
where the time goes in v2:
time: 177 us; the launch traced here: 174 us
  starting transfers between devices  72.2 us (41%)
  waiting for transfers between devices  62 us (35%)
  Pallas kernels  17.3 us (10%)
  other arithmetic  10.5 us (6%)
  local copies, waits for them, and re-layouts  9.16 us (5%)
  matrix products  2.01 us (1%)
    ppermute x1, waiting for transfers between devices, special(): up2 = lax.ppermute(up1, 'ctx', up)  19.4 us
    all_to_all x1, waiting for transfers between devices, special(): lax.all_to_all(packed, 'ctx', split_axis=0, concat_axis=0, tiled=True)  14.4 us
    ppermute x1, starting transfers between devices, special(): up3 = lax.ppermute(after(up2, packed), 'ctx', up)  13.1 us
    ppermute x4, starting transfers between devices, special(): pieces.append(lax.ppermute(piece, BOTH, hops))  10.8 us
    pallas_call x2, Pallas kernels, multiply(): pl.pallas_call(functools.partial(multiply_kernel, part), out_shape=[out]...  10.2 us
    ppermute x4, waiting for transfers between devices, special(): pieces += [lax.ppermute(piece, 'ctx', flips) for piece in pieces]  9.59 us
    all_to_all x1, starting transfers between devices, special(): lax.all_to_all(packed, 'ctx', split_axis=0, concat_axis=0, tiled=True)  9.51 us
    ppermute x6, starting transfers between devices, special(): lax.ppermute(gated[part], 'ctx', shifts[s])  9.3 us
  transfers between devices with their start and end apart: 31, of which 10 were waited for; matrix products, arithmetic and copies ran while one was open for 10% of the time, Pallas kernels for 7%

profile of v2, /device:TPU:0, one launch (start us, length us, event | category | flops | bytes accessed | tf_op | source)
XLA Modules:
  0.0 174.4 jit_solution(4034463724606206423)
XLA Ops:
  0.6 1.3 collective-permute-start.1
  1.9 6.3 %collective-permute-start = (bf16[192,1024]{1,0:T(8,128)(2,1)}, bf16[192,1024]{1,0:T(8,128)(2,1)}, u32[]{:S(2)}, u32[]{:S(2)}) collective-permute-start(bf16[192,1024]{1,0:T(8,128)(2,1)} %param.9), channel_id=1, source_target_pairs={{0,8},{4,12},{8,16},{12,20},{16,24},{20,28},{1,9},{5,13},{9,17},{1... | collective-permute-start | bytes 1179656 | tf_op jit(solution)/shard_map/ppermute | solution.py:401
  8.3 1.7 copy.26
  10.0 1.4 copy.27
  11.4 3.6 %collective-permute-done.1 = bf16[192,1024]{1,0:T(8,128)(2,1)} collective-permute-done((bf16[192,1024]{1,0:T(8,128)(2,1)}, bf16[192,1024]{1,0:T(8,128)(2,1)}, u32[]{:S(2)}, u32[]{:S(2)}) %collective-permute-start.1) | collective-permute-done | bytes 393248 | tf_op jit(solution)/shard_map/ppermute | solution.py:402
  15.0 1.3 collective-permute-start.2
  16.3 2.7 %dynamic-slice_bitcast_fusion = (bf16[384,512]{1,0:T(8,128)(2,1)}, bf16[384,512]{1,0:T(8,128)(2,1)}, bf16[384,512]{1,0:T(8,128)(2,1)}, bf16[384,512]{1,0:T(8,128)(2,1)}) fusion(bf16[4,384,512]{2,1,0:T(8,128)(2,1)} %bitcast.138, s32[]{:T(128)S(6)} %select_n.202, s32[]{:T(128)S(6)} %select_n.200, s32[]{:T(128)S(6)} %select_n.198, s32[]{:T(128)S(6)} %select_n.196), kind=kLoop, calls=%fused_computation.35 | loop fusion | bytes 3145744 | tf_op jit(solution)/shard_map/jit(dynamic_index_in_dim)/squeeze | solution.py:412
  19.0 1.6 collective-permute-start.6
  20.7 3.0 %collective-permute-start.7 = (bf16[384,512]{1,0:T(8,128)(2,1)}, bf16[384,512]{1,0:T(8,128)(2,1)S(1)}, u32[]{:S(2)}, u32[]{:S(2)}) collective-permute-start(bf16[384,512]{1,0:T(8,128)(2,1)} %get-tuple-element.30), channel_id=1, source_target_pairs={{0,8},{1,16},{2,24},{3,0},{4,12},{5,20},{6,28},{7,4},{8,9},{9,17},... | collective-permute-start | bytes 1179656 | tf_op jit(solution)/shard_map/ppermute | solution.py:415
  23.7 1.8 %shard_map.104 = bf16[8,2,192,128]{3,2,1,0:T(8,128)(2,1)} custom-call(s32[2]{0:T(128)S(1)} %pad_add_fusion.1.flag_ref, f32[2,192,512]{2,1,0:T(8,128)S(1)} %copy-done.4, bf16[192,4096]{1,0:T(8,128)(2,1)S(1)} %copy-done.1), custom_call_target="tpu_custom_call" | custom-call | flops 100000000 | bytes 4194304 | tf_op jit(solution)/shard_map/pallas_call | solution.py:359
  25.6 2.6 %collective-permute-start.8 = (bf16[384,512]{1,0:T(8,128)(2,1)}, bf16[384,512]{1,0:T(8,128)(2,1)S(1)}, u32[]{:S(2)}, u32[]{:S(2)}) collective-permute-start(bf16[384,512]{1,0:T(8,128)(2,1)} %get-tuple-element.13), channel_id=1, source_target_pairs={{0,16},{1,24},{2,0},{3,8},{4,20},{5,28},{6,4},{7,12},{8,17},{9,25}... | collective-permute-start | bytes 1179656 | tf_op jit(solution)/shard_map/ppermute | solution.py:415
  28.2 3.6 %collective-permute-start.9 = (bf16[384,512]{1,0:T(8,128)(2,1)}, bf16[384,512]{1,0:T(8,128)(2,1)S(1)}, u32[]{:S(2)}, u32[]{:S(2)}) collective-permute-start(bf16[384,512]{1,0:T(8,128)(2,1)} %get-tuple-element.14), channel_id=1, source_target_pairs={{0,24},{1,0},{2,8},{3,16},{4,28},{5,4},{6,12},{7,20},{8,25},{9,1},... | collective-permute-start | bytes 1179656 | tf_op jit(solution)/shard_map/ppermute | solution.py:415
  31.8 3.6 %collective-permute-start.4 = (bf16[192,1024]{1,0:T(8,128)(2,1)}, bf16[192,1024]{1,0:T(8,128)(2,1)S(1)}, u32[]{:S(2)}, u32[]{:S(2)}) collective-permute-start(bf16[192,1024]{1,0:T(8,128)(2,1)} %collective-permute-done), channel_id=1, source_target_pairs={{0,8},{4,12},{8,16},{12,20},{16,24},{20,28},{1,9},{5,13},{9,17},{1... | collective-permute-start | bytes 1179656 | tf_op jit(solution)/shard_map/ppermute | solution.py:421
  35.5 1.3 collective-permute-start.3
  37.2 1.6 collective-permute-start.10
  38.7 19.4 %collective-permute-done.4 = bf16[192,1024]{1,0:T(8,128)(2,1)S(1)} collective-permute-done((bf16[192,1024]{1,0:T(8,128)(2,1)}, bf16[192,1024]{1,0:T(8,128)(2,1)S(1)}, u32[]{:S(2)}, u32[]{:S(2)}) %collective-permute-start.4) | collective-permute-done | bytes 393248 | tf_op jit(solution)/shard_map/ppermute | solution.py:421
  58.2 1.7 collective-permute-start.11
  59.9 13.1 %collective-permute-start.5 = (bf16[192,1024]{1,0:T(8,128)(2,1)S(1)}, bf16[192,1024]{1,0:T(8,128)(2,1)S(1)}, u32[]{:S(2)}, u32[]{:S(2)}) collective-permute-start(bf16[192,1024]{1,0:T(8,128)(2,1)S(1)} %collective-permute-done.4), channel_id=1, source_target_pairs={{0,8},{4,12},{8,16},{12,20},{16,24},{20,28},{1,9},{5,13},{9,17},{1... | collective-permute-start | bytes 1179656 | tf_op jit(solution)/shard_map/ppermute | solution.py:423
  73.5 1.5 collective-permute-start.13
  75.2 1.1 bitcast_dynamic-update-slice_fusion.1
  76.3 2.3 %collective-permute-done.5 = bf16[192,1024]{1,0:T(8,128)(2,1)S(1)} collective-permute-done((bf16[192,1024]{1,0:T(8,128)(2,1)S(1)}, bf16[192,1024]{1,0:T(8,128)(2,1)S(1)}, u32[]{:S(2)}, u32[]{:S(2)}) %collective-permute-start.5) | collective-permute-done | bytes 393248 | tf_op jit(solution)/shard_map/ppermute | solution.py:423
  78.6 1.1 bitcast_dynamic-update-slice_fusion
  79.7 5.3 %collective-permute-done.12.refs_6_ = bf16[384,512]{1,0:T(8,128)(2,1)S(1)} collective-permute-done((bf16[384,512]{1,0:T(8,128)(2,1)S(1)}, bf16[384,512]{1,0:T(8,128)(2,1)S(1)}, u32[]{:S(2)}, u32[]{:S(2)}) %collective-permute-start.12) | collective-permute-done | bytes 393248 | tf_op jit(solution)/shard_map/ppermute | solution.py:416
  85.0 4.3 %collective-permute-done.13.refs_7_ = bf16[384,512]{1,0:T(8,128)(2,1)S(1)} collective-permute-done((bf16[384,512]{1,0:T(8,128)(2,1)S(1)}, bf16[384,512]{1,0:T(8,128)(2,1)S(1)}, u32[]{:S(2)}, u32[]{:S(2)}) %collective-permute-start.13) | collective-permute-done | bytes 393248 | tf_op jit(solution)/shard_map/ppermute | solution.py:416
  89.3 5.1 %shard_map.107 = (f32[2,192,768]{2,1,0:T(8,128)}, f32[2,192,768]{2,1,0:T(8,128)S(1)}) custom-call(s32[2,8]{1,0:T(2,128)S(1)} %pad_add_fusion.slots, bf16[768,1024]{1,0:T(8,128)(2,1)S(1)} %bitcast.131, bf16[384,512]{1,0:T(8,128)(2,1)S(1)} %collective-permute-done.6.refs_0_, bf16[384,512]{1,0:T(8,128)(2,1)S(1)} %collective-permute-done.7.refs_1_, ...), custom_call_target="tpu_custom_call" | custom-call | flops 1207959552 | bytes 6291456 | tf_op jit(solution)/shard_map/pallas_call | solution.py:309
  94.5 5.1 %shard_map.105 = (f32[2,192,768]{2,1,0:T(8,128)}, f32[2,192,768]{2,1,0:T(8,128)S(1)}) custom-call(s32[2,8]{1,0:T(2,128)S(1)} %pad_add_fusion.slots, bf16[768,1024]{1,0:T(8,128)(2,1)S(1)} %bitcast.132, bf16[384,512]{1,0:T(8,128)(2,1)S(1)} %collective-permute-done.6.refs_0_, bf16[384,512]{1,0:T(8,128)(2,1)S(1)} %collective-permute-done.7.refs_1_, ...), custom_call_target="tpu_custom_call" | custom-call | flops 1207959552 | bytes 6291456 | tf_op jit(solution)/shard_map/pallas_call | solution.py:309
  100.2 9.5 %all-to-all-start = ((bf16[8,2,192,128]{3,2,1,0:T(8,128)(2,1)}), bf16[8,2,192,128]{3,2,1,0:T(8,128)(2,1)}, u32[]{:S(2)}, u32[]{:S(2)}) async-start(bf16[8,2,192,128]{3,2,1,0:T(8,128)(2,1)} %shard_map.104), calls=%async_computation | async-start | bytes 1572864 | tf_op jit(solution)/shard_map/all_to_all | solution.py:440
  110.2 1.8 %fusion.17 = bf16[192,768]{1,0:T(8,128)(2,1)} fusion(f32[2,192,768]{2,1,0:T(8,128)} %collective-permute-done.21, f32[2,192,768]{2,1,0:T(8,128)S(1)} %copy-done.3), kind=kLoop, calls=%fused_computation.44 | loop fusion | flops 294912 | bytes 1474560 | tf_op jit(solution)/shard_map/convert_element_type | solution.py:448
  112.0 1.7 collective-permute-start.22
  113.7 1.8 %fusion.16 = bf16[192,768]{1,0:T(8,128)(2,1)} fusion(f32[2,192,768]{2,1,0:T(8,128)} %collective-permute-done.14, f32[2,192,768]{2,1,0:T(8,128)S(1)} %get-tuple-element.15), kind=kLoop, calls=%fused_computation.43 | loop fusion | flops 294912 | bytes 1474560 | tf_op jit(solution)/shard_map/convert_element_type | solution.py:448
  115.9 14.4 %all-to-all-done = bf16[8,2,192,128]{3,2,1,0:T(8,128)(2,1)} async-done(((bf16[8,2,192,128]{3,2,1,0:T(8,128)(2,1)}), bf16[8,2,192,128]{3,2,1,0:T(8,128)(2,1)}, u32[]{:S(2)}, u32[]{:S(2)}) %all-to-all-start) | async-done | bytes 786464 | tf_op jit(solution)/shard_map/all_to_all | solution.py:440
  130.3 1.2 fusion.29
  131.5 1.3 fusion.11
  132.8 1.5 collective-permute-start.23
  134.3 1.2 fusion.15
  136.2 2.9 %collective-permute-done.23.other_ref = bf16[96,768]{1,0:T(8,128)(2,1)S(1)} collective-permute-done((bf16[96,768]{1,0:T(8,128)(2,1)S(1)}, bf16[96,768]{1,0:T(8,128)(2,1)S(1)}, u32[]{:S(2)}, u32[]{:S(2)}) %collective-permute-start.23) | collective-permute-done | bytes 147488 | tf_op jit(solution)/shard_map/ppermute | solution.py:456
  139.1 2.6 %shard_map.108 = bf16[32,1536]{1,0:T(8,128)(2,1)S(1)} custom-call(s32[1]{0:T(128)} %bitcast.odd_ref, bf16[96,768]{1,0:T(8,128)(2,1)S(1)} %get-tuple-element.63.mine_ref, bf16[96,768]{1,0:T(8,128)(2,1)S(1)} %collective-permute-done.23.other_ref, f32[3,96,1]{2,1,0:T(8,128)S(1)} %squeeze.67.taps_ref, ...), custom_call_target="tpu_custom_call" | custom-call | flops 1000000000 | bytes 4000000 | tf_op jit(solution)/shard_map/pallas_call | solution.py:262
  143.4 2.2 %collective-permute-start.26 = (bf16[32,1536]{1,0:T(8,128)(2,1)S(1)}, bf16[32,1536]{1,0:T(8,128)(2,1)S(1)}, u32[]{:S(2)}, u32[]{:S(2)}) collective-permute-start(bf16[32,1536]{1,0:T(8,128)(2,1)S(1)} %shard_map.108), channel_id=1, source_target_pairs={{0,24},{4,28},{8,0},{12,4},{16,8},{20,12},{24,16},{28,20},{1,25},{... | collective-permute-start | bytes 294920 | tf_op jit(solution)/shard_map/ppermute | solution.py:477
  145.8 1.8 %collective-permute-start.28 = (bf16[1536,128]{1,0:T(8,128)(2,1)S(1)}, bf16[1536,128]{1,0:T(8,128)(2,1)S(1)}, u32[]{:S(2)}, u32[]{:S(2)}) collective-permute-start(bf16[1536,128]{1,0:T(8,128)(2,1)S(1)} %bitcast.142), channel_id=1, source_target_pairs={{0,2},{1,3},{2,0},{3,1},{4,6},{5,7},{6,4},{7,5},{8,10},{9,11},{10,... | collective-permute-start | bytes 1179656 | tf_op jit(solution)/shard_map/ppermute | solution.py:399
  147.6 2.6 %shard_map.106 = bf16[32,1536]{1,0:T(8,128)(2,1)S(1)} custom-call(s32[1]{0:T(128)} %bitcast.odd_ref, bf16[96,768]{1,0:T(8,128)(2,1)S(1)} %get-tuple-element.65.mine_ref, bf16[96,768]{1,0:T(8,128)(2,1)S(1)} %collective-permute-done.16.other_ref, f32[3,96,1]{2,1,0:T(8,128)S(1)} %squeeze.66.taps_ref, ...), custom_call_target="tpu_custom_call" | custom-call | flops 1000000000 | bytes 4000000 | tf_op jit(solution)/shard_map/pallas_call | solution.py:262
  150.8 1.5 collective-permute-start.18
  152.4 3.3 %collective-permute-start.19 = (bf16[32,1536]{1,0:T(8,128)(2,1)S(1)}, bf16[32,1536]{1,0:T(8,128)(2,1)S(1)}, u32[]{:S(2)}, u32[]{:S(2)}) collective-permute-start(bf16[32,1536]{1,0:T(8,128)(2,1)S(1)} %shard_map.106), channel_id=1, source_target_pairs={{0,24},{4,28},{8,0},{12,4},{16,8},{20,12},{24,16},{28,20},{1,25},{... | collective-permute-start | bytes 294920 | tf_op jit(solution)/shard_map/ppermute | solution.py:477
  155.7 1.8 %collective-permute-start.27 = (bf16[4,32,1536]{2,1,0:T(8,128)(2,1)S(1)}, bf16[4,32,1536]{2,1,0:T(8,128)(2,1)S(1)}, u32[]{:S(2)}, u32[]{:S(2)}) collective-permute-start(bf16[4,32,1536]{2,1,0:T(8,128)(2,1)S(1)} %pad_maximum_fusion.2), channel_id=1, source_target_pairs={{0,4},{4,0},{8,12},{12,8},{16,20},{20,16},{24,28},{28,24},{1,5},{5... | collective-permute-start | bytes 1179656 | tf_op jit(solution)/shard_map/ppermute | solution.py:479
  158.6 1.8 %collective-permute-start.20 = (bf16[4,32,1536]{2,1,0:T(8,128)(2,1)S(1)}, bf16[4,32,1536]{2,1,0:T(8,128)(2,1)S(1)}, u32[]{:S(2)}, u32[]{:S(2)}) collective-permute-start(bf16[4,32,1536]{2,1,0:T(8,128)(2,1)S(1)} %pad_maximum_fusion.1), channel_id=1, source_target_pairs={{0,4},{4,0},{8,12},{12,8},{16,20},{20,16},{24,28},{28,24},{1,5},{5... | collective-permute-start | bytes 1179656 | tf_op jit(solution)/shard_map/ppermute | solution.py:479
  160.7 4.6 %collective-permute-done.27 = bf16[4,32,1536]{2,1,0:T(8,128)(2,1)S(1)} collective-permute-done((bf16[4,32,1536]{2,1,0:T(8,128)(2,1)S(1)}, bf16[4,32,1536]{2,1,0:T(8,128)(2,1)S(1)}, u32[]{:S(2)}, u32[]{:S(2)}) %collective-permute-start.27) | collective-permute-done | bytes 393248 | tf_op jit(solution)/shard_map/ppermute | solution.py:479
  165.5 4.1 %collective-permute-done.20 = bf16[4,32,1536]{2,1,0:T(8,128)(2,1)S(1)} collective-permute-done((bf16[4,32,1536]{2,1,0:T(8,128)(2,1)S(1)}, bf16[4,32,1536]{2,1,0:T(8,128)(2,1)S(1)}, u32[]{:S(2)}, u32[]{:S(2)}) %collective-permute-start.20) | collective-permute-done | bytes 393248 | tf_op jit(solution)/shard_map/ppermute | solution.py:479
  171.0 1.2 broadcast_select_fusion.1
  172.4 2.0 %fusion = f32[512,512]{1,0:T(8,128)} fusion(bf16[512,1536]{1,0:T(8,128)(2,1)S(1)} %bitcast.140, bf16[1536,128]{1,0:T(8,128)(2,1)S(1)} %get-tuple-element.35, bf16[1536,128]{1,0:T(8,128)(2,1)S(1)} %get-tuple-element.68, bf16[1536,128]{1,0:T(8,128)(2,1)S(1)} %get-tuple-element.34, bf16[1536,128]{1,0:T(8,128)(2,1)S(1)} %get-tuple-element.69), kind=kOutput, calls=%fused_computation | convolution fusion | flops 811597824 | bytes 4194304 | tf_op jit(solution)/shard_map/dot_general | solution.py:489
  (85 shorter events, 8.7 us)
Async XLA Ops:
  0.6 109.1 %copy-start = (f32[3,3,512]{2,1,0:T(4,128)S(1)}, f32[3,3,512]{2,1,0:T(4,128)}, u32[]{:S(2)}) copy-start(f32[3,3,512]{2,1,0:T(4,128)} %param.11) | copy-start | bytes 55300
  0.6 14.4 %collective-permute-start.1 = (bf16[192,1024]{1,0:T(8,128)(2,1)}, bf16[192,1024]{1,0:T(8,128)(2,1)}, u32[]{:S(2)}, u32[]{:S(2)}) collective-permute-start(bf16[192,1024]{1,0:T(8,128)(2,1)} %param.9), channel_id=1, source_target_pairs={{8,0},{12,4},{16,8},{20,12},{24,16},{28,20},{9,1},{13,5},{17,9},{2... | collective-permute-start | bytes 1179656 | tf_op jit(solution)/shard_map/ppermute | solution.py:402
  1.9 23.6 %collective-permute-start = (bf16[192,1024]{1,0:T(8,128)(2,1)}, bf16[192,1024]{1,0:T(8,128)(2,1)}, u32[]{:S(2)}, u32[]{:S(2)}) collective-permute-start(bf16[192,1024]{1,0:T(8,128)(2,1)} %param.9), channel_id=1, source_target_pairs={{0,8},{4,12},{8,16},{12,20},{16,24},{20,28},{1,9},{5,13},{9,17},{1... | collective-permute-start | bytes 1179656 | tf_op jit(solution)/shard_map/ppermute | solution.py:401
  15.0 16.8 %collective-permute-start.2 = (bf16[192,1024]{1,0:T(8,128)(2,1)}, bf16[192,1024]{1,0:T(8,128)(2,1)}, u32[]{:S(2)}, u32[]{:S(2)}) collective-permute-start(bf16[192,1024]{1,0:T(8,128)(2,1)} %collective-permute-done.1), channel_id=1, source_target_pairs={{8,0},{12,4},{16,8},{20,12},{24,16},{28,20},{9,1},{13,5},{17,9},{2... | collective-permute-start | bytes 1179656 | tf_op jit(solution)/shard_map/ppermute | solution.py:422
  16.3 7.4 %copy-start.1 = (bf16[192,4096]{1,0:T(8,128)(2,1)S(1)}, bf16[192,4096]{1,0:T(8,128)(2,1)}, u32[]{:S(2)}) copy-start(bf16[192,4096]{1,0:T(8,128)(2,1)} %grad_ref.1) | copy-start | bytes 4718596
  16.3 7.4 %copy-start.4 = (f32[2,192,512]{2,1,0:T(8,128)S(1)}, f32[2,192,512]{2,1,0:T(8,128)}, u32[]{:S(2)}) copy-start(f32[2,192,512]{2,1,0:T(8,128)} %value_ref.1) | copy-start | bytes 2359300
  19.0 16.4 %collective-permute-start.6 = (bf16[384,512]{1,0:T(8,128)(2,1)}, bf16[384,512]{1,0:T(8,128)(2,1)S(1)}, u32[]{:S(2)}, u32[]{:S(2)}) collective-permute-start(bf16[384,512]{1,0:T(8,128)(2,1)} %get-tuple-element.31), channel_id=1, source_target_pairs={{0,0},{1,8},{2,16},{3,24},{4,4},{5,12},{6,20},{7,28},{8,1},{9,9},{... | collective-permute-start | bytes 1179656 | tf_op jit(solution)/shard_map/ppermute | solution.py:415
  20.7 16.5 %collective-permute-start.7 = (bf16[384,512]{1,0:T(8,128)(2,1)}, bf16[384,512]{1,0:T(8,128)(2,1)S(1)}, u32[]{:S(2)}, u32[]{:S(2)}) collective-permute-start(bf16[384,512]{1,0:T(8,128)(2,1)} %get-tuple-element.30), channel_id=1, source_target_pairs={{0,8},{1,16},{2,24},{3,0},{4,12},{5,20},{6,28},{7,4},{8,9},{9,17},... | collective-permute-start | bytes 1179656 | tf_op jit(solution)/shard_map/ppermute | solution.py:415
  25.6 11.5 %copy-start.7 = (bf16[192,1024]{1,0:T(8,128)(2,1)S(1)}, bf16[192,1024]{1,0:T(8,128)(2,1)}, u32[]{:S(2)}) copy-start(bf16[192,1024]{1,0:T(8,128)(2,1)} %param.9) | copy-start | bytes 1179652
  25.6 34.3 %collective-permute-start.8 = (bf16[384,512]{1,0:T(8,128)(2,1)}, bf16[384,512]{1,0:T(8,128)(2,1)S(1)}, u32[]{:S(2)}, u32[]{:S(2)}) collective-permute-start(bf16[384,512]{1,0:T(8,128)(2,1)} %get-tuple-element.13), channel_id=1, source_target_pairs={{0,16},{1,24},{2,0},{3,8},{4,20},{5,28},{6,4},{7,12},{8,17},{9,25}... | collective-permute-start | bytes 1179656 | tf_op jit(solution)/shard_map/ppermute | solution.py:415
  28.2 44.7 %collective-permute-start.9 = (bf16[384,512]{1,0:T(8,128)(2,1)}, bf16[384,512]{1,0:T(8,128)(2,1)S(1)}, u32[]{:S(2)}, u32[]{:S(2)}) collective-permute-start(bf16[384,512]{1,0:T(8,128)(2,1)} %get-tuple-element.14), channel_id=1, source_target_pairs={{0,24},{1,0},{2,8},{3,16},{4,28},{5,4},{6,12},{7,20},{8,25},{9,1},... | collective-permute-start | bytes 1179656 | tf_op jit(solution)/shard_map/ppermute | solution.py:415
  31.8 26.4 %collective-permute-start.4 = (bf16[192,1024]{1,0:T(8,128)(2,1)}, bf16[192,1024]{1,0:T(8,128)(2,1)S(1)}, u32[]{:S(2)}, u32[]{:S(2)}) collective-permute-start(bf16[192,1024]{1,0:T(8,128)(2,1)} %collective-permute-done), channel_id=1, source_target_pairs={{0,8},{4,12},{8,16},{12,20},{16,24},{20,28},{1,9},{5,13},{9,17},{1... | collective-permute-start | bytes 1179656 | tf_op jit(solution)/shard_map/ppermute | solution.py:421
  35.5 38.0 %collective-permute-start.3 = (bf16[192,1024]{1,0:T(8,128)(2,1)}, bf16[192,1024]{1,0:T(8,128)(2,1)S(1)}, u32[]{:S(2)}, u32[]{:S(2)}) collective-permute-start(bf16[192,1024]{1,0:T(8,128)(2,1)} %collective-permute-done.2), channel_id=1, source_target_pairs={{8,0},{12,4},{16,8},{20,12},{24,16},{28,20},{9,1},{13,5},{17,9},{2... | collective-permute-start | bytes 1179656 | tf_op jit(solution)/shard_map/ppermute | solution.py:424
  37.2 42.5 %collective-permute-start.10 = (bf16[384,512]{1,0:T(8,128)(2,1)S(1)}, bf16[384,512]{1,0:T(8,128)(2,1)S(1)}, u32[]{:S(2)}, u32[]{:S(2)}) collective-permute-start(bf16[384,512]{1,0:T(8,128)(2,1)S(1)} %collective-permute-done.6.refs_0_), channel_id=1, source_target_pairs={{0,4},{4,0},{8,12},{12,8},{16,20},{20,16},{24,28},{28,24},{1,5},{5... | collective-permute-start | bytes 1179656 | tf_op jit(solution)/shard_map/ppermute | solution.py:416
  58.2 21.5 %collective-permute-start.11 = (bf16[384,512]{1,0:T(8,128)(2,1)S(1)}, bf16[384,512]{1,0:T(8,128)(2,1)S(1)}, u32[]{:S(2)}, u32[]{:S(2)}) collective-permute-start(bf16[384,512]{1,0:T(8,128)(2,1)S(1)} %collective-permute-done.7.refs_1_), channel_id=1, source_target_pairs={{0,4},{4,0},{8,12},{12,8},{16,20},{20,16},{24,28},{28,24},{1,5},{5... | collective-permute-start | bytes 1179656 | tf_op jit(solution)/shard_map/ppermute | solution.py:416
  59.9 18.7 %collective-permute-start.5 = (bf16[192,1024]{1,0:T(8,128)(2,1)S(1)}, bf16[192,1024]{1,0:T(8,128)(2,1)S(1)}, u32[]{:S(2)}, u32[]{:S(2)}) collective-permute-start(bf16[192,1024]{1,0:T(8,128)(2,1)S(1)} %collective-permute-done.4), channel_id=1, source_target_pairs={{0,8},{4,12},{8,16},{12,20},{16,24},{20,28},{1,9},{5,13},{9,17},{1... | collective-permute-start | bytes 1179656 | tf_op jit(solution)/shard_map/ppermute | solution.py:423
  72.9 12.1 %collective-permute-start.12 = (bf16[384,512]{1,0:T(8,128)(2,1)S(1)}, bf16[384,512]{1,0:T(8,128)(2,1)S(1)}, u32[]{:S(2)}, u32[]{:S(2)}) collective-permute-start(bf16[384,512]{1,0:T(8,128)(2,1)S(1)} %collective-permute-done.8.refs_2_), channel_id=1, source_target_pairs={{0,4},{4,0},{8,12},{12,8},{16,20},{20,16},{24,28},{28,24},{1,5},{5... | collective-permute-start | bytes 1179656 | tf_op jit(solution)/shard_map/ppermute | solution.py:416
  73.5 15.8 %collective-permute-start.13 = (bf16[384,512]{1,0:T(8,128)(2,1)S(1)}, bf16[384,512]{1,0:T(8,128)(2,1)S(1)}, u32[]{:S(2)}, u32[]{:S(2)}) collective-permute-start(bf16[384,512]{1,0:T(8,128)(2,1)S(1)} %collective-permute-done.9.refs_3_), channel_id=1, source_target_pairs={{0,4},{4,0},{8,12},{12,8},{16,20},{20,16},{24,28},{28,24},{1,5},{5... | collective-permute-start | bytes 1179656 | tf_op jit(solution)/shard_map/ppermute | solution.py:416
  94.4 5.2 %copy-start.2 = (f32[2,192,768]{2,1,0:T(8,128)}, f32[2,192,768]{2,1,0:T(8,128)S(1)}, u32[]{:S(2)}) copy-start(f32[2,192,768]{2,1,0:T(8,128)S(1)} %get-tuple-element.18) | copy-start | bytes 3538948
  94.4 15.7 %collective-permute-start.21 = (f32[2,192,768]{2,1,0:T(8,128)}, f32[2,192,768]{2,1,0:T(8,128)}, u32[]{:S(2)}, u32[]{:S(2)}) collective-permute-start(f32[2,192,768]{2,1,0:T(8,128)} %get-tuple-element.19), channel_id=1, source_target_pairs={{0,1},{1,0},{2,3},{3,2},{4,5},{5,4},{6,7},{7,6},{8,9},{9,8},{10,11... | collective-permute-start | bytes 3538952 | tf_op jit(solution)/shard_map/ppermute | solution.py:399
  99.7 10.5 %copy-start.3 = (f32[2,192,768]{2,1,0:T(8,128)S(1)}, f32[2,192,768]{2,1,0:T(8,128)}, u32[]{:S(2)}) copy-start(f32[2,192,768]{2,1,0:T(8,128)} %copy-done.2) | copy-start | bytes 3538948
  99.7 14.0 %collective-permute-start.14 = (f32[2,192,768]{2,1,0:T(8,128)}, f32[2,192,768]{2,1,0:T(8,128)}, u32[]{:S(2)}, u32[]{:S(2)}) collective-permute-start(f32[2,192,768]{2,1,0:T(8,128)} %get-tuple-element.16), channel_id=1, source_target_pairs={{0,1},{1,0},{2,3},{3,2},{4,5},{5,4},{6,7},{7,6},{8,9},{9,8},{10,11... | collective-permute-start | bytes 3538952 | tf_op jit(solution)/shard_map/ppermute | solution.py:399
  100.2 30.1 %all-to-all-start = ((bf16[8,2,192,128]{3,2,1,0:T(8,128)(2,1)}), bf16[8,2,192,128]{3,2,1,0:T(8,128)(2,1)}, u32[]{:S(2)}, u32[]{:S(2)}) async-start(bf16[8,2,192,128]{3,2,1,0:T(8,128)(2,1)} %shard_map.104), calls=%async_computation | async-start | bytes 1572864 | tf_op jit(solution)/shard_map/all_to_all | solution.py:440
  112.0 19.5 %collective-permute-start.22 = (bf16[192,768]{1,0:T(8,128)(2,1)}, bf16[192,768]{1,0:T(8,128)(2,1)}, u32[]{:S(2)}, u32[]{:S(2)}) collective-permute-start(bf16[192,768]{1,0:T(8,128)(2,1)} %fusion.17), channel_id=1, source_target_pairs={{0,2},{1,3},{2,0},{3,1},{4,6},{5,7},{6,4},{7,5},{8,10},{9,11},{10,... | collective-permute-start | bytes 884744 | tf_op jit(solution)/shard_map/ppermute | solution.py:399
  115.5 18.8 %collective-permute-start.15 = (bf16[192,768]{1,0:T(8,128)(2,1)}, bf16[192,768]{1,0:T(8,128)(2,1)S(1)}, u32[]{:S(2)}, u32[]{:S(2)}) collective-permute-start(bf16[192,768]{1,0:T(8,128)(2,1)} %fusion.16), channel_id=1, source_target_pairs={{0,2},{1,3},{2,0},{3,1},{4,6},{5,7},{6,4},{7,5},{8,10},{9,11},{10,... | collective-permute-start | bytes 884744 | tf_op jit(solution)/shard_map/ppermute | solution.py:399
  132.8 6.3 %copy-start.5 = (f32[192,512]{1,0:T(8,128)S(1)}, f32[192,512]{1,0:T(8,128)}, u32[]{:S(2)}) copy-start(f32[192,512]{1,0:T(8,128)} %constant.139.clone.table_ref) | copy-start | bytes 1179652
  132.8 6.3 %copy-start.6 = (f32[2,5,192]{2,1,0:T(8,128)S(1)}, f32[2,5,192]{2,1,0:T(8,128)}, u32[]{:S(2)}) copy-start(f32[2,5,192]{2,1,0:T(8,128)} %constant.140.clone.turn_ref) | copy-start | bytes 23044
  132.8 6.3 %collective-permute-start.23 = (bf16[96,768]{1,0:T(8,128)(2,1)S(1)}, bf16[96,768]{1,0:T(8,128)(2,1)S(1)}, u32[]{:S(2)}, u32[]{:S(2)}) collective-permute-start(bf16[96,768]{1,0:T(8,128)(2,1)S(1)} %get-tuple-element.62), channel_id=1, source_target_pairs={{0,4},{4,0},{8,12},{12,8},{16,20},{20,16},{24,28},{28,24},{1,5},{5... | collective-permute-start | bytes 442376 | tf_op jit(solution)/shard_map/ppermute | solution.py:456
  135.5 12.0 %collective-permute-start.16 = (bf16[96,768]{1,0:T(8,128)(2,1)S(1)}, bf16[96,768]{1,0:T(8,128)(2,1)S(1)}, u32[]{:S(2)}, u32[]{:S(2)}) collective-permute-start(bf16[96,768]{1,0:T(8,128)(2,1)S(1)} %get-tuple-element.64), channel_id=1, source_target_pairs={{0,4},{4,0},{8,12},{12,8},{16,20},{20,16},{24,28},{28,24},{1,5},{5... | collective-permute-start | bytes 442376 | tf_op jit(solution)/shard_map/ppermute | solution.py:456
  141.8 9.1 %collective-permute-start.24 = (bf16[32,1536]{1,0:T(8,128)(2,1)S(1)}, bf16[32,1536]{1,0:T(8,128)(2,1)S(1)}, u32[]{:S(2)}, u32[]{:S(2)}) collective-permute-start(bf16[32,1536]{1,0:T(8,128)(2,1)S(1)} %shard_map.108), channel_id=1, source_target_pairs={{0,8},{4,12},{8,16},{12,20},{16,24},{20,28},{24,0},{28,4},{1,9},{5... | collective-permute-start | bytes 294920 | tf_op jit(solution)/shard_map/ppermute | solution.py:477
  142.5 9.9 %collective-permute-start.25 = (bf16[32,1536]{1,0:T(8,128)(2,1)S(1)}, bf16[32,1536]{1,0:T(8,128)(2,1)S(1)}, u32[]{:S(2)}, u32[]{:S(2)}) collective-permute-start(bf16[32,1536]{1,0:T(8,128)(2,1)S(1)} %shard_map.108), channel_id=1, source_target_pairs={{0,16},{4,20},{8,24},{12,28},{16,0},{20,4},{24,8},{28,12},{1,17},{... | collective-permute-start | bytes 294920 | tf_op jit(solution)/shard_map/ppermute | solution.py:477
  143.4 12.2 %collective-permute-start.26 = (bf16[32,1536]{1,0:T(8,128)(2,1)S(1)}, bf16[32,1536]{1,0:T(8,128)(2,1)S(1)}, u32[]{:S(2)}, u32[]{:S(2)}) collective-permute-start(bf16[32,1536]{1,0:T(8,128)(2,1)S(1)} %shard_map.108), channel_id=1, source_target_pairs={{0,24},{4,28},{8,0},{12,4},{16,8},{20,12},{24,16},{28,20},{1,25},{... | collective-permute-start | bytes 294920 | tf_op jit(solution)/shard_map/ppermute | solution.py:477
  145.8 14.6 %collective-permute-start.28 = (bf16[1536,128]{1,0:T(8,128)(2,1)S(1)}, bf16[1536,128]{1,0:T(8,128)(2,1)S(1)}, u32[]{:S(2)}, u32[]{:S(2)}) collective-permute-start(bf16[1536,128]{1,0:T(8,128)(2,1)S(1)} %bitcast.142), channel_id=1, source_target_pairs={{0,2},{1,3},{2,0},{3,1},{4,6},{5,7},{6,4},{7,5},{8,10},{9,11},{10,... | collective-permute-start | bytes 1179656 | tf_op jit(solution)/shard_map/ppermute | solution.py:399
  150.2 7.3 %collective-permute-start.17 = (bf16[32,1536]{1,0:T(8,128)(2,1)S(1)}, bf16[32,1536]{1,0:T(8,128)(2,1)S(1)}, u32[]{:S(2)}, u32[]{:S(2)}) collective-permute-start(bf16[32,1536]{1,0:T(8,128)(2,1)S(1)} %shard_map.106), channel_id=1, source_target_pairs={{0,8},{4,12},{8,16},{12,20},{16,24},{20,28},{24,0},{28,4},{1,9},{5... | collective-permute-start | bytes 294920 | tf_op jit(solution)/shard_map/ppermute | solution.py:477
  150.8 7.7 %collective-permute-start.18 = (bf16[32,1536]{1,0:T(8,128)(2,1)S(1)}, bf16[32,1536]{1,0:T(8,128)(2,1)S(1)}, u32[]{:S(2)}, u32[]{:S(2)}) collective-permute-start(bf16[32,1536]{1,0:T(8,128)(2,1)S(1)} %shard_map.106), channel_id=1, source_target_pairs={{0,16},{4,20},{8,24},{12,28},{16,0},{20,4},{24,8},{28,12},{1,17},{... | collective-permute-start | bytes 294920 | tf_op jit(solution)/shard_map/ppermute | solution.py:477
  152.4 6.2 %collective-permute-start.19 = (bf16[32,1536]{1,0:T(8,128)(2,1)S(1)}, bf16[32,1536]{1,0:T(8,128)(2,1)S(1)}, u32[]{:S(2)}, u32[]{:S(2)}) collective-permute-start(bf16[32,1536]{1,0:T(8,128)(2,1)S(1)} %shard_map.106), channel_id=1, source_target_pairs={{0,24},{4,28},{8,0},{12,4},{16,8},{20,12},{24,16},{28,20},{1,25},{... | collective-permute-start | bytes 294920 | tf_op jit(solution)/shard_map/ppermute | solution.py:477
  155.7 9.6 %collective-permute-start.27 = (bf16[4,32,1536]{2,1,0:T(8,128)(2,1)S(1)}, bf16[4,32,1536]{2,1,0:T(8,128)(2,1)S(1)}, u32[]{:S(2)}, u32[]{:S(2)}) collective-permute-start(bf16[4,32,1536]{2,1,0:T(8,128)(2,1)S(1)} %pad_maximum_fusion.2), channel_id=1, source_target_pairs={{0,4},{4,0},{8,12},{12,8},{16,20},{20,16},{24,28},{28,24},{1,5},{5... | collective-permute-start | bytes 1179656 | tf_op jit(solution)/shard_map/ppermute | solution.py:479
  158.6 10.9 %collective-permute-start.20 = (bf16[4,32,1536]{2,1,0:T(8,128)(2,1)S(1)}, bf16[4,32,1536]{2,1,0:T(8,128)(2,1)S(1)}, u32[]{:S(2)}, u32[]{:S(2)}) collective-permute-start(bf16[4,32,1536]{2,1,0:T(8,128)(2,1)S(1)} %pad_maximum_fusion.1), channel_id=1, source_target_pairs={{0,4},{4,0},{8,12},{12,8},{16,20},{20,16},{24,28},{28,24},{1,5},{5... | collective-permute-start | bytes 1179656 | tf_op jit(solution)/shard_map/ppermute | solution.py:479
  160.6 10.4 %collective-permute-start.29 = (bf16[2,1536,128]{2,1,0:T(8,128)(2,1)S(1)}, bf16[2,1536,128]{2,1,0:T(8,128)(2,1)}, u32[]{:S(2)}, u32[]{:S(2)}) collective-permute-start(bf16[2,1536,128]{2,1,0:T(8,128)(2,1)S(1)} %pad_maximum_fusion), channel_id=1, source_target_pairs={{0,1},{1,0},{2,3},{3,2},{4,5},{5,4},{6,7},{7,6},{8,9},{9,8},{10,11... | collective-permute-start | bytes 2359304 | tf_op jit(solution)/shard_map/ppermute | solution.py:399

commit v3 on v2

--- a/solution.py
+++ b/solution.py
@@ -208,7 +208,7 @@
             ins += [real[r] * cos + imag[r] * sin, imag[r] * cos - real[r] * sin]
     spectrum = exact(jnp.concatenate(ins, axis=0), table_ref[...])
     response = [
-        jnp.concatenate([response_ref[ORDER[r], i] for i in range(response_ref.shape[1])], axis=1)
+        jnp.concatenate([response_ref[odd_ref[1 + r], i] for i in range(response_ref.shape[1])], axis=1)
         for r in range(8)
     ]
     response = [value.astype(jnp.float32) for value in response]
@@ -269,61 +269,6 @@
 PARTS = 2
 
 
-def multiply_kernel(part, slots, whole_ref, *refs):
-    send_ref, keep_ref, held, sems = refs[-4:]
-    pieces = refs[:-4]
-    share, spots, spot, block_depth = held.shape
-    copies = []
-    for step, piece in enumerate(pieces):
-        copies.append(
-            pltpu.make_async_copy(
-                piece.at[pl.ds(part * spot, spot)],
-                held.at[slots[0, step], slots[1, step]],
-                sems.at[step],
-            )
-        )
-    for copy in copies:
-        copy.start()
-    for copy in copies:
-        copy.wait()
-    for place in (1, 3, 2, 0):
-        total = jnp.zeros((spot, whole_ref.shape[0]), jnp.float32)
-        for block in range(share):
-            total += lax.dot_general(
-                held[block, place],
-                whole_ref[:, block * block_depth : (block + 1) * block_depth],
-                (((1,), (1,)), ((), ())),
-                preferred_element_type=jnp.float32,
-            )
-        out_ref = send_ref if place % 2 else keep_ref
-        out_ref[place // 2] = total
-
-
-def multiply(part, slots, whole, pieces, share):
-    rows, block_depth = pieces[0].shape
-    spot = rows // PARTS
-    spots = len(pieces) // share
-    vmem = pl.BlockSpec(memory_space=pltpu.VMEM)
-    anywhere = pl.BlockSpec(memory_space=pl.ANY)
-    out = jax.ShapeDtypeStruct((spots // 2, spot, whole.shape[0]), jnp.float32)
-    return pl.pallas_call(
-        functools.partial(multiply_kernel, part),
-        out_shape=[out] * 2,
-        in_specs=[pl.BlockSpec(memory_space=pltpu.SMEM), vmem] + [anywhere] * len(pieces),
-        out_specs=[vmem] * 2,
-        scratch_shapes=[
-            pltpu.VMEM((share, spots, spot, block_depth), jnp.bfloat16),
-            pltpu.SemaphoreType.DMA((len(pieces),)),
-        ],
-        compiler_params=pltpu.CompilerParams(vmem_limit_bytes=32 * 2**20),
-        cost_estimate=pl.CostEstimate(
-            flops=2 * spots * spot * whole.shape[0] * whole.shape[1],
-            bytes_accessed=6 * 2**20,
-            transcendentals=0,
-        ),
-    )(slots, whole, *pieces)
-
-
 def pack_kernel(flag_ref, value_ref, grad_ref, out_ref):
     rows = value_ref.shape[1]
     n, _, count, lanes = out_ref.shape
@@ -366,6 +311,34 @@
     )(flags, value, grad)
 
 
+def cut_kernel(step, which_ref, value_ref, *outs):
+    kinds, _, width = value_ref.shape
+    size = width // len(outs)
+    for index, out_ref in enumerate(outs):
+        start = pl.multiple_of(which_ref[index] * size, size)
+        for kind in range(kinds):
+            piece = value_ref[kind, :, pl.ds(start, size)].T
+            for group in range(size // step):
+                place = group % PARTS * 2 + group // PARTS
+                first = (place * kinds + kind) * step
+                out_ref[first : first + step] = piece[group * step : (group + 1) * step]
+
+
+def cut(step, which, value):
+    kinds, deep, width = value.shape
+    vmem = pl.BlockSpec(memory_space=pltpu.VMEM)
+    count = which.shape[0]
+    out = jax.ShapeDtypeStruct((kinds * width // count, deep), value.dtype)
+    return pl.pallas_call(
+        functools.partial(cut_kernel, step),
+        out_shape=[out] * count,
+        in_specs=[pl.BlockSpec(memory_space=pltpu.SMEM), vmem],
+        out_specs=[vmem] * count,
+        compiler_params=pltpu.CompilerParams(vmem_limit_bytes=32 * 2**20),
+        cost_estimate=pl.CostEstimate(flops=0, bytes_accessed=3 * 2**20, transcendentals=0),
+    )(which, value)
+
+
 def fits(mesh):
     return mesh.shape["ctx"] == 8 and mesh.shape["ch"] == 4
 
@@ -401,16 +374,15 @@
     up1 = lax.ppermute(features, "ctx", up)
     down1 = lax.ppermute(features, "ctx", down)
 
-    turned = w_in.reshape(block_depth, 3, pairs, 2, PARTS, sub).transpose(2, 4, 3, 1, 5, 0)
-    turned = turned.reshape(pairs, PARTS * 2 * 3 * sub, block_depth)
+    which = (column + jnp.arange(m, dtype=jnp.int32)) % m
+    turned = cut(sub, which, w_in.transpose(1, 0, 2))
     pieces = []
-    for step in range(m):
+    for step, piece in enumerate(turned):
         hops = []
         for i in range(n):
             for j in range(m):
                 hops.append((i * m + j, ((j + step) % m * 2 + i % 2) * m + i // 2))
-        piece = lax.dynamic_index_in_dim(turned, (column + step) % m, 0, keepdims=False)
-        if step >= m // 2:
+        if step == m - 1:
             piece = after(piece, up1, down1)
         pieces.append(lax.ppermute(piece, BOTH, hops))
     pieces += [lax.ppermute(piece, "ctx", flips) for piece in pieces]
@@ -429,24 +401,60 @@
     ]
     whole = jnp.zeros((pairs, rows, depth), features.dtype)
     for shift, value in enumerate([features] + behind):
+        value = jnp.where(
+            odd == 0,
+            value,
+            jnp.concatenate([value[:, block_depth:], value[:, :block_depth]], axis=1),
+        )
         whole = lax.dynamic_update_slice(whole, value[None], ((line - shift) % pairs, 0, 0))
     whole = whole.reshape(pairs * rows, depth)
 
-    sources = (line - jnp.arange(m, dtype=jnp.int32)) % m ^ column
-    blocks = jnp.concatenate([jnp.full((m,), odd), jnp.full((m,), 1 - odd)])
-    slots = jnp.stack([blocks, jnp.concatenate([sources, sources])])
-
-    packed = after(packed, up3, down3, *pieces[:m])
-    packed = lax.all_to_all(packed, "ctx", split_axis=0, concat_axis=0, tiled=True)
-    response = packed[:, 0].reshape(n, rows // own, own, packed.shape[3])
+    count = m // 2
+    spot = 3 * 2 * sub
+    weights = jnp.zeros((2, PARTS, count, spot, share * block_depth), w_in.dtype)
+    for index, piece in enumerate(pieces):
+        block, step = divmod(index, m)
+        slot = (line - step) % m ^ column
+        weights = lax.dynamic_update_slice(
+            weights,
+            piece.reshape(1, PARTS, 1, spot, block_depth),
+            (slot % 2, 0, slot // 2, 0, block * block_depth),
+        )
+
+    def multiply(kind, part):
+        left = weights[kind, part].reshape(count * spot, share * block_depth)
+        result = lax.dot_general(
+            left, whole, (((1,), (1,)), ((), ())), preferred_element_type=jnp.float32
+        )
+        return result.reshape(count, spot, -1)
+
+    def along(value, *others):
+        value = value.reshape(pairs, 2, *value.shape[1:])
+        found = []
+        for shift in range(pairs):
+            piece = lax.dynamic_index_in_dim(value, (line - shift) % pairs, 0, keepdims=False)
+            if shift:
+                back = [(i, (i // 2 - shift) % pairs * 2 + i % 2) for i in range(n)]
+                piece = lax.ppermute(after(piece, *others), "ctx", back)
+            found.append(piece)
+        found = jnp.stack(found)
+        mine = lax.dynamic_index_in_dim(found, odd, 1, keepdims=False)
+        give = lax.dynamic_index_in_dim(found, 1 - odd, 1, keepdims=False)
+        return mine, lax.ppermute(give, "ctx", flips)
+
+    mine, other = along(packed[:, 0], up3, down3, *pieces[:m])
+    response = jnp.concatenate([mine, other]).reshape(n, rows // own, own, -1)
+    order = jnp.asarray(ORDER, jnp.int32)
+    places = (order % 2 ^ odd) * pairs + (order // 2 - line) % pairs
+    places = jnp.concatenate([odd.reshape(1), places])
 
     taps = lax.dynamic_slice_in_dim(short_filter, place * own, own, 2)
     taps = taps.reshape(3, 3, PARTS, sub).transpose(2, 0, 1, 3).reshape(PARTS, 3, 3 * sub, 1)
-    sends, keeps = zip(*[multiply(part, slots, whole, pieces, share) for part in range(PARTS)])
+    sends = [multiply(1, part) for part in range(PARTS)]
+    keeps = [multiply(0, part) for part in range(PARTS)]
     gots = [trade(send, 0) for send in sends]
-    across = [
-        trade((keep[1] + got[1]).astype(jnp.bfloat16), 1) for keep, got in zip(keeps, gots)
-    ]
+    onwards = [(keep[1] + got[1]).astype(jnp.bfloat16) for keep, got in zip(keeps, gots)]
+    across = [trade(onward, 1) for onward in onwards]
     gated = []
     for part in range(PARTS):
         projected = keeps[part][0] + gots[part][0] + across[part].astype(jnp.float32)
@@ -456,12 +464,18 @@
         other = lax.ppermute(give, "ctx", flips)
         gated.append(
             convolve(
-                odd.reshape(1), mine, other, taps[part],
+                places, mine, other, taps[part],
                 response[:, :, part * sub : (part + 1) * sub],
             )
         )
 
-    grads = packed[:, 1].reshape(total, packed.shape[3])
+    mine, other = along(packed[:, 1], *onwards)
+    low, high = jnp.where(odd == 0, mine, other), jnp.where(odd == 0, other, mine)
+    grads = jnp.stack([low, high], axis=1)
+    grads = lax.dynamic_slice_in_dim(
+        jnp.concatenate([grads, grads]), (pairs - line) % pairs, pairs, 0
+    )
+    grads = grads.reshape(total, grads.shape[3])
     for bit in (1, 0):
         other = trade(grads, bit)
         low = column >> bit & 1 == 0

time: 177 us -> 159 us (0.90); the launches traced: 174 us -> 158 us
  waiting for transfers between devices: 62 us -> 43.2 us
  starting transfers between devices: 72.2 us -> 81.4 us
  Pallas kernels: 17.3 us -> 8.91 us
  other arithmetic: 10.5 us -> 6.27 us
  matrix products: 2.01 us -> 5.31 us
  local copies, waits for them, and re-layouts: 9.16 us -> 11.8 us
    ppermute x1, waiting for transfers between devices: 19.4 us -> 0.01 us  [special(): up2 = lax.ppermute(up1, 'ctx', up)]
    all_to_all x1 -> x0, waiting for transfers between devices: 14.4 us -> none  [special(): lax.all_to_all(packed, 'ctx', split_axis=0, concat_axis=0, tiled=True)]
    ppermute x0 -> x8, waiting for transfers between devices: none -> 14.2 us  [the longest x6 10.5 us: along(): piece = lax.ppermute(after(piece, *others), 'ctx', back)]
    ppermute x0 -> x8, starting transfers between devices: none -> 12.5 us  [the longest x6 10.4 us: along(): piece = lax.ppermute(after(piece, *others), 'ctx', back)]
    all_to_all x1 -> x0, starting transfers between devices: 9.51 us -> none  [special(): lax.all_to_all(packed, 'ctx', split_axis=0, concat_axis=0, tiled=True)]
    pallas_call x2 -> x1, Pallas kernels: 10.2 us -> 1.59 us  [cut(): pl.pallas_call(functools.partial(cut_kernel, step), out_shape=[out] * cou...]
    ppermute x4, waiting for transfers between devices: 9.59 us -> 1.64 us  [special(): pieces += [lax.ppermute(piece, 'ctx', flips) for piece in pieces]]
    ppermute x1, starting transfers between devices: 13.1 us -> 18.9 us  [special(): up3 = lax.ppermute(after(up2, packed), 'ctx', up)]
  transfers between devices with their start and end apart: 31 -> 38, of which waited for: 10 -> 14; matrix products, arithmetic and copies ran while one was open for 10% -> 11% of each run, Pallas kernels for 7% -> 6%
where the time goes in v3:
time: 159 us; the launch traced here: 158 us
  starting transfers between devices  81.4 us (51%)
  waiting for transfers between devices  43.2 us (27%)
  local copies, waits for them, and re-layouts  11.8 us (7%)
  Pallas kernels  8.91 us (6%)
  other arithmetic  6.27 us (4%)
  matrix products  5.31 us (3%)
    ppermute x1, starting transfers between devices, special(): up3 = lax.ppermute(after(up2, packed), 'ctx', up)  18.9 us
    ppermute x6, starting transfers between devices, special(): lax.ppermute(gated[part], 'ctx', shifts[s])  14 us
    ppermute x6, waiting for transfers between devices, along(): piece = lax.ppermute(after(piece, *others), 'ctx', back)  10.5 us
    ppermute x6, starting transfers between devices, along(): piece = lax.ppermute(after(piece, *others), 'ctx', back)  10.4 us
    ppermute x2, waiting for transfers between devices, special(): other = lax.ppermute(near, 'ctx', flips)  9.32 us
    ppermute x4, starting transfers between devices, special(): pieces.append(lax.ppermute(piece, BOTH, hops))  8.38 us
    ppermute x6, starting transfers between devices, trade(): return lax.ppermute(value, 'ch', [(j, j ^ 1 << bit) for j in range(m)])  6.76 us
    pallas_call x2, Pallas kernels, convolve(): pl.pallas_call(convolve_kernel, out_shape=jax.ShapeDtypeStruct((own, tota...  6.37 us
  transfers between devices with their start and end apart: 38, of which 14 were waited for; matrix products, arithmetic and copies ran while one was open for 11% of the time, Pallas kernels for 6%

profile of v3, /device:TPU:0, one launch (start us, length us, event | category | flops | bytes accessed | tf_op | source)
XLA Modules:
  0.0 158.4 jit_solution(12170263671028968352)
XLA Ops:
  0.6 5.7 %collective-permute-start.3 = (bf16[192,1024]{1,0:T(8,128)(2,1)}, bf16[192,1024]{1,0:T(8,128)(2,1)}, u32[]{:S(2)}, u32[]{:S(2)}) collective-permute-start(bf16[192,1024]{1,0:T(8,128)(2,1)} %param.10), channel_id=1, source_target_pairs={{0,8},{4,12},{8,16},{12,20},{16,24},{20,28},{1,9},{5,13},{9,17},{1... | collective-permute-start | bytes 1179656 | tf_op jit(solution)/shard_map/ppermute | solution.py:374
  6.3 1.3 collective-permute-start.4
  7.7 1.4 copy-done.1
  9.1 1.6 %shard_map.113 = (bf16[384,512]{1,0:T(8,128)(2,1)}, bf16[384,512]{1,0:T(8,128)(2,1)}, bf16[384,512]{1,0:T(8,128)(2,1)S(1)}, bf16[384,512]{1,0:T(8,128)(2,1)S(1)}) custom-call(s32[4]{0:T(128)S(1)} %and_select_fusion.which_ref, bf16[3,512,512]{2,1,0:T(8,128)(2,1)S(1)} %bitcast.216), custom_call_target="tpu_custom_call" | custom-call | bytes 3145728 | tf_op jit(solution)/shard_map/pallas_call | solution.py:332
  10.7 4.5 %collective-permute-start = (bf16[384,512]{1,0:T(8,128)(2,1)}, bf16[384,512]{1,0:T(8,128)(2,1)}, u32[]{:S(2)}, u32[]{:S(2)}) collective-permute-start(bf16[384,512]{1,0:T(8,128)(2,1)} %get-tuple-element.15), channel_id=1, source_target_pairs={{0,0},{1,8},{2,16},{3,24},{4,4},{5,12},{6,20},{7,28},{8,1},{9,9},{... | collective-permute-start | bytes 1179656 | tf_op jit(solution)/shard_map/ppermute | solution.py:387
  15.3 2.4 %collective-permute-start.2 = (bf16[384,512]{1,0:T(8,128)(2,1)S(1)}, bf16[384,512]{1,0:T(8,128)(2,1)}, u32[]{:S(2)}, u32[]{:S(2)}) collective-permute-start(bf16[384,512]{1,0:T(8,128)(2,1)S(1)} %get-tuple-element.17), channel_id=1, source_target_pairs={{0,16},{1,24},{2,0},{3,8},{4,20},{5,28},{6,4},{7,12},{8,17},{9,25}... | collective-permute-start | bytes 1179656 | tf_op jit(solution)/shard_map/ppermute | solution.py:387
  17.7 1.7 %fusion.55 = (bf16[192,512]{1,0:T(8,128)(2,1)S(1)}, bf16[192,512]{1,0:T(8,128)(2,1)}) fusion(bf16[192,1024]{1,0:T(8,128)(2,1)} %param.10), kind=kLoop, calls=%fused_computation.137 | loop fusion | bytes 786432 | tf_op jit(solution)/shard_map/slice | solution.py:407
  21.6 1.0 fusion.24
  24.3 1.3 collective-permute-start.10
  25.6 4.7 %collective-permute-start.12 = (bf16[192,1024]{1,0:T(8,128)(2,1)}, bf16[192,1024]{1,0:T(8,128)(2,1)S(1)}, u32[]{:S(2)}, u32[]{:S(2)}) collective-permute-start(bf16[192,1024]{1,0:T(8,128)(2,1)} %collective-permute-done.3), channel_id=1, source_target_pairs={{0,8},{4,12},{8,16},{12,20},{16,24},{20,28},{1,9},{5,13},{9,17},{1... | collective-permute-start | bytes 1179656 | tf_op jit(solution)/shard_map/ppermute | solution.py:393
  30.9 1.4 collective-permute-start.5
  32.7 1.0 constant_dynamic-update-slice_fusion.7
  33.8 1.6 %collective-permute-start.6 = (bf16[384,512]{1,0:T(8,128)(2,1)}, bf16[384,512]{1,0:T(8,128)(2,1)S(1)}, u32[]{:S(2)}, u32[]{:S(2)}) collective-permute-start(bf16[384,512]{1,0:T(8,128)(2,1)} %collective-permute-done), channel_id=1, source_target_pairs={{0,4},{4,0},{8,12},{12,8},{16,20},{20,16},{24,28},{28,24},{1,5},{5... | collective-permute-start | bytes 1179656 | tf_op jit(solution)/shard_map/ppermute | solution.py:388
  37.0 1.0 constant_dynamic-update-slice_fusion.5
  38.0 3.2 %collective-permute-done.10 = bf16[192,1024]{1,0:T(8,128)(2,1)} collective-permute-done((bf16[192,1024]{1,0:T(8,128)(2,1)}, bf16[192,1024]{1,0:T(8,128)(2,1)}, u32[]{:S(2)}, u32[]{:S(2)}) %collective-permute-start.10) | collective-permute-done | bytes 393248 | tf_op jit(solution)/shard_map/ppermute | solution.py:394
  41.2 1.5 collective-permute-start.8
  42.7 1.3 collective-permute-start.11
  44.0 1.1 broadcast_select_fusion.3
  45.1 4.6 %collective-permute-done.5 = bf16[384,512]{1,0:T(8,128)(2,1)S(1)} collective-permute-done((bf16[384,512]{1,0:T(8,128)(2,1)S(1)}, bf16[384,512]{1,0:T(8,128)(2,1)S(1)}, u32[]{:S(2)}, u32[]{:S(2)}) %collective-permute-start.5) | collective-permute-done | bytes 393248 | tf_op jit(solution)/shard_map/ppermute | solution.py:387
  49.7 18.9 %collective-permute-start.13 = (bf16[192,1024]{1,0:T(8,128)(2,1)S(1)}, bf16[192,1024]{1,0:T(8,128)(2,1)S(1)}, u32[]{:S(2)}, u32[]{:S(2)}) collective-permute-start(bf16[192,1024]{1,0:T(8,128)(2,1)S(1)} %collective-permute-done.12), channel_id=1, source_target_pairs={{0,8},{4,12},{8,16},{12,20},{16,24},{20,28},{1,9},{5,13},{9,17},{1... | collective-permute-start | bytes 1179656 | tf_op jit(solution)/shard_map/ppermute | solution.py:395
  69.4 2.1 %collective-permute-done.11 = bf16[192,1024]{1,0:T(8,128)(2,1)S(1)} collective-permute-done((bf16[192,1024]{1,0:T(8,128)(2,1)}, bf16[192,1024]{1,0:T(8,128)(2,1)S(1)}, u32[]{:S(2)}, u32[]{:S(2)}) %collective-permute-start.11) | collective-permute-done | bytes 393248 | tf_op jit(solution)/shard_map/ppermute | solution.py:396
  71.5 2.3 %collective-permute-done.13 = bf16[192,1024]{1,0:T(8,128)(2,1)S(1)} collective-permute-done((bf16[192,1024]{1,0:T(8,128)(2,1)S(1)}, bf16[192,1024]{1,0:T(8,128)(2,1)S(1)}, u32[]{:S(2)}, u32[]{:S(2)}) %collective-permute-start.13) | collective-permute-done | bytes 393248 | tf_op jit(solution)/shard_map/ppermute | solution.py:395
  73.8 1.1 broadcast_select_fusion.2
  75.0 1.6 %collective-permute-done.9 = bf16[384,512]{1,0:T(8,128)(2,1)S(1)} collective-permute-done((bf16[384,512]{1,0:T(8,128)(2,1)S(1)}, bf16[384,512]{1,0:T(8,128)(2,1)S(1)}, u32[]{:S(2)}, u32[]{:S(2)}) %collective-permute-start.9) | collective-permute-done | bytes 393248 | tf_op jit(solution)/shard_map/ppermute | solution.py:388
  79.6 3.2 %collective-permute-start.17 = (bf16[2,192,128]{2,1,0:T(8,128)(2,1)S(1)}, bf16[2,192,128]{2,1,0:T(8,128)(2,1)S(1)}, u32[]{:S(2)}, u32[]{:S(2)}) collective-permute-start(bf16[2,192,128]{2,1,0:T(8,128)(2,1)S(1)} %copy-done.12), channel_id=1, source_target_pairs={{0,24},{4,28},{8,0},{12,4},{16,8},{20,12},{24,16},{28,20},{1,25},{... | collective-permute-start | bytes 294920 | tf_op jit(solution)/shard_map/ppermute | solution.py:438
  82.8 3.1 %collective-permute-start.18 = (bf16[2,192,128]{2,1,0:T(8,128)(2,1)S(1)}, bf16[2,192,128]{2,1,0:T(8,128)(2,1)S(1)}, u32[]{:S(2)}, u32[]{:S(2)}) collective-permute-start(bf16[2,192,128]{2,1,0:T(8,128)(2,1)S(1)} %copy-done.11), channel_id=1, source_target_pairs={{0,16},{4,20},{8,24},{12,28},{16,0},{20,4},{24,8},{28,12},{1,17},{... | collective-permute-start | bytes 294920 | tf_op jit(solution)/shard_map/ppermute | solution.py:438
  86.0 2.0 %collective-permute-start.19 = (bf16[2,192,128]{2,1,0:T(8,128)(2,1)S(1)}, bf16[2,192,128]{2,1,0:T(8,128)(2,1)S(1)}, u32[]{:S(2)}, u32[]{:S(2)}) collective-permute-start(bf16[2,192,128]{2,1,0:T(8,128)(2,1)S(1)} %copy-done.10), channel_id=1, source_target_pairs={{0,8},{4,12},{8,16},{12,20},{16,24},{20,28},{24,0},{28,4},{1,9},{5... | collective-permute-start | bytes 294920 | tf_op jit(solution)/shard_map/ppermute | solution.py:438
  89.6 6.1 %collective-permute-done.18 = bf16[2,192,128]{2,1,0:T(8,128)(2,1)S(1)} collective-permute-done((bf16[2,192,128]{2,1,0:T(8,128)(2,1)S(1)}, bf16[2,192,128]{2,1,0:T(8,128)(2,1)S(1)}, u32[]{:S(2)}, u32[]{:S(2)}) %collective-permute-start.18) | collective-permute-done | bytes 98336 | tf_op jit(solution)/shard_map/ppermute | solution.py:438
  95.8 1.6 collective-permute-start.20
  97.5 3.0 %collective-permute-start.26 = (bf16[192,768]{1,0:T(8,128)(2,1)S(1)}, bf16[192,768]{1,0:T(8,128)(2,1)S(1)}, u32[]{:S(2)}, u32[]{:S(2)}) collective-permute-start(bf16[192,768]{1,0:T(8,128)(2,1)S(1)} %fusion.11), channel_id=1, source_target_pairs={{0,2},{1,3},{2,0},{3,1},{4,6},{5,7},{6,4},{7,5},{8,10},{9,11},{10,... | collective-permute-start | bytes 884744 | tf_op jit(solution)/shard_map/ppermute | solution.py:372
  100.9 1.7 %collective-permute-start.34 = (bf16[2,192,128]{2,1,0:T(8,128)(2,1)S(1)}, bf16[2,192,128]{2,1,0:T(8,128)(2,1)S(1)}, u32[]{:S(2)}, u32[]{:S(2)}) collective-permute-start(bf16[2,192,128]{2,1,0:T(8,128)(2,1)S(1)} %get-tuple-element.27), channel_id=1, source_target_pairs={{0,8},{4,12},{8,16},{12,20},{16,24},{20,28},{24,0},{28,4},{1,9},{5... | collective-permute-start | bytes 294920 | tf_op jit(solution)/shard_map/ppermute | solution.py:438
  102.7 2.8 %collective-permute-start.15 = (bf16[192,768]{1,0:T(8,128)(2,1)S(1)}, bf16[192,768]{1,0:T(8,128)(2,1)S(1)}, u32[]{:S(2)}, u32[]{:S(2)}) collective-permute-start(bf16[192,768]{1,0:T(8,128)(2,1)S(1)} %fusion.16), channel_id=1, source_target_pairs={{0,2},{1,3},{2,0},{3,1},{4,6},{5,7},{6,4},{7,5},{8,10},{9,11},{10,... | collective-permute-start | bytes 884744 | tf_op jit(solution)/shard_map/ppermute | solution.py:372
  105.6 4.3 %collective-permute-done.33 = bf16[2,192,128]{2,1,0:T(8,128)(2,1)S(1)} collective-permute-done((bf16[2,192,128]{2,1,0:T(8,128)(2,1)S(1)}, bf16[2,192,128]{2,1,0:T(8,128)(2,1)S(1)}, u32[]{:S(2)}, u32[]{:S(2)}) %collective-permute-start.33) | collective-permute-done | bytes 98336 | tf_op jit(solution)/shard_map/ppermute | solution.py:438
  110.7 1.6 %collective-permute-start.27 = (bf16[96,768]{1,0:T(8,128)(2,1)S(1)}, bf16[96,768]{1,0:T(8,128)(2,1)S(1)}, u32[]{:S(2)}, u32[]{:S(2)}) collective-permute-start(bf16[96,768]{1,0:T(8,128)(2,1)S(1)} %get-tuple-element.86), channel_id=1, source_target_pairs={{0,4},{4,0},{8,12},{12,8},{16,20},{20,16},{24,28},{28,24},{1,5},{5... | collective-permute-start | bytes 442376 | tf_op jit(solution)/shard_map/ppermute | solution.py:464
  112.3 1.1 collective-permute-done.15
  114.1 3.7 %collective-permute-done.35 = bf16[4,192,128]{2,1,0:T(8,128)(2,1)S(1)} collective-permute-done((bf16[4,192,128]{2,1,0:T(8,128)(2,1)S(1)}, bf16[4,192,128]{2,1,0:T(8,128)(2,1)S(1)}, u32[]{:S(2)}, u32[]{:S(2)}) %collective-permute-start.35) | collective-permute-done | bytes 196640 | tf_op jit(solution)/shard_map/ppermute | solution.py:443
  117.9 2.6 %collective-permute-done.27.other_ref = bf16[96,768]{1,0:T(8,128)(2,1)S(1)} collective-permute-done((bf16[96,768]{1,0:T(8,128)(2,1)S(1)}, bf16[96,768]{1,0:T(8,128)(2,1)S(1)}, u32[]{:S(2)}, u32[]{:S(2)}) %collective-permute-start.27) | collective-permute-done | bytes 147488 | tf_op jit(solution)/shard_map/ppermute | solution.py:464
  120.5 3.2 %shard_map.116 = bf16[32,1536]{1,0:T(8,128)(2,1)S(1)} custom-call(s32[9]{0:T(128)S(1)} %pad_add_fusion.odd_ref, bf16[96,768]{1,0:T(8,128)(2,1)S(1)} %get-tuple-element.87.mine_ref, bf16[96,768]{1,0:T(8,128)(2,1)S(1)} %collective-permute-done.27.other_ref, f32[3,96,1]{2,1,0:T(8,128)S(1)} %squeeze.103.taps_ref, ...), custom_call_target="tpu_custom_call" | custom-call | flops 1000000000 | bytes 4000000 | tf_op jit(solution)/shard_map/pallas_call | solution.py:262
  124.4 2.0 %collective-permute-start.29 = (bf16[32,1536]{1,0:T(8,128)(2,1)S(1)}, bf16[32,1536]{1,0:T(8,128)(2,1)S(1)}, u32[]{:S(2)}, u32[]{:S(2)}) collective-permute-start(bf16[32,1536]{1,0:T(8,128)(2,1)S(1)} %shard_map.116), channel_id=1, source_target_pairs={{0,16},{4,20},{8,24},{12,28},{16,0},{20,4},{24,8},{28,12},{1,17},{... | collective-permute-start | bytes 294920 | tf_op jit(solution)/shard_map/ppermute | solution.py:491
  126.4 2.8 %collective-permute-start.30 = (bf16[32,1536]{1,0:T(8,128)(2,1)S(1)}, bf16[32,1536]{1,0:T(8,128)(2,1)S(1)}, u32[]{:S(2)}, u32[]{:S(2)}) collective-permute-start(bf16[32,1536]{1,0:T(8,128)(2,1)S(1)} %shard_map.116), channel_id=1, source_target_pairs={{0,24},{4,28},{8,0},{12,4},{16,8},{20,12},{24,16},{28,20},{1,25},{... | collective-permute-start | bytes 294920 | tf_op jit(solution)/shard_map/ppermute | solution.py:491
  129.8 3.2 %shard_map.115 = bf16[32,1536]{1,0:T(8,128)(2,1)S(1)} custom-call(s32[9]{0:T(128)S(1)} %pad_add_fusion.odd_ref, bf16[96,768]{1,0:T(8,128)(2,1)S(1)} %get-tuple-element.89.mine_ref, bf16[96,768]{1,0:T(8,128)(2,1)S(1)} %collective-permute-done.16.other_ref, f32[3,96,1]{2,1,0:T(8,128)S(1)} %squeeze.102.taps_ref, ...), custom_call_target="tpu_custom_call" | custom-call | flops 1000000000 | bytes 4000000 | tf_op jit(solution)/shard_map/pallas_call | solution.py:262
  133.0 1.8 %collective-permute-start.22 = (bf16[32,1536]{1,0:T(8,128)(2,1)S(1)}, bf16[32,1536]{1,0:T(8,128)(2,1)S(1)}, u32[]{:S(2)}, u32[]{:S(2)}) collective-permute-start(bf16[32,1536]{1,0:T(8,128)(2,1)S(1)} %shard_map.115), channel_id=1, source_target_pairs={{0,16},{4,20},{8,24},{12,28},{16,0},{20,4},{24,8},{28,12},{1,17},{... | collective-permute-start | bytes 294920 | tf_op jit(solution)/shard_map/ppermute | solution.py:491
  134.9 6.6 %collective-permute-start.23 = (bf16[32,1536]{1,0:T(8,128)(2,1)S(1)}, bf16[32,1536]{1,0:T(8,128)(2,1)S(1)}, u32[]{:S(2)}, u32[]{:S(2)}) collective-permute-start(bf16[32,1536]{1,0:T(8,128)(2,1)S(1)} %shard_map.115), channel_id=1, source_target_pairs={{0,24},{4,28},{8,0},{12,4},{16,8},{20,12},{24,16},{28,20},{1,25},{... | collective-permute-start | bytes 294920 | tf_op jit(solution)/shard_map/ppermute | solution.py:491
  141.6 2.1 %collective-permute-done.23 = bf16[32,1536]{1,0:T(8,128)(2,1)S(1)} collective-permute-done((bf16[32,1536]{1,0:T(8,128)(2,1)S(1)}, bf16[32,1536]{1,0:T(8,128)(2,1)S(1)}, u32[]{:S(2)}, u32[]{:S(2)}) %collective-permute-start.23) | collective-permute-done | bytes 98336 | tf_op jit(solution)/shard_map/ppermute | solution.py:491
  144.1 5.3 %collective-permute-done.31 = bf16[4,32,1536]{2,1,0:T(8,128)(2,1)S(1)} collective-permute-done((bf16[4,32,1536]{2,1,0:T(8,128)(2,1)S(1)}, bf16[4,32,1536]{2,1,0:T(8,128)(2,1)S(1)}, u32[]{:S(2)}, u32[]{:S(2)}) %collective-permute-start.31) | collective-permute-done | bytes 393248 | tf_op jit(solution)/shard_map/ppermute | solution.py:493
  149.5 4.1 %collective-permute-done.24 = bf16[4,32,1536]{2,1,0:T(8,128)(2,1)S(1)} collective-permute-done((bf16[4,32,1536]{2,1,0:T(8,128)(2,1)S(1)}, bf16[4,32,1536]{2,1,0:T(8,128)(2,1)S(1)}, u32[]{:S(2)}, u32[]{:S(2)}) %collective-permute-start.24) | collective-permute-done | bytes 393248 | tf_op jit(solution)/shard_map/ppermute | solution.py:493
  155.0 1.2 broadcast_select_fusion.1
  156.4 2.0 %fusion = f32[512,512]{1,0:T(8,128)} fusion(bf16[512,1536]{1,0:T(8,128)(2,1)S(1)} %bitcast.222, bf16[1536,128]{1,0:T(8,128)(2,1)S(1)} %get-tuple-element.39, bf16[1536,128]{1,0:T(8,128)(2,1)S(1)} %get-tuple-element.98, bf16[1536,128]{1,0:T(8,128)(2,1)S(1)} %get-tuple-element.38, bf16[1536,128]{1,0:T(8,128)(2,1)S(1)} %get-tuple-element.99), kind=kOutput, calls=%fused_computation | convolution fusion | flops 811597824 | bytes 4194304 | tf_op jit(solution)/shard_map/dot_general | solution.py:503
  (135 shorter events, 17.6 us)
Async XLA Ops:
  0.6 23.5 %copy-start = (f32[3,3,512]{2,1,0:T(4,128)S(1)}, f32[3,3,512]{2,1,0:T(4,128)}, u32[]{:S(2)}) copy-start(f32[3,3,512]{2,1,0:T(4,128)} %param.12) | copy-start | bytes 55300
  0.6 25.0 %collective-permute-start.3 = (bf16[192,1024]{1,0:T(8,128)(2,1)}, bf16[192,1024]{1,0:T(8,128)(2,1)}, u32[]{:S(2)}, u32[]{:S(2)}) collective-permute-start(bf16[192,1024]{1,0:T(8,128)(2,1)} %param.10), channel_id=1, source_target_pairs={{0,8},{4,12},{8,16},{12,20},{16,24},{20,28},{1,9},{5,13},{9,17},{1... | collective-permute-start | bytes 1179656 | tf_op jit(solution)/shard_map/ppermute | solution.py:374
  6.3 18.0 %collective-permute-start.4 = (bf16[192,1024]{1,0:T(8,128)(2,1)}, bf16[192,1024]{1,0:T(8,128)(2,1)}, u32[]{:S(2)}, u32[]{:S(2)}) collective-permute-start(bf16[192,1024]{1,0:T(8,128)(2,1)} %param.10), channel_id=1, source_target_pairs={{8,0},{12,4},{16,8},{20,12},{24,16},{28,20},{9,1},{13,5},{17,9},{2... | collective-permute-start | bytes 1179656 | tf_op jit(solution)/shard_map/ppermute | solution.py:375
  7.7 1.4 copy-start.1
  9.1 10.4 %copy-start.2 = (bf16[192,4096]{1,0:T(8,128)(2,1)S(1)}, bf16[192,4096]{1,0:T(8,128)(2,1)}, u32[]{:S(2)}) copy-start(bf16[192,4096]{1,0:T(8,128)(2,1)} %grad_ref.1) | copy-start | bytes 4718596
  9.1 10.4 %copy-start.3 = (f32[2,192,512]{2,1,0:T(8,128)S(1)}, f32[2,192,512]{2,1,0:T(8,128)}, u32[]{:S(2)}) copy-start(f32[2,192,512]{2,1,0:T(8,128)} %value_ref.1) | copy-start | bytes 2359300
  10.7 20.3 %collective-permute-start = (bf16[384,512]{1,0:T(8,128)(2,1)}, bf16[384,512]{1,0:T(8,128)(2,1)}, u32[]{:S(2)}, u32[]{:S(2)}) collective-permute-start(bf16[384,512]{1,0:T(8,128)(2,1)} %get-tuple-element.15), channel_id=1, source_target_pairs={{0,0},{1,8},{2,16},{3,24},{4,4},{5,12},{6,20},{7,28},{8,1},{9,9},{... | collective-permute-start | bytes 1179656 | tf_op jit(solution)/shard_map/ppermute | solution.py:387
  15.1 18.6 %collective-permute-start.1 = (bf16[384,512]{1,0:T(8,128)(2,1)}, bf16[384,512]{1,0:T(8,128)(2,1)}, u32[]{:S(2)}, u32[]{:S(2)}) collective-permute-start(bf16[384,512]{1,0:T(8,128)(2,1)} %get-tuple-element.16), channel_id=1, source_target_pairs={{0,8},{1,16},{2,24},{3,0},{4,12},{5,20},{6,28},{7,4},{8,9},{9,17},... | collective-permute-start | bytes 1179656 | tf_op jit(solution)/shard_map/ppermute | solution.py:387
  15.3 21.1 %collective-permute-start.2 = (bf16[384,512]{1,0:T(8,128)(2,1)S(1)}, bf16[384,512]{1,0:T(8,128)(2,1)}, u32[]{:S(2)}, u32[]{:S(2)}) collective-permute-start(bf16[384,512]{1,0:T(8,128)(2,1)S(1)} %get-tuple-element.17), channel_id=1, source_target_pairs={{0,16},{1,24},{2,0},{3,8},{4,20},{5,28},{6,4},{7,12},{8,17},{9,25}... | collective-permute-start | bytes 1179656 | tf_op jit(solution)/shard_map/ppermute | solution.py:387
  24.3 16.9 %collective-permute-start.10 = (bf16[192,1024]{1,0:T(8,128)(2,1)}, bf16[192,1024]{1,0:T(8,128)(2,1)}, u32[]{:S(2)}, u32[]{:S(2)}) collective-permute-start(bf16[192,1024]{1,0:T(8,128)(2,1)} %collective-permute-done.4), channel_id=1, source_target_pairs={{8,0},{12,4},{16,8},{20,12},{24,16},{28,20},{9,1},{13,5},{17,9},{2... | collective-permute-start | bytes 1179656 | tf_op jit(solution)/shard_map/ppermute | solution.py:394
  25.6 17.1 %collective-permute-start.12 = (bf16[192,1024]{1,0:T(8,128)(2,1)}, bf16[192,1024]{1,0:T(8,128)(2,1)S(1)}, u32[]{:S(2)}, u32[]{:S(2)}) collective-permute-start(bf16[192,1024]{1,0:T(8,128)(2,1)} %collective-permute-done.3), channel_id=1, source_target_pairs={{0,8},{4,12},{8,16},{12,20},{16,24},{20,28},{1,9},{5,13},{9,17},{1... | collective-permute-start | bytes 1179656 | tf_op jit(solution)/shard_map/ppermute | solution.py:393
  30.9 18.7 %collective-permute-start.5 = (bf16[384,512]{1,0:T(8,128)(2,1)S(1)}, bf16[384,512]{1,0:T(8,128)(2,1)S(1)}, u32[]{:S(2)}, u32[]{:S(2)}) collective-permute-start(bf16[384,512]{1,0:T(8,128)(2,1)S(1)} %get-tuple-element.19), channel_id=1, source_target_pairs={{0,24},{1,0},{2,8},{3,16},{4,28},{5,4},{6,12},{7,20},{8,25},{9,1},... | collective-permute-start | bytes 1179656 | tf_op jit(solution)/shard_map/ppermute | solution.py:387
  33.8 34.9 %collective-permute-start.6 = (bf16[384,512]{1,0:T(8,128)(2,1)}, bf16[384,512]{1,0:T(8,128)(2,1)S(1)}, u32[]{:S(2)}, u32[]{:S(2)}) collective-permute-start(bf16[384,512]{1,0:T(8,128)(2,1)} %collective-permute-done), channel_id=1, source_target_pairs={{0,4},{4,0},{8,12},{12,8},{16,20},{20,16},{24,28},{28,24},{1,5},{5... | collective-permute-start | bytes 1179656 | tf_op jit(solution)/shard_map/ppermute | solution.py:388
  36.4 32.3 %collective-permute-start.7 = (bf16[384,512]{1,0:T(8,128)(2,1)}, bf16[384,512]{1,0:T(8,128)(2,1)S(1)}, u32[]{:S(2)}, u32[]{:S(2)}) collective-permute-start(bf16[384,512]{1,0:T(8,128)(2,1)} %collective-permute-done.1), channel_id=1, source_target_pairs={{0,4},{4,0},{8,12},{12,8},{16,20},{20,16},{24,28},{28,24},{1,5},{5... | collective-permute-start | bytes 1179656 | tf_op jit(solution)/shard_map/ppermute | solution.py:388
  41.2 28.1 %collective-permute-start.8 = (bf16[384,512]{1,0:T(8,128)(2,1)}, bf16[384,512]{1,0:T(8,128)(2,1)S(1)}, u32[]{:S(2)}, u32[]{:S(2)}) collective-permute-start(bf16[384,512]{1,0:T(8,128)(2,1)} %collective-permute-done.2), channel_id=1, source_target_pairs={{0,4},{4,0},{8,12},{12,8},{16,20},{20,16},{24,28},{28,24},{1,5},{5... | collective-permute-start | bytes 1179656 | tf_op jit(solution)/shard_map/ppermute | solution.py:388
  42.7 28.8 %collective-permute-start.11 = (bf16[192,1024]{1,0:T(8,128)(2,1)}, bf16[192,1024]{1,0:T(8,128)(2,1)S(1)}, u32[]{:S(2)}, u32[]{:S(2)}) collective-permute-start(bf16[192,1024]{1,0:T(8,128)(2,1)} %collective-permute-done.10), channel_id=1, source_target_pairs={{8,0},{12,4},{16,8},{20,12},{24,16},{28,20},{9,1},{13,5},{17,9},{2... | collective-permute-start | bytes 1179656 | tf_op jit(solution)/shard_map/ppermute | solution.py:396
  49.7 24.2 %collective-permute-start.13 = (bf16[192,1024]{1,0:T(8,128)(2,1)S(1)}, bf16[192,1024]{1,0:T(8,128)(2,1)S(1)}, u32[]{:S(2)}, u32[]{:S(2)}) collective-permute-start(bf16[192,1024]{1,0:T(8,128)(2,1)S(1)} %collective-permute-done.12), channel_id=1, source_target_pairs={{0,8},{4,12},{8,16},{12,20},{16,24},{20,28},{1,9},{5,13},{9,17},{1... | collective-permute-start | bytes 1179656 | tf_op jit(solution)/shard_map/ppermute | solution.py:395
  68.8 7.8 %collective-permute-start.9 = (bf16[384,512]{1,0:T(8,128)(2,1)S(1)}, bf16[384,512]{1,0:T(8,128)(2,1)S(1)}, u32[]{:S(2)}, u32[]{:S(2)}) collective-permute-start(bf16[384,512]{1,0:T(8,128)(2,1)S(1)} %collective-permute-done.5), channel_id=1, source_target_pairs={{0,4},{4,0},{8,12},{12,8},{16,20},{20,16},{24,28},{28,24},{1,5},{5... | collective-permute-start | bytes 1179656 | tf_op jit(solution)/shard_map/ppermute | solution.py:388
  77.8 19.6 %collective-permute-start.25 = (f32[2,192,768]{2,1,0:T(8,128)S(1)}, f32[2,192,768]{2,1,0:T(8,128)S(1)}, u32[]{:S(2)}, u32[]{:S(2)}) collective-permute-start(f32[2,192,768]{2,1,0:T(8,128)S(1)} %fusion.8), channel_id=1, source_target_pairs={{0,1},{1,0},{2,3},{3,2},{4,5},{5,4},{6,7},{7,6},{8,9},{9,8},{10,11... | collective-permute-start | bytes 3538952 | tf_op jit(solution)/shard_map/ppermute | solution.py:372
  78.8 4.1 %copy-start.11 = (bf16[2,192,128]{2,1,0:T(8,128)(2,1)S(1)}, bf16[2,192,128]{2,1,0:T(8,128)(2,1)}, u32[]{:S(2)}) copy-start(bf16[2,192,128]{2,1,0:T(8,128)(2,1)} %get-tuple-element.23) | copy-start | bytes 294916
  78.8 7.2 %copy-start.10 = (bf16[2,192,128]{2,1,0:T(8,128)(2,1)S(1)}, bf16[2,192,128]{2,1,0:T(8,128)(2,1)}, u32[]{:S(2)}) copy-start(bf16[2,192,128]{2,1,0:T(8,128)(2,1)} %get-tuple-element.24) | copy-start | bytes 294916
  78.8 21.7 %collective-permute-start.14 = (f32[2,192,768]{2,1,0:T(8,128)S(1)}, f32[2,192,768]{2,1,0:T(8,128)S(1)}, u32[]{:S(2)}, u32[]{:S(2)}) collective-permute-start(f32[2,192,768]{2,1,0:T(8,128)S(1)} %fusion.9), channel_id=1, source_target_pairs={{0,1},{1,0},{2,3},{3,2},{4,5},{5,4},{6,7},{7,6},{8,9},{9,8},{10,11... | collective-permute-start | bytes 3538952 | tf_op jit(solution)/shard_map/ppermute | solution.py:372
  79.6 10.0 %collective-permute-start.17 = (bf16[2,192,128]{2,1,0:T(8,128)(2,1)S(1)}, bf16[2,192,128]{2,1,0:T(8,128)(2,1)S(1)}, u32[]{:S(2)}, u32[]{:S(2)}) collective-permute-start(bf16[2,192,128]{2,1,0:T(8,128)(2,1)S(1)} %copy-done.12), channel_id=1, source_target_pairs={{0,24},{4,28},{8,0},{12,4},{16,8},{20,12},{24,16},{28,20},{1,25},{... | collective-permute-start | bytes 294920 | tf_op jit(solution)/shard_map/ppermute | solution.py:438
  82.8 12.9 %collective-permute-start.18 = (bf16[2,192,128]{2,1,0:T(8,128)(2,1)S(1)}, bf16[2,192,128]{2,1,0:T(8,128)(2,1)S(1)}, u32[]{:S(2)}, u32[]{:S(2)}) collective-permute-start(bf16[2,192,128]{2,1,0:T(8,128)(2,1)S(1)} %copy-done.11), channel_id=1, source_target_pairs={{0,16},{4,20},{8,24},{12,28},{16,0},{20,4},{24,8},{28,12},{1,17},{... | collective-permute-start | bytes 294920 | tf_op jit(solution)/shard_map/ppermute | solution.py:438
  86.0 9.7 %collective-permute-start.19 = (bf16[2,192,128]{2,1,0:T(8,128)(2,1)S(1)}, bf16[2,192,128]{2,1,0:T(8,128)(2,1)S(1)}, u32[]{:S(2)}, u32[]{:S(2)}) collective-permute-start(bf16[2,192,128]{2,1,0:T(8,128)(2,1)S(1)} %copy-done.10), channel_id=1, source_target_pairs={{0,8},{4,12},{8,16},{12,20},{16,24},{20,28},{24,0},{28,4},{1,9},{5... | collective-permute-start | bytes 294920 | tf_op jit(solution)/shard_map/ppermute | solution.py:438
  95.8 4.7 %copy-start.9 = (bf16[2,192,128]{2,1,0:T(8,128)(2,1)S(1)}, bf16[2,192,128]{2,1,0:T(8,128)(2,1)}, u32[]{:S(2)}) copy-start(bf16[2,192,128]{2,1,0:T(8,128)(2,1)} %get-tuple-element.25) | copy-start | bytes 294916
  95.8 4.8 %copy-start.8 = (bf16[2,192,128]{2,1,0:T(8,128)(2,1)S(1)}, bf16[2,192,128]{2,1,0:T(8,128)(2,1)}, u32[]{:S(2)}) copy-start(bf16[2,192,128]{2,1,0:T(8,128)(2,1)} %get-tuple-element.26) | copy-start | bytes 294916
  95.8 6.8 %collective-permute-start.20 = (bf16[4,192,128]{2,1,0:T(8,128)(2,1)S(1)}, bf16[4,192,128]{2,1,0:T(8,128)(2,1)S(1)}, u32[]{:S(2)}, u32[]{:S(2)}) collective-permute-start(bf16[4,192,128]{2,1,0:T(8,128)(2,1)S(1)} %get-tuple-element.72), channel_id=1, source_target_pairs={{0,4},{4,0},{8,12},{12,8},{16,20},{20,16},{24,28},{28,24},{1,5},{5... | collective-permute-start | bytes 589832 | tf_op jit(solution)/shard_map/ppermute | solution.py:443
  97.5 13.0 %collective-permute-start.26 = (bf16[192,768]{1,0:T(8,128)(2,1)S(1)}, bf16[192,768]{1,0:T(8,128)(2,1)S(1)}, u32[]{:S(2)}, u32[]{:S(2)}) collective-permute-start(bf16[192,768]{1,0:T(8,128)(2,1)S(1)} %fusion.11), channel_id=1, source_target_pairs={{0,2},{1,3},{2,0},{3,1},{4,6},{5,7},{6,4},{7,5},{8,10},{9,11},{10,... | collective-permute-start | bytes 884744 | tf_op jit(solution)/shard_map/ppermute | solution.py:372
  100.5 5.0 %collective-permute-start.32 = (bf16[2,192,128]{2,1,0:T(8,128)(2,1)S(1)}, bf16[2,192,128]{2,1,0:T(8,128)(2,1)S(1)}, u32[]{:S(2)}, u32[]{:S(2)}) collective-permute-start(bf16[2,192,128]{2,1,0:T(8,128)(2,1)S(1)} %copy-done.9), channel_id=1, source_target_pairs={{0,24},{4,28},{8,0},{12,4},{16,8},{20,12},{24,16},{28,20},{1,25},{... | collective-permute-start | bytes 294920 | tf_op jit(solution)/shard_map/ppermute | solution.py:438
  100.6 9.2 %collective-permute-start.33 = (bf16[2,192,128]{2,1,0:T(8,128)(2,1)S(1)}, bf16[2,192,128]{2,1,0:T(8,128)(2,1)S(1)}, u32[]{:S(2)}, u32[]{:S(2)}) collective-permute-start(bf16[2,192,128]{2,1,0:T(8,128)(2,1)S(1)} %copy-done.8), channel_id=1, source_target_pairs={{0,16},{4,20},{8,24},{12,28},{16,0},{20,4},{24,8},{28,12},{1,17},{... | collective-permute-start | bytes 294920 | tf_op jit(solution)/shard_map/ppermute | solution.py:438
  100.9 8.9 %collective-permute-start.34 = (bf16[2,192,128]{2,1,0:T(8,128)(2,1)S(1)}, bf16[2,192,128]{2,1,0:T(8,128)(2,1)S(1)}, u32[]{:S(2)}, u32[]{:S(2)}) collective-permute-start(bf16[2,192,128]{2,1,0:T(8,128)(2,1)S(1)} %get-tuple-element.27), channel_id=1, source_target_pairs={{0,8},{4,12},{8,16},{12,20},{16,24},{20,28},{24,0},{28,4},{1,9},{5... | collective-permute-start | bytes 294920 | tf_op jit(solution)/shard_map/ppermute | solution.py:438
  102.7 10.7 %collective-permute-start.15 = (bf16[192,768]{1,0:T(8,128)(2,1)S(1)}, bf16[192,768]{1,0:T(8,128)(2,1)S(1)}, u32[]{:S(2)}, u32[]{:S(2)}) collective-permute-start(bf16[192,768]{1,0:T(8,128)(2,1)S(1)} %fusion.16), channel_id=1, source_target_pairs={{0,2},{1,3},{2,0},{3,1},{4,6},{5,7},{6,4},{7,5},{8,10},{9,11},{10,... | collective-permute-start | bytes 884744 | tf_op jit(solution)/shard_map/ppermute | solution.py:372
  109.9 7.9 %collective-permute-start.35 = (bf16[4,192,128]{2,1,0:T(8,128)(2,1)S(1)}, bf16[4,192,128]{2,1,0:T(8,128)(2,1)S(1)}, u32[]{:S(2)}, u32[]{:S(2)}) collective-permute-start(bf16[4,192,128]{2,1,0:T(8,128)(2,1)S(1)} %dynamic-slice_bitcast_fusion.1), channel_id=1, source_target_pairs={{0,4},{4,0},{8,12},{12,8},{16,20},{20,16},{24,28},{28,24},{1,5},{5... | collective-permute-start | bytes 589832 | tf_op jit(solution)/shard_map/ppermute | solution.py:443
  110.6 9.9 %copy-start.4 = (f32[192,512]{1,0:T(8,128)S(1)}, f32[192,512]{1,0:T(8,128)}, u32[]{:S(2)}) copy-start(f32[192,512]{1,0:T(8,128)} %constant.269.clone.table_ref) | copy-start | bytes 1179652
  110.7 9.9 %copy-start.5 = (f32[2,5,192]{2,1,0:T(8,128)S(1)}, f32[2,5,192]{2,1,0:T(8,128)}, u32[]{:S(2)}) copy-start(f32[2,5,192]{2,1,0:T(8,128)} %constant.270.clone.turn_ref) | copy-start | bytes 23044
  110.7 9.8 %collective-permute-start.27 = (bf16[96,768]{1,0:T(8,128)(2,1)S(1)}, bf16[96,768]{1,0:T(8,128)(2,1)S(1)}, u32[]{:S(2)}, u32[]{:S(2)}) collective-permute-start(bf16[96,768]{1,0:T(8,128)(2,1)S(1)} %get-tuple-element.86), channel_id=1, source_target_pairs={{0,4},{4,0},{8,12},{12,8},{16,20},{20,16},{24,28},{28,24},{1,5},{5... | collective-permute-start | bytes 442376 | tf_op jit(solution)/shard_map/ppermute | solution.py:464
  113.5 16.2 %collective-permute-start.16 = (bf16[96,768]{1,0:T(8,128)(2,1)S(1)}, bf16[96,768]{1,0:T(8,128)(2,1)S(1)}, u32[]{:S(2)}, u32[]{:S(2)}) collective-permute-start(bf16[96,768]{1,0:T(8,128)(2,1)S(1)} %get-tuple-element.88), channel_id=1, source_target_pairs={{0,4},{4,0},{8,12},{12,8},{16,20},{20,16},{24,28},{28,24},{1,5},{5... | collective-permute-start | bytes 442376 | tf_op jit(solution)/shard_map/ppermute | solution.py:464
  123.7 9.3 %collective-permute-start.28 = (bf16[32,1536]{1,0:T(8,128)(2,1)S(1)}, bf16[32,1536]{1,0:T(8,128)(2,1)S(1)}, u32[]{:S(2)}, u32[]{:S(2)}) collective-permute-start(bf16[32,1536]{1,0:T(8,128)(2,1)S(1)} %shard_map.116), channel_id=1, source_target_pairs={{0,8},{4,12},{8,16},{12,20},{16,24},{20,28},{24,0},{28,4},{1,9},{5... | collective-permute-start | bytes 294920 | tf_op jit(solution)/shard_map/ppermute | solution.py:491
  124.4 10.4 %collective-permute-start.29 = (bf16[32,1536]{1,0:T(8,128)(2,1)S(1)}, bf16[32,1536]{1,0:T(8,128)(2,1)S(1)}, u32[]{:S(2)}, u32[]{:S(2)}) collective-permute-start(bf16[32,1536]{1,0:T(8,128)(2,1)S(1)} %shard_map.116), channel_id=1, source_target_pairs={{0,16},{4,20},{8,24},{12,28},{16,0},{20,4},{24,8},{28,12},{1,17},{... | collective-permute-start | bytes 294920 | tf_op jit(solution)/shard_map/ppermute | solution.py:491
  126.4 15.0 %collective-permute-start.30 = (bf16[32,1536]{1,0:T(8,128)(2,1)S(1)}, bf16[32,1536]{1,0:T(8,128)(2,1)S(1)}, u32[]{:S(2)}, u32[]{:S(2)}) collective-permute-start(bf16[32,1536]{1,0:T(8,128)(2,1)S(1)} %shard_map.116), channel_id=1, source_target_pairs={{0,24},{4,28},{8,0},{12,4},{16,8},{20,12},{24,16},{28,20},{1,25},{... | collective-permute-start | bytes 294920 | tf_op jit(solution)/shard_map/ppermute | solution.py:491
  129.5 14.3 %collective-permute-start.36 = (bf16[1536,128]{1,0:T(8,128)(2,1)S(1)}, bf16[1536,128]{1,0:T(8,128)(2,1)S(1)}, u32[]{:S(2)}, u32[]{:S(2)}) collective-permute-start(bf16[1536,128]{1,0:T(8,128)(2,1)S(1)} %bitcast.229), channel_id=1, source_target_pairs={{0,2},{1,3},{2,0},{3,1},{4,6},{5,7},{6,4},{7,5},{8,10},{9,11},{10,... | collective-permute-start | bytes 1179656 | tf_op jit(solution)/shard_map/ppermute | solution.py:372
  132.9 8.6 %collective-permute-start.21 = (bf16[32,1536]{1,0:T(8,128)(2,1)S(1)}, bf16[32,1536]{1,0:T(8,128)(2,1)S(1)}, u32[]{:S(2)}, u32[]{:S(2)}) collective-permute-start(bf16[32,1536]{1,0:T(8,128)(2,1)S(1)} %shard_map.115), channel_id=1, source_target_pairs={{0,8},{4,12},{8,16},{12,20},{16,24},{20,28},{24,0},{28,4},{1,9},{5... | collective-permute-start | bytes 294920 | tf_op jit(solution)/shard_map/ppermute | solution.py:491
  133.0 8.5 %collective-permute-start.22 = (bf16[32,1536]{1,0:T(8,128)(2,1)S(1)}, bf16[32,1536]{1,0:T(8,128)(2,1)S(1)}, u32[]{:S(2)}, u32[]{:S(2)}) collective-permute-start(bf16[32,1536]{1,0:T(8,128)(2,1)S(1)} %shard_map.115), channel_id=1, source_target_pairs={{0,16},{4,20},{8,24},{12,28},{16,0},{20,4},{24,8},{28,12},{1,17},{... | collective-permute-start | bytes 294920 | tf_op jit(solution)/shard_map/ppermute | solution.py:491
  134.9 8.8 %collective-permute-start.23 = (bf16[32,1536]{1,0:T(8,128)(2,1)S(1)}, bf16[32,1536]{1,0:T(8,128)(2,1)S(1)}, u32[]{:S(2)}, u32[]{:S(2)}) collective-permute-start(bf16[32,1536]{1,0:T(8,128)(2,1)S(1)} %shard_map.115), channel_id=1, source_target_pairs={{0,24},{4,28},{8,0},{12,4},{16,8},{20,12},{24,16},{28,20},{1,25},{... | collective-permute-start | bytes 294920 | tf_op jit(solution)/shard_map/ppermute | solution.py:491
  141.5 7.8 %collective-permute-start.31 = (bf16[4,32,1536]{2,1,0:T(8,128)(2,1)S(1)}, bf16[4,32,1536]{2,1,0:T(8,128)(2,1)S(1)}, u32[]{:S(2)}, u32[]{:S(2)}) collective-permute-start(bf16[4,32,1536]{2,1,0:T(8,128)(2,1)S(1)} %pad_maximum_fusion.3), channel_id=1, source_target_pairs={{0,4},{4,0},{8,12},{12,8},{16,20},{20,16},{24,28},{28,24},{1,5},{5... | collective-permute-start | bytes 1179656 | tf_op jit(solution)/shard_map/ppermute | solution.py:493
  143.7 9.8 %collective-permute-start.24 = (bf16[4,32,1536]{2,1,0:T(8,128)(2,1)S(1)}, bf16[4,32,1536]{2,1,0:T(8,128)(2,1)S(1)}, u32[]{:S(2)}, u32[]{:S(2)}) collective-permute-start(bf16[4,32,1536]{2,1,0:T(8,128)(2,1)S(1)} %pad_maximum_fusion.2), channel_id=1, source_target_pairs={{0,4},{4,0},{8,12},{12,8},{16,20},{20,16},{24,28},{28,24},{1,5},{5... | collective-permute-start | bytes 1179656 | tf_op jit(solution)/shard_map/ppermute | solution.py:493
  144.0 11.0 %collective-permute-start.37 = (bf16[2,1536,128]{2,1,0:T(8,128)(2,1)S(1)}, bf16[2,1536,128]{2,1,0:T(8,128)(2,1)}, u32[]{:S(2)}, u32[]{:S(2)}) collective-permute-start(bf16[2,1536,128]{2,1,0:T(8,128)(2,1)S(1)} %pad_maximum_fusion), channel_id=1, source_target_pairs={{0,1},{1,0},{2,3},{3,2},{4,5},{5,4},{6,7},{7,6},{8,9},{9,8},{10,11... | collective-permute-start | bytes 2359304 | tf_op jit(solution)/shard_map/ppermute | solution.py:372
  (5 other events, 5.1 us)

commit v4 on v3

--- a/solution.py
+++ b/solution.py
@@ -399,6 +399,19 @@
         jnp.where(line >= 2, up2, down2),
         jnp.where(line >= 3, up3, down1),
     ]
+    def along(value, *others):
+        value = value.reshape(pairs, 2, *value.shape[1:])
+        found = []
+        for shift in range(pairs):
+            piece = lax.dynamic_index_in_dim(value, (line - shift) % pairs, 0, keepdims=False)
+            if shift:
+                back = [(i, (i // 2 - shift) % pairs * 2 + i % 2) for i in range(n)]
+                piece = lax.ppermute(after(piece, *others), "ctx", back)
+            found.append(piece)
+        return found
+
+    filters = along(packed[:, 0], up3, down3, *pieces[:m])
+
     whole = jnp.zeros((pairs, rows, depth), features.dtype)
     for shift, value in enumerate([features] + behind):
         value = jnp.where(
@@ -407,7 +420,7 @@
             jnp.concatenate([value[:, block_depth:], value[:, :block_depth]], axis=1),
         )
         whole = lax.dynamic_update_slice(whole, value[None], ((line - shift) % pairs, 0, 0))
-    whole = whole.reshape(pairs * rows, depth)
+    whole = after(whole.reshape(pairs * rows, depth), *filters)
 
     count = m // 2
     spot = 3 * 2 * sub
@@ -428,22 +441,12 @@
         )
         return result.reshape(count, spot, -1)
 
-    def along(value, *others):
-        value = value.reshape(pairs, 2, *value.shape[1:])
-        found = []
-        for shift in range(pairs):
-            piece = lax.dynamic_index_in_dim(value, (line - shift) % pairs, 0, keepdims=False)
-            if shift:
-                back = [(i, (i // 2 - shift) % pairs * 2 + i % 2) for i in range(n)]
-                piece = lax.ppermute(after(piece, *others), "ctx", back)
-            found.append(piece)
-        found = jnp.stack(found)
+    def beside(found, *others):
+        found = jnp.stack([after(value, *others) for value in found])
         mine = lax.dynamic_index_in_dim(found, odd, 1, keepdims=False)
         give = lax.dynamic_index_in_dim(found, 1 - odd, 1, keepdims=False)
         return mine, lax.ppermute(give, "ctx", flips)
 
-    mine, other = along(packed[:, 0], up3, down3, *pieces[:m])
-    response = jnp.concatenate([mine, other]).reshape(n, rows // own, own, -1)
     order = jnp.asarray(ORDER, jnp.int32)
     places = (order % 2 ^ odd) * pairs + (order // 2 - line) % pairs
     places = jnp.concatenate([odd.reshape(1), places])
@@ -455,13 +458,19 @@
     gots = [trade(send, 0) for send in sends]
     onwards = [(keep[1] + got[1]).astype(jnp.bfloat16) for keep, got in zip(keeps, gots)]
     across = [trade(onward, 1) for onward in onwards]
+    mine, other = beside(filters, onwards[0])
+    response = jnp.concatenate([mine, other]).reshape(n, rows // own, own, -1)
     gated = []
+    crossed = []
+    gives = []
     for part in range(PARTS):
-        projected = keeps[part][0] + gots[part][0] + across[part].astype(jnp.float32)
+        projected = keeps[part][0] + gots[part][0] + after(across[part], *crossed).astype(jnp.float32)
         projected = projected.astype(jnp.bfloat16).reshape(2, 3 * sub, total // 2)
         mine = lax.dynamic_index_in_dim(projected, odd, 0, keepdims=False)
         give = lax.dynamic_index_in_dim(projected, 1 - odd, 0, keepdims=False)
         other = lax.ppermute(give, "ctx", flips)
+        crossed.append(other)
+        gives.append(give)
         gated.append(
             convolve(
                 places, mine, other, taps[part],
@@ -469,7 +478,8 @@
             )
         )
 
-    mine, other = along(packed[:, 1], *onwards)
+    mine, other = beside(along(packed[:, 1], *onwards), crossed[0], *gives)
+    gates = [crossed, [other]]
     low, high = jnp.where(odd == 0, mine, other), jnp.where(odd == 0, other, mine)
     grads = jnp.stack([low, high], axis=1)
     grads = lax.dynamic_slice_in_dim(
@@ -489,6 +499,7 @@
     for part in range(PARTS):
         near = [gated[part]]
         near += [lax.ppermute(gated[part], "ctx", shifts[s]) for s in range(1, pairs)]
+        near = [after(value, *gates[part]) for value in near]
         near = jnp.stack(near)
         other = lax.ppermute(near, "ctx", flips)
         low = jnp.where(odd == 0, near, other)

time: 159 us -> 153 us (0.962)
  starting transfers between devices: 81.4 us -> 69.4 us
  waiting for transfers between devices: 43.2 us -> 37.8 us
  other arithmetic: 6.27 us -> 11.2 us
  local copies, waits for them, and re-layouts: 11.8 us -> 15.3 us
  matrix products: 5.31 us -> 7.39 us
    ppermute x1, waiting for transfers between devices: 3.17 us -> 12.4 us  [special(): down2 = lax.ppermute(down1, 'ctx', down)]
    ppermute x6, waiting for transfers between devices: 10.5 us -> 2.24 us  [along(): piece = lax.ppermute(after(piece, *others), 'ctx', back)]
    ppermute x1, starting transfers between devices: 18.9 us -> 11.6 us  [special(): up3 = lax.ppermute(after(up2, packed), 'ctx', up)]
    ppermute x6, starting transfers between devices: 14 us -> 9.28 us  [special(): lax.ppermute(gated[part], 'ctx', shifts[s])]
    ppermute x6, waiting for transfers between devices: 1.15 us -> 5.8 us  [trade(): return lax.ppermute(value, 'ch', [(j, j ^ 1 << bit) for j in range(m)])]
    ppermute x4, waiting for transfers between devices: 4.57 us -> 0.01 us  [special(): pieces.append(lax.ppermute(piece, BOTH, hops))]
    ppermute x6, starting transfers between devices: 6.76 us -> 3 us  [trade(): return lax.ppermute(value, 'ch', [(j, j ^ 1 << bit) for j in range(m)])]
    ppermute x2, waiting for transfers between devices: 3.71 us -> 0.01 us  [beside(): return (mine, lax.ppermute(give, 'ctx', flips))]
  transfers between devices with their start and end apart: 38 -> 38, of which waited for: 14 -> 9; matrix products, arithmetic and copies ran while one was open for 11% -> 18% of each run, Pallas kernels for 6% -> 6%
where the time goes in v4:
time: 153 us; the launch traced here: 151 us
  starting transfers between devices  69.4 us (45%)
  waiting for transfers between devices  37.8 us (25%)
  local copies, waits for them, and re-layouts  15.3 us (10%)
  other arithmetic  11.2 us (7%)
  Pallas kernels  8.9 us (6%)
  matrix products  7.39 us (5%)
    ppermute x1, waiting for transfers between devices, special(): down2 = lax.ppermute(down1, 'ctx', down)  12.4 us
    ppermute x1, starting transfers between devices, special(): up3 = lax.ppermute(after(up2, packed), 'ctx', up)  11.6 us
    ppermute x6, starting transfers between devices, along(): piece = lax.ppermute(after(piece, *others), 'ctx', back)  10.5 us
    ppermute x4, starting transfers between devices, special(): pieces.append(lax.ppermute(piece, BOTH, hops))  9.92 us
    ppermute x6, starting transfers between devices, special(): lax.ppermute(gated[part], 'ctx', shifts[s])  9.28 us
    ppermute x2, waiting for transfers between devices, special(): other = lax.ppermute(near, 'ctx', flips)  8.78 us
    pallas_call x2, Pallas kernels, convolve(): pl.pallas_call(convolve_kernel, out_shape=jax.ShapeDtypeStruct((own, tota...  6.36 us
    ppermute x6, waiting for transfers between devices, trade(): return lax.ppermute(value, 'ch', [(j, j ^ 1 << bit) for j in range(m)])  5.8 us
  transfers between devices with their start and end apart: 38, of which 9 were waited for; matrix products, arithmetic and copies ran while one was open for 18% of the time, Pallas kernels for 6%

profile of v4, /device:TPU:0, one launch (start us, length us, event | category | flops | bytes accessed | tf_op | source)
XLA Modules:
  0.0 151.5 jit_solution(11545168226989512026)
XLA Ops:
  0.6 5.7 %collective-permute-start.3 = (bf16[192,1024]{1,0:T(8,128)(2,1)}, bf16[192,1024]{1,0:T(8,128)(2,1)}, u32[]{:S(2)}, u32[]{:S(2)}) collective-permute-start(bf16[192,1024]{1,0:T(8,128)(2,1)} %param.10), channel_id=1, source_target_pairs={{0,8},{4,12},{8,16},{12,20},{16,24},{20,28},{1,9},{5,13},{9,17},{1... | collective-permute-start | bytes 1179656 | tf_op jit(solution)/shard_map/ppermute | solution.py:374
  6.3 1.3 collective-permute-start.4
  7.7 1.4 copy-done.1
  9.1 1.6 %shard_map.113 = (bf16[384,512]{1,0:T(8,128)(2,1)}, bf16[384,512]{1,0:T(8,128)(2,1)}, bf16[384,512]{1,0:T(8,128)(2,1)S(1)}, bf16[384,512]{1,0:T(8,128)(2,1)S(1)}) custom-call(s32[4]{0:T(128)S(1)} %and_select_fusion.which_ref, bf16[3,512,512]{2,1,0:T(8,128)(2,1)S(1)} %bitcast.221), custom_call_target="tpu_custom_call" | custom-call | bytes 3145728 | tf_op jit(solution)/shard_map/pallas_call | solution.py:332
  10.7 4.5 %collective-permute-start = (bf16[384,512]{1,0:T(8,128)(2,1)}, bf16[384,512]{1,0:T(8,128)(2,1)}, u32[]{:S(2)}, u32[]{:S(2)}) collective-permute-start(bf16[384,512]{1,0:T(8,128)(2,1)} %get-tuple-element.33), channel_id=1, source_target_pairs={{0,0},{1,8},{2,16},{3,24},{4,4},{5,12},{6,20},{7,28},{8,1},{9,9},{... | collective-permute-start | bytes 1179656 | tf_op jit(solution)/shard_map/ppermute | solution.py:387
  15.3 2.4 %collective-permute-start.2 = (bf16[384,512]{1,0:T(8,128)(2,1)S(1)}, bf16[384,512]{1,0:T(8,128)(2,1)}, u32[]{:S(2)}, u32[]{:S(2)}) collective-permute-start(bf16[384,512]{1,0:T(8,128)(2,1)S(1)} %get-tuple-element.35), channel_id=1, source_target_pairs={{0,16},{1,24},{2,0},{3,8},{4,20},{5,28},{6,4},{7,12},{8,17},{9,25}... | collective-permute-start | bytes 1179656 | tf_op jit(solution)/shard_map/ppermute | solution.py:387
  17.7 1.7 %fusion.57 = (bf16[192,512]{1,0:T(8,128)(2,1)S(1)}, bf16[192,512]{1,0:T(8,128)(2,1)}) fusion(bf16[192,1024]{1,0:T(8,128)(2,1)} %param.10), kind=kLoop, calls=%fused_computation.139 | loop fusion | bytes 786432 | tf_op jit(solution)/shard_map/slice | solution.py:420
  21.5 1.0 fusion.26
  22.7 1.8 %dynamic-slice_bitcast_fusion.11 = (bf16[2,192,128]{2,1,0:T(8,128)(2,1)}, bf16[2,192,128]{2,1,0:T(8,128)(2,1)}, bf16[2,192,128]{2,1,0:T(8,128)(2,1)}, bf16[2,192,128]{2,1,0:T(8,128)(2,1)S(1)}) fusion(bf16[4,2,192,128]{3,2,1,0:T(8,128)(2,1)} %bitcast.233, s32[]{:T(128)S(6)} %select_n.361, s32[]{:T(128)S(6)} %select_n.357, s32[]{:T(128)S(6)} %select_n.353, ...), kind=kLoop, calls=%fused_computation.102 | loop fusion | bytes 786448 | tf_op jit(solution)/shard_map/jit(dynamic_index_in_dim)/squeeze | solution.py:406
  25.2 2.9 %collective-permute-start.5 = (bf16[384,512]{1,0:T(8,128)(2,1)S(1)}, bf16[384,512]{1,0:T(8,128)(2,1)S(1)}, u32[]{:S(2)}, u32[]{:S(2)}) collective-permute-start(bf16[384,512]{1,0:T(8,128)(2,1)S(1)} %get-tuple-element.37), channel_id=1, source_target_pairs={{0,24},{1,0},{2,8},{3,16},{4,28},{5,4},{6,12},{7,20},{8,25},{9,1},... | collective-permute-start | bytes 1179656 | tf_op jit(solution)/shard_map/ppermute | solution.py:387
  28.1 1.3 collective-permute-start.10
  29.4 5.3 %collective-permute-start.12 = (bf16[192,1024]{1,0:T(8,128)(2,1)}, bf16[192,1024]{1,0:T(8,128)(2,1)}, u32[]{:S(2)}, u32[]{:S(2)}) collective-permute-start(bf16[192,1024]{1,0:T(8,128)(2,1)} %collective-permute-done.3), channel_id=1, source_target_pairs={{0,8},{4,12},{8,16},{12,20},{16,24},{20,28},{1,9},{5,13},{9,17},{1... | collective-permute-start | bytes 1179656 | tf_op jit(solution)/shard_map/ppermute | solution.py:393
  34.9 1.6 %collective-permute-start.6 = (bf16[384,512]{1,0:T(8,128)(2,1)}, bf16[384,512]{1,0:T(8,128)(2,1)S(1)}, u32[]{:S(2)}, u32[]{:S(2)}) collective-permute-start(bf16[384,512]{1,0:T(8,128)(2,1)} %collective-permute-done), channel_id=1, source_target_pairs={{0,4},{4,0},{8,12},{12,8},{16,20},{20,16},{24,28},{28,24},{1,5},{5... | collective-permute-start | bytes 1179656 | tf_op jit(solution)/shard_map/ppermute | solution.py:388
  37.9 1.0 constant_dynamic-update-slice_fusion.6
  40.6 12.4 %collective-permute-done.10 = bf16[192,1024]{1,0:T(8,128)(2,1)} collective-permute-done((bf16[192,1024]{1,0:T(8,128)(2,1)}, bf16[192,1024]{1,0:T(8,128)(2,1)}, u32[]{:S(2)}, u32[]{:S(2)}) %collective-permute-start.10) | collective-permute-done | bytes 393248 | tf_op jit(solution)/shard_map/ppermute | solution.py:394
  53.0 1.5 %collective-permute-start.8 = (bf16[384,512]{1,0:T(8,128)(2,1)}, bf16[384,512]{1,0:T(8,128)(2,1)S(1)}, u32[]{:S(2)}, u32[]{:S(2)}) collective-permute-start(bf16[384,512]{1,0:T(8,128)(2,1)} %collective-permute-done.2), channel_id=1, source_target_pairs={{0,4},{4,0},{8,12},{12,8},{16,20},{20,16},{24,28},{28,24},{1,5},{5... | collective-permute-start | bytes 1179656 | tf_op jit(solution)/shard_map/ppermute | solution.py:388
  54.6 1.3 collective-permute-start.11
  55.9 11.6 %collective-permute-start.13 = (bf16[192,1024]{1,0:T(8,128)(2,1)}, bf16[192,1024]{1,0:T(8,128)(2,1)S(1)}, u32[]{:S(2)}, u32[]{:S(2)}) collective-permute-start(bf16[192,1024]{1,0:T(8,128)(2,1)} %collective-permute-done.12), channel_id=1, source_target_pairs={{0,8},{4,12},{8,16},{12,20},{16,24},{20,28},{1,9},{5,13},{9,17},{1... | collective-permute-start | bytes 1179656 | tf_op jit(solution)/shard_map/ppermute | solution.py:395
  69.4 5.0 %collective-permute-done.11 = bf16[192,1024]{1,0:T(8,128)(2,1)S(1)} collective-permute-done((bf16[192,1024]{1,0:T(8,128)(2,1)}, bf16[192,1024]{1,0:T(8,128)(2,1)S(1)}, u32[]{:S(2)}, u32[]{:S(2)}) %collective-permute-start.11) | collective-permute-done | bytes 393248 | tf_op jit(solution)/shard_map/ppermute | solution.py:396
  74.4 1.3 collective-permute-done.13
  75.7 2.4 %collective-permute-start.16 = (bf16[2,192,128]{2,1,0:T(8,128)(2,1)S(1)}, bf16[2,192,128]{2,1,0:T(8,128)(2,1)S(1)}, u32[]{:S(2)}, u32[]{:S(2)}) collective-permute-start(bf16[2,192,128]{2,1,0:T(8,128)(2,1)S(1)} %copy-done.12), channel_id=1, source_target_pairs={{0,8},{4,12},{8,16},{12,20},{16,24},{20,28},{24,0},{28,4},{1,9},{5... | collective-permute-start | bytes 294920 | tf_op jit(solution)/shard_map/ppermute | solution.py:409
  78.0 1.5 collective-permute-start.15
  79.5 2.6 %collective-permute-start.14 = (bf16[2,192,128]{2,1,0:T(8,128)(2,1)S(1)}, bf16[2,192,128]{2,1,0:T(8,128)(2,1)S(1)}, u32[]{:S(2)}, u32[]{:S(2)}) collective-permute-start(bf16[2,192,128]{2,1,0:T(8,128)(2,1)S(1)} %copy-done.10), channel_id=1, source_target_pairs={{0,24},{4,28},{8,0},{12,4},{16,8},{20,12},{24,16},{28,20},{1,25},{... | collective-permute-start | bytes 294920 | tf_op jit(solution)/shard_map/ppermute | solution.py:409
  82.5 1.1 broadcast_select_fusion.2
  83.8 2.2 %collective-permute-done.15 = bf16[2,192,128]{2,1,0:T(8,128)(2,1)S(1)} collective-permute-done((bf16[2,192,128]{2,1,0:T(8,128)(2,1)S(1)}, bf16[2,192,128]{2,1,0:T(8,128)(2,1)S(1)}, u32[]{:S(2)}, u32[]{:S(2)}) %collective-permute-start.15) | collective-permute-done | bytes 98336 | tf_op jit(solution)/shard_map/ppermute | solution.py:409
  86.0 1.9 %fusion.10 = f32[2,192,768]{2,1,0:T(8,128)} fusion(bf16[768,1024]{1,0:T(8,128)(2,1)S(1)} %bitcast.228, bf16[2,2,2,192,1024]{4,3,2,1,0:T(8,128)(2,1)S(1)} %constant_dynamic-update-slice_fusion), kind=kOutput, calls=%fused_computation.10 | convolution fusion | flops 603979776 | bytes 3538944 | tf_op jit(solution)/shard_map/dot_general | solution.py:439
  87.9 1.8 %fusion.8 = f32[2,192,768]{2,1,0:T(8,128)} fusion(bf16[768,1024]{1,0:T(8,128)(2,1)S(1)} %bitcast.229, bf16[2,2,2,192,1024]{4,3,2,1,0:T(8,128)(2,1)S(1)} %constant_dynamic-update-slice_fusion), kind=kOutput, calls=%fused_computation.8 | convolution fusion | flops 603979776 | bytes 3538944 | tf_op jit(solution)/shard_map/dot_general | solution.py:439
  90.3 1.5 fusion.48
  93.5 1.2 fusion.18
  95.5 2.0 %collective-permute-start.22 = (bf16[192,768]{1,0:T(8,128)(2,1)}, bf16[192,768]{1,0:T(8,128)(2,1)}, u32[]{:S(2)}, u32[]{:S(2)}) collective-permute-start(bf16[192,768]{1,0:T(8,128)(2,1)} %fusion.13), channel_id=1, source_target_pairs={{0,2},{1,3},{2,0},{3,1},{4,6},{5,7},{6,4},{7,5},{8,10},{9,11},{10,... | collective-permute-start | bytes 884744 | tf_op jit(solution)/shard_map/ppermute | solution.py:372
  98.8 5.8 %collective-permute-done.18 = bf16[192,768]{1,0:T(8,128)(2,1)S(1)} collective-permute-done((bf16[192,768]{1,0:T(8,128)(2,1)S(1)}, bf16[192,768]{1,0:T(8,128)(2,1)S(1)}, u32[]{:S(2)}, u32[]{:S(2)}) %collective-permute-start.18) | collective-permute-done | bytes 294944 | tf_op jit(solution)/shard_map/ppermute | solution.py:372
  104.6 1.2 fusion.21
  107.4 3.3 %collective-permute-start.28 = (bf16[2,192,128]{2,1,0:T(8,128)(2,1)}, bf16[2,192,128]{2,1,0:T(8,128)(2,1)S(1)}, u32[]{:S(2)}, u32[]{:S(2)}) collective-permute-start(bf16[2,192,128]{2,1,0:T(8,128)(2,1)} %get-tuple-element.54), channel_id=1, source_target_pairs={{0,24},{4,28},{8,0},{12,4},{16,8},{20,12},{24,16},{28,20},{1,25},{... | collective-permute-start | bytes 294920 | tf_op jit(solution)/shard_map/ppermute | solution.py:409
  112.4 1.1 fusion.16
  113.5 1.6 %collective-permute-start.23 = (bf16[96,768]{1,0:T(8,128)(2,1)S(1)}, bf16[96,768]{1,0:T(8,128)(2,1)S(1)}, u32[]{:S(2)}, u32[]{:S(2)}) collective-permute-start(bf16[96,768]{1,0:T(8,128)(2,1)S(1)} %get-tuple-element.123), channel_id=1, source_target_pairs={{0,4},{4,0},{8,12},{12,8},{16,20},{20,16},{24,28},{28,24},{1,5},{5... | collective-permute-start | bytes 442376 | tf_op jit(solution)/shard_map/ppermute | solution.py:471
  115.1 3.2 %shard_map.115 = bf16[32,1536]{1,0:T(8,128)(2,1)S(1)} custom-call(s32[9]{0:T(128)S(1)} %pad_add_fusion.odd_ref, bf16[96,768]{1,0:T(8,128)(2,1)S(1)} %get-tuple-element.125.mine_ref, bf16[96,768]{1,0:T(8,128)(2,1)S(1)} %collective-permute-done.19.other_ref, f32[3,96,1]{2,1,0:T(8,128)S(1)} %squeeze.108.taps_ref, ...), custom_call_target="tpu_custom_call" | custom-call | flops 1000000000 | bytes 4000000 | tf_op jit(solution)/shard_map/pallas_call | solution.py:262
  118.3 2.9 %collective-permute-start.24 = (bf16[32,1536]{1,0:T(8,128)(2,1)S(1)}, bf16[32,1536]{1,0:T(8,128)(2,1)S(1)}, u32[]{:S(2)}, u32[]{:S(2)}) collective-permute-start(bf16[32,1536]{1,0:T(8,128)(2,1)S(1)} %shard_map.115), channel_id=1, source_target_pairs={{0,8},{4,12},{8,16},{12,20},{16,24},{20,28},{24,0},{28,4},{1,9},{5... | collective-permute-start | bytes 294920 | tf_op jit(solution)/shard_map/ppermute | solution.py:501
  122.1 1.5 %collective-permute-start.26 = (bf16[32,1536]{1,0:T(8,128)(2,1)S(1)}, bf16[32,1536]{1,0:T(8,128)(2,1)S(1)}, u32[]{:S(2)}, u32[]{:S(2)}) collective-permute-start(bf16[32,1536]{1,0:T(8,128)(2,1)S(1)} %shard_map.115), channel_id=1, source_target_pairs={{0,24},{4,28},{8,0},{12,4},{16,8},{20,12},{24,16},{28,20},{1,25},{... | collective-permute-start | bytes 294920 | tf_op jit(solution)/shard_map/ppermute | solution.py:501
  124.3 3.2 %shard_map.116 = bf16[32,1536]{1,0:T(8,128)(2,1)S(1)} custom-call(s32[9]{0:T(128)S(1)} %pad_add_fusion.odd_ref, bf16[96,768]{1,0:T(8,128)(2,1)S(1)} %get-tuple-element.122.mine_ref, bf16[96,768]{1,0:T(8,128)(2,1)S(1)} %collective-permute-done.23.other_ref, f32[3,96,1]{2,1,0:T(8,128)S(1)} %squeeze.109.taps_ref, ...), custom_call_target="tpu_custom_call" | custom-call | flops 1000000000 | bytes 4000000 | tf_op jit(solution)/shard_map/pallas_call | solution.py:262
  128.1 2.0 %collective-permute-start.33 = (bf16[32,1536]{1,0:T(8,128)(2,1)S(1)}, bf16[32,1536]{1,0:T(8,128)(2,1)S(1)}, u32[]{:S(2)}, u32[]{:S(2)}) collective-permute-start(bf16[32,1536]{1,0:T(8,128)(2,1)S(1)} %shard_map.116), channel_id=1, source_target_pairs={{0,16},{4,20},{8,24},{12,28},{16,0},{20,4},{24,8},{28,12},{1,17},{... | collective-permute-start | bytes 294920 | tf_op jit(solution)/shard_map/ppermute | solution.py:501
  130.1 1.4 collective-permute-start.34
  131.5 1.6 %collective-permute-start.27 = (bf16[4,32,1536]{2,1,0:T(8,128)(2,1)S(1)}, bf16[4,32,1536]{2,1,0:T(8,128)(2,1)S(1)}, u32[]{:S(2)}, u32[]{:S(2)}) collective-permute-start(bf16[4,32,1536]{2,1,0:T(8,128)(2,1)S(1)} %pad_maximum_fusion.2), channel_id=1, source_target_pairs={{0,4},{4,0},{8,12},{12,8},{16,20},{20,16},{24,28},{28,24},{1,5},{5... | collective-permute-start | bytes 1179656 | tf_op jit(solution)/shard_map/ppermute | solution.py:504
  134.1 1.8 %collective-permute-done.33 = bf16[32,1536]{1,0:T(8,128)(2,1)S(1)} collective-permute-done((bf16[32,1536]{1,0:T(8,128)(2,1)S(1)}, bf16[32,1536]{1,0:T(8,128)(2,1)S(1)}, u32[]{:S(2)}, u32[]{:S(2)}) %collective-permute-start.33) | collective-permute-done | bytes 98336 | tf_op jit(solution)/shard_map/ppermute | solution.py:501
  136.0 1.3 collective-permute-start.35
  137.3 5.3 %collective-permute-done.27 = bf16[4,32,1536]{2,1,0:T(8,128)(2,1)S(1)} collective-permute-done((bf16[4,32,1536]{2,1,0:T(8,128)(2,1)S(1)}, bf16[4,32,1536]{2,1,0:T(8,128)(2,1)S(1)}, u32[]{:S(2)}, u32[]{:S(2)}) %collective-permute-start.27) | collective-permute-done | bytes 393248 | tf_op jit(solution)/shard_map/ppermute | solution.py:504
  143.3 3.5 %collective-permute-done.35 = bf16[4,32,1536]{2,1,0:T(8,128)(2,1)S(1)} collective-permute-done((bf16[4,32,1536]{2,1,0:T(8,128)(2,1)S(1)}, bf16[4,32,1536]{2,1,0:T(8,128)(2,1)S(1)}, u32[]{:S(2)}, u32[]{:S(2)}) %collective-permute-start.35) | collective-permute-done | bytes 393248 | tf_op jit(solution)/shard_map/ppermute | solution.py:504
  148.0 1.3 broadcast_select_fusion.1
  149.5 2.0 %fusion = f32[512,512]{1,0:T(8,128)} fusion(bf16[512,1536]{1,0:T(8,128)(2,1)S(1)} %bitcast.227, bf16[1536,128]{1,0:T(8,128)(2,1)S(1)} %get-tuple-element.75, bf16[1536,128]{1,0:T(8,128)(2,1)S(1)} %get-tuple-element.134, bf16[1536,128]{1,0:T(8,128)(2,1)S(1)} %get-tuple-element.74, bf16[1536,128]{1,0:T(8,128)(2,1)S(1)} %get-tuple-element.135), kind=kOutput, calls=%fused_computation | convolution fusion | flops 811597824 | bytes 4194304 | tf_op jit(solution)/shard_map/dot_general | solution.py:514
  (135 shorter events, 21.3 us)
Async XLA Ops:
  0.6 34.0 %copy-start = (f32[3,3,512]{2,1,0:T(4,128)S(1)}, f32[3,3,512]{2,1,0:T(4,128)}, u32[]{:S(2)}) copy-start(f32[3,3,512]{2,1,0:T(4,128)} %param.12) | copy-start | bytes 55300
  0.6 24.5 %collective-permute-start.3 = (bf16[192,1024]{1,0:T(8,128)(2,1)}, bf16[192,1024]{1,0:T(8,128)(2,1)}, u32[]{:S(2)}, u32[]{:S(2)}) collective-permute-start(bf16[192,1024]{1,0:T(8,128)(2,1)} %param.10), channel_id=1, source_target_pairs={{0,8},{4,12},{8,16},{12,20},{16,24},{20,28},{1,9},{5,13},{9,17},{1... | collective-permute-start | bytes 1179656 | tf_op jit(solution)/shard_map/ppermute | solution.py:374
  6.3 18.8 %collective-permute-start.4 = (bf16[192,1024]{1,0:T(8,128)(2,1)}, bf16[192,1024]{1,0:T(8,128)(2,1)}, u32[]{:S(2)}, u32[]{:S(2)}) collective-permute-start(bf16[192,1024]{1,0:T(8,128)(2,1)} %param.10), channel_id=1, source_target_pairs={{8,0},{12,4},{16,8},{20,12},{24,16},{28,20},{9,1},{13,5},{17,9},{2... | collective-permute-start | bytes 1179656 | tf_op jit(solution)/shard_map/ppermute | solution.py:375
  9.1 10.4 %copy-start.2 = (bf16[192,4096]{1,0:T(8,128)(2,1)S(1)}, bf16[192,4096]{1,0:T(8,128)(2,1)}, u32[]{:S(2)}) copy-start(bf16[192,4096]{1,0:T(8,128)(2,1)} %grad_ref.1) | copy-start | bytes 4718596
  9.1 10.4 %copy-start.3 = (f32[2,192,512]{2,1,0:T(8,128)S(1)}, f32[2,192,512]{2,1,0:T(8,128)}, u32[]{:S(2)}) copy-start(f32[2,192,512]{2,1,0:T(8,128)} %value_ref.1) | copy-start | bytes 2359300
  10.7 18.7 %collective-permute-start = (bf16[384,512]{1,0:T(8,128)(2,1)}, bf16[384,512]{1,0:T(8,128)(2,1)}, u32[]{:S(2)}, u32[]{:S(2)}) collective-permute-start(bf16[384,512]{1,0:T(8,128)(2,1)} %get-tuple-element.33), channel_id=1, source_target_pairs={{0,0},{1,8},{2,16},{3,24},{4,4},{5,12},{6,20},{7,28},{8,1},{9,9},{... | collective-permute-start | bytes 1179656 | tf_op jit(solution)/shard_map/ppermute | solution.py:387
  15.1 19.8 %collective-permute-start.1 = (bf16[384,512]{1,0:T(8,128)(2,1)}, bf16[384,512]{1,0:T(8,128)(2,1)}, u32[]{:S(2)}, u32[]{:S(2)}) collective-permute-start(bf16[384,512]{1,0:T(8,128)(2,1)} %get-tuple-element.34), channel_id=1, source_target_pairs={{0,8},{1,16},{2,24},{3,0},{4,12},{5,20},{6,28},{7,4},{8,9},{9,17},... | collective-permute-start | bytes 1179656 | tf_op jit(solution)/shard_map/ppermute | solution.py:387
  15.3 23.7 %collective-permute-start.2 = (bf16[384,512]{1,0:T(8,128)(2,1)S(1)}, bf16[384,512]{1,0:T(8,128)(2,1)}, u32[]{:S(2)}, u32[]{:S(2)}) collective-permute-start(bf16[384,512]{1,0:T(8,128)(2,1)S(1)} %get-tuple-element.35), channel_id=1, source_target_pairs={{0,16},{1,24},{2,0},{3,8},{4,20},{5,28},{6,4},{7,12},{8,17},{9,25}... | collective-permute-start | bytes 1179656 | tf_op jit(solution)/shard_map/ppermute | solution.py:387
  25.2 30.7 %collective-permute-start.5 = (bf16[384,512]{1,0:T(8,128)(2,1)S(1)}, bf16[384,512]{1,0:T(8,128)(2,1)S(1)}, u32[]{:S(2)}, u32[]{:S(2)}) collective-permute-start(bf16[384,512]{1,0:T(8,128)(2,1)S(1)} %get-tuple-element.37), channel_id=1, source_target_pairs={{0,24},{1,0},{2,8},{3,16},{4,28},{5,4},{6,12},{7,20},{8,25},{9,1},... | collective-permute-start | bytes 1179656 | tf_op jit(solution)/shard_map/ppermute | solution.py:387
  28.1 25.0 %collective-permute-start.10 = (bf16[192,1024]{1,0:T(8,128)(2,1)}, bf16[192,1024]{1,0:T(8,128)(2,1)}, u32[]{:S(2)}, u32[]{:S(2)}) collective-permute-start(bf16[192,1024]{1,0:T(8,128)(2,1)} %collective-permute-done.4), channel_id=1, source_target_pairs={{8,0},{12,4},{16,8},{20,12},{24,16},{28,20},{9,1},{13,5},{17,9},{2... | collective-permute-start | bytes 1179656 | tf_op jit(solution)/shard_map/ppermute | solution.py:394
  29.4 25.2 %collective-permute-start.12 = (bf16[192,1024]{1,0:T(8,128)(2,1)}, bf16[192,1024]{1,0:T(8,128)(2,1)}, u32[]{:S(2)}, u32[]{:S(2)}) collective-permute-start(bf16[192,1024]{1,0:T(8,128)(2,1)} %collective-permute-done.3), channel_id=1, source_target_pairs={{0,8},{4,12},{8,16},{12,20},{16,24},{20,28},{1,9},{5,13},{9,17},{1... | collective-permute-start | bytes 1179656 | tf_op jit(solution)/shard_map/ppermute | solution.py:393
  34.9 32.6 %collective-permute-start.6 = (bf16[384,512]{1,0:T(8,128)(2,1)}, bf16[384,512]{1,0:T(8,128)(2,1)S(1)}, u32[]{:S(2)}, u32[]{:S(2)}) collective-permute-start(bf16[384,512]{1,0:T(8,128)(2,1)} %collective-permute-done), channel_id=1, source_target_pairs={{0,4},{4,0},{8,12},{12,8},{16,20},{20,16},{24,28},{28,24},{1,5},{5... | collective-permute-start | bytes 1179656 | tf_op jit(solution)/shard_map/ppermute | solution.py:388
  39.0 30.2 %collective-permute-start.7 = (bf16[384,512]{1,0:T(8,128)(2,1)}, bf16[384,512]{1,0:T(8,128)(2,1)S(1)}, u32[]{:S(2)}, u32[]{:S(2)}) collective-permute-start(bf16[384,512]{1,0:T(8,128)(2,1)} %collective-permute-done.1), channel_id=1, source_target_pairs={{0,4},{4,0},{8,12},{12,8},{16,20},{20,16},{24,28},{28,24},{1,5},{5... | collective-permute-start | bytes 1179656 | tf_op jit(solution)/shard_map/ppermute | solution.py:388
  53.0 16.3 %collective-permute-start.8 = (bf16[384,512]{1,0:T(8,128)(2,1)}, bf16[384,512]{1,0:T(8,128)(2,1)S(1)}, u32[]{:S(2)}, u32[]{:S(2)}) collective-permute-start(bf16[384,512]{1,0:T(8,128)(2,1)} %collective-permute-done.2), channel_id=1, source_target_pairs={{0,4},{4,0},{8,12},{12,8},{16,20},{20,16},{24,28},{28,24},{1,5},{5... | collective-permute-start | bytes 1179656 | tf_op jit(solution)/shard_map/ppermute | solution.py:388
  54.6 19.8 %collective-permute-start.11 = (bf16[192,1024]{1,0:T(8,128)(2,1)}, bf16[192,1024]{1,0:T(8,128)(2,1)S(1)}, u32[]{:S(2)}, u32[]{:S(2)}) collective-permute-start(bf16[192,1024]{1,0:T(8,128)(2,1)} %collective-permute-done.10), channel_id=1, source_target_pairs={{8,0},{12,4},{16,8},{20,12},{24,16},{28,20},{9,1},{13,5},{17,9},{2... | collective-permute-start | bytes 1179656 | tf_op jit(solution)/shard_map/ppermute | solution.py:396
  55.9 19.8 %collective-permute-start.13 = (bf16[192,1024]{1,0:T(8,128)(2,1)}, bf16[192,1024]{1,0:T(8,128)(2,1)S(1)}, u32[]{:S(2)}, u32[]{:S(2)}) collective-permute-start(bf16[192,1024]{1,0:T(8,128)(2,1)} %collective-permute-done.12), channel_id=1, source_target_pairs={{0,8},{4,12},{8,16},{12,20},{16,24},{20,28},{1,9},{5,13},{9,17},{1... | collective-permute-start | bytes 1179656 | tf_op jit(solution)/shard_map/ppermute | solution.py:395
  67.6 8.1 %copy-start.12 = (bf16[2,192,128]{2,1,0:T(8,128)(2,1)S(1)}, bf16[2,192,128]{2,1,0:T(8,128)(2,1)}, u32[]{:S(2)}) copy-start(bf16[2,192,128]{2,1,0:T(8,128)(2,1)} %get-tuple-element.42) | copy-start | bytes 294916
  67.6 10.4 %copy-start.11 = (bf16[2,192,128]{2,1,0:T(8,128)(2,1)S(1)}, bf16[2,192,128]{2,1,0:T(8,128)(2,1)}, u32[]{:S(2)}) copy-start(bf16[2,192,128]{2,1,0:T(8,128)(2,1)} %get-tuple-element.41) | copy-start | bytes 294916
  67.6 11.9 %copy-start.10 = (bf16[2,192,128]{2,1,0:T(8,128)(2,1)S(1)}, bf16[2,192,128]{2,1,0:T(8,128)(2,1)}, u32[]{:S(2)}) copy-start(bf16[2,192,128]{2,1,0:T(8,128)(2,1)} %get-tuple-element.40) | copy-start | bytes 294916
  67.6 16.1 %collective-permute-start.9 = (bf16[384,512]{1,0:T(8,128)(2,1)S(1)}, bf16[384,512]{1,0:T(8,128)(2,1)S(1)}, u32[]{:S(2)}, u32[]{:S(2)}) collective-permute-start(bf16[384,512]{1,0:T(8,128)(2,1)S(1)} %collective-permute-done.5), channel_id=1, source_target_pairs={{0,4},{4,0},{8,12},{12,8},{16,20},{20,16},{24,28},{28,24},{1,5},{5... | collective-permute-start | bytes 1179656 | tf_op jit(solution)/shard_map/ppermute | solution.py:388
  75.7 8.1 %collective-permute-start.16 = (bf16[2,192,128]{2,1,0:T(8,128)(2,1)S(1)}, bf16[2,192,128]{2,1,0:T(8,128)(2,1)S(1)}, u32[]{:S(2)}, u32[]{:S(2)}) collective-permute-start(bf16[2,192,128]{2,1,0:T(8,128)(2,1)S(1)} %copy-done.12), channel_id=1, source_target_pairs={{0,8},{4,12},{8,16},{12,20},{16,24},{20,28},{24,0},{28,4},{1,9},{5... | collective-permute-start | bytes 294920 | tf_op jit(solution)/shard_map/ppermute | solution.py:409
  78.0 8.0 %collective-permute-start.15 = (bf16[2,192,128]{2,1,0:T(8,128)(2,1)S(1)}, bf16[2,192,128]{2,1,0:T(8,128)(2,1)S(1)}, u32[]{:S(2)}, u32[]{:S(2)}) collective-permute-start(bf16[2,192,128]{2,1,0:T(8,128)(2,1)S(1)} %copy-done.11), channel_id=1, source_target_pairs={{0,16},{4,20},{8,24},{12,28},{16,0},{20,4},{24,8},{28,12},{1,17},{... | collective-permute-start | bytes 294920 | tf_op jit(solution)/shard_map/ppermute | solution.py:409
  79.5 6.5 %collective-permute-start.14 = (bf16[2,192,128]{2,1,0:T(8,128)(2,1)S(1)}, bf16[2,192,128]{2,1,0:T(8,128)(2,1)S(1)}, u32[]{:S(2)}, u32[]{:S(2)}) collective-permute-start(bf16[2,192,128]{2,1,0:T(8,128)(2,1)S(1)} %copy-done.10), channel_id=1, source_target_pairs={{0,24},{4,28},{8,0},{12,4},{16,8},{20,12},{24,16},{28,20},{1,25},{... | collective-permute-start | bytes 294920 | tf_op jit(solution)/shard_map/ppermute | solution.py:409
  83.8 4.1 %copy-start.6 = (bf16[2,2,2,192,1024]{4,3,2,1,0:T(8,128)(2,1)}, bf16[2,2,2,192,1024]{4,3,2,1,0:T(8,128)(2,1)S(1)}, u32[]{:S(2)}) copy-start(bf16[2,2,2,192,1024]{4,3,2,1,0:T(8,128)(2,1)S(1)} %constant_dynamic-update-slice_fusion) | copy-start | bytes 9437188
  87.9 5.6 %collective-permute-start.17 = (f32[2,192,768]{2,1,0:T(8,128)}, f32[2,192,768]{2,1,0:T(8,128)}, u32[]{:S(2)}, u32[]{:S(2)}) collective-permute-start(f32[2,192,768]{2,1,0:T(8,128)} %fusion.10), channel_id=1, source_target_pairs={{0,1},{1,0},{2,3},{3,2},{4,5},{5,4},{6,7},{7,6},{8,9},{9,8},{10,11... | collective-permute-start | bytes 3538952 | tf_op jit(solution)/shard_map/ppermute | solution.py:372
  89.8 5.0 %collective-permute-start.21 = (f32[2,192,768]{2,1,0:T(8,128)}, f32[2,192,768]{2,1,0:T(8,128)S(1)}, u32[]{:S(2)}, u32[]{:S(2)}) collective-permute-start(f32[2,192,768]{2,1,0:T(8,128)} %fusion.8), channel_id=1, source_target_pairs={{0,1},{1,0},{2,3},{3,2},{4,5},{5,4},{6,7},{7,6},{8,9},{9,8},{10,11... | collective-permute-start | bytes 3538952 | tf_op jit(solution)/shard_map/ppermute | solution.py:372
  94.7 9.9 %collective-permute-start.18 = (bf16[192,768]{1,0:T(8,128)(2,1)S(1)}, bf16[192,768]{1,0:T(8,128)(2,1)S(1)}, u32[]{:S(2)}, u32[]{:S(2)}) collective-permute-start(bf16[192,768]{1,0:T(8,128)(2,1)S(1)} %fusion.18), channel_id=1, source_target_pairs={{0,2},{1,3},{2,0},{3,1},{4,6},{5,7},{6,4},{7,5},{8,10},{9,11},{10,... | collective-permute-start | bytes 884744 | tf_op jit(solution)/shard_map/ppermute | solution.py:372
  95.5 16.9 %collective-permute-start.22 = (bf16[192,768]{1,0:T(8,128)(2,1)}, bf16[192,768]{1,0:T(8,128)(2,1)}, u32[]{:S(2)}, u32[]{:S(2)}) collective-permute-start(bf16[192,768]{1,0:T(8,128)(2,1)} %fusion.13), channel_id=1, source_target_pairs={{0,2},{1,3},{2,0},{3,1},{4,6},{5,7},{6,4},{7,5},{8,10},{9,11},{10,... | collective-permute-start | bytes 884744 | tf_op jit(solution)/shard_map/ppermute | solution.py:372
  98.3 14.1 %copy-start.9 = (f32[384,768]{1,0:T(8,128)S(1)}, f32[384,768]{1,0:T(8,128)}, u32[]{:S(2)}) copy-start(f32[384,768]{1,0:T(8,128)} %copy-done.8) | copy-start | bytes 3538948
  98.3 12.4 %collective-permute-start.20 = (bf16[4,192,128]{2,1,0:T(8,128)(2,1)}, bf16[4,192,128]{2,1,0:T(8,128)(2,1)}, u32[]{:S(2)}, u32[]{:S(2)}) collective-permute-start(bf16[4,192,128]{2,1,0:T(8,128)(2,1)} %get-tuple-element.108), channel_id=1, source_target_pairs={{0,4},{4,0},{8,12},{12,8},{16,20},{20,16},{24,28},{28,24},{1,5},{5... | collective-permute-start | bytes 589832 | tf_op jit(solution)/shard_map/ppermute | solution.py:448
  106.4 6.0 %collective-permute-start.19 = (bf16[96,768]{1,0:T(8,128)(2,1)}, bf16[96,768]{1,0:T(8,128)(2,1)S(1)}, u32[]{:S(2)}, u32[]{:S(2)}) collective-permute-start(bf16[96,768]{1,0:T(8,128)(2,1)} %get-tuple-element.124), channel_id=1, source_target_pairs={{0,4},{4,0},{8,12},{12,8},{16,20},{20,16},{24,28},{28,24},{1,5},{5... | collective-permute-start | bytes 442376 | tf_op jit(solution)/shard_map/ppermute | solution.py:471
  107.4 13.8 %collective-permute-start.28 = (bf16[2,192,128]{2,1,0:T(8,128)(2,1)}, bf16[2,192,128]{2,1,0:T(8,128)(2,1)S(1)}, u32[]{:S(2)}, u32[]{:S(2)}) collective-permute-start(bf16[2,192,128]{2,1,0:T(8,128)(2,1)} %get-tuple-element.54), channel_id=1, source_target_pairs={{0,24},{4,28},{8,0},{12,4},{16,8},{20,12},{24,16},{28,20},{1,25},{... | collective-permute-start | bytes 294920 | tf_op jit(solution)/shard_map/ppermute | solution.py:409
  110.7 11.4 %collective-permute-start.29 = (bf16[2,192,128]{2,1,0:T(8,128)(2,1)}, bf16[2,192,128]{2,1,0:T(8,128)(2,1)S(1)}, u32[]{:S(2)}, u32[]{:S(2)}) collective-permute-start(bf16[2,192,128]{2,1,0:T(8,128)(2,1)} %get-tuple-element.56), channel_id=1, source_target_pairs={{0,16},{4,20},{8,24},{12,28},{16,0},{20,4},{24,8},{28,12},{1,17},{... | collective-permute-start | bytes 294920 | tf_op jit(solution)/shard_map/ppermute | solution.py:409
  110.7 12.9 %collective-permute-start.30 = (bf16[2,192,128]{2,1,0:T(8,128)(2,1)S(1)}, bf16[2,192,128]{2,1,0:T(8,128)(2,1)S(1)}, u32[]{:S(2)}, u32[]{:S(2)}) collective-permute-start(bf16[2,192,128]{2,1,0:T(8,128)(2,1)S(1)} %get-tuple-element.58), channel_id=1, source_target_pairs={{0,8},{4,12},{8,16},{12,20},{16,24},{20,28},{24,0},{28,4},{1,9},{5... | collective-permute-start | bytes 294920 | tf_op jit(solution)/shard_map/ppermute | solution.py:409
  111.4 3.8 %copy-start.4 = (f32[192,512]{1,0:T(8,128)S(1)}, f32[192,512]{1,0:T(8,128)}, u32[]{:S(2)}) copy-start(f32[192,512]{1,0:T(8,128)} %constant.269.clone.table_ref) | copy-start | bytes 1179652
  111.4 3.8 %copy-start.5 = (f32[2,5,192]{2,1,0:T(8,128)S(1)}, f32[2,5,192]{2,1,0:T(8,128)}, u32[]{:S(2)}) copy-start(f32[2,5,192]{2,1,0:T(8,128)} %constant.270.clone.turn_ref) | copy-start | bytes 23044
  113.5 10.8 %collective-permute-start.23 = (bf16[96,768]{1,0:T(8,128)(2,1)S(1)}, bf16[96,768]{1,0:T(8,128)(2,1)S(1)}, u32[]{:S(2)}, u32[]{:S(2)}) collective-permute-start(bf16[96,768]{1,0:T(8,128)(2,1)S(1)} %get-tuple-element.123), channel_id=1, source_target_pairs={{0,4},{4,0},{8,12},{12,8},{16,20},{20,16},{24,28},{28,24},{1,5},{5... | collective-permute-start | bytes 442376 | tf_op jit(solution)/shard_map/ppermute | solution.py:471
  118.3 9.8 %collective-permute-start.24 = (bf16[32,1536]{1,0:T(8,128)(2,1)S(1)}, bf16[32,1536]{1,0:T(8,128)(2,1)S(1)}, u32[]{:S(2)}, u32[]{:S(2)}) collective-permute-start(bf16[32,1536]{1,0:T(8,128)(2,1)S(1)} %shard_map.115), channel_id=1, source_target_pairs={{0,8},{4,12},{8,16},{12,20},{16,24},{20,28},{24,0},{28,4},{1,9},{5... | collective-permute-start | bytes 294920 | tf_op jit(solution)/shard_map/ppermute | solution.py:501
  121.2 8.9 %collective-permute-start.25 = (bf16[32,1536]{1,0:T(8,128)(2,1)S(1)}, bf16[32,1536]{1,0:T(8,128)(2,1)S(1)}, u32[]{:S(2)}, u32[]{:S(2)}) collective-permute-start(bf16[32,1536]{1,0:T(8,128)(2,1)S(1)} %shard_map.115), channel_id=1, source_target_pairs={{0,16},{4,20},{8,24},{12,28},{16,0},{20,4},{24,8},{28,12},{1,17},{... | collective-permute-start | bytes 294920 | tf_op jit(solution)/shard_map/ppermute | solution.py:501
  122.1 9.3 %collective-permute-start.26 = (bf16[32,1536]{1,0:T(8,128)(2,1)S(1)}, bf16[32,1536]{1,0:T(8,128)(2,1)S(1)}, u32[]{:S(2)}, u32[]{:S(2)}) collective-permute-start(bf16[32,1536]{1,0:T(8,128)(2,1)S(1)} %shard_map.115), channel_id=1, source_target_pairs={{0,24},{4,28},{8,0},{12,4},{16,8},{20,12},{24,16},{28,20},{1,25},{... | collective-permute-start | bytes 294920 | tf_op jit(solution)/shard_map/ppermute | solution.py:501
  123.7 9.4 %collective-permute-start.31 = (bf16[4,192,128]{2,1,0:T(8,128)(2,1)S(1)}, bf16[4,192,128]{2,1,0:T(8,128)(2,1)S(1)}, u32[]{:S(2)}, u32[]{:S(2)}) collective-permute-start(bf16[4,192,128]{2,1,0:T(8,128)(2,1)S(1)} %dynamic-slice_bitcast_fusion.1), channel_id=1, source_target_pairs={{0,4},{4,0},{8,12},{12,8},{16,20},{20,16},{24,28},{28,24},{1,5},{5... | collective-permute-start | bytes 589832 | tf_op jit(solution)/shard_map/ppermute | solution.py:448
  127.5 6.6 %collective-permute-start.32 = (bf16[32,1536]{1,0:T(8,128)(2,1)S(1)}, bf16[32,1536]{1,0:T(8,128)(2,1)S(1)}, u32[]{:S(2)}, u32[]{:S(2)}) collective-permute-start(bf16[32,1536]{1,0:T(8,128)(2,1)S(1)} %shard_map.116), channel_id=1, source_target_pairs={{0,8},{4,12},{8,16},{12,20},{16,24},{20,28},{24,0},{28,4},{1,9},{5... | collective-permute-start | bytes 294920 | tf_op jit(solution)/shard_map/ppermute | solution.py:501
  128.1 7.9 %collective-permute-start.33 = (bf16[32,1536]{1,0:T(8,128)(2,1)S(1)}, bf16[32,1536]{1,0:T(8,128)(2,1)S(1)}, u32[]{:S(2)}, u32[]{:S(2)}) collective-permute-start(bf16[32,1536]{1,0:T(8,128)(2,1)S(1)} %shard_map.116), channel_id=1, source_target_pairs={{0,16},{4,20},{8,24},{12,28},{16,0},{20,4},{24,8},{28,12},{1,17},{... | collective-permute-start | bytes 294920 | tf_op jit(solution)/shard_map/ppermute | solution.py:501
  130.1 5.8 %collective-permute-start.34 = (bf16[32,1536]{1,0:T(8,128)(2,1)S(1)}, bf16[32,1536]{1,0:T(8,128)(2,1)S(1)}, u32[]{:S(2)}, u32[]{:S(2)}) collective-permute-start(bf16[32,1536]{1,0:T(8,128)(2,1)S(1)} %shard_map.116), channel_id=1, source_target_pairs={{0,24},{4,28},{8,0},{12,4},{16,8},{20,12},{24,16},{28,20},{1,25},{... | collective-permute-start | bytes 294920 | tf_op jit(solution)/shard_map/ppermute | solution.py:501
  131.5 11.1 %collective-permute-start.27 = (bf16[4,32,1536]{2,1,0:T(8,128)(2,1)S(1)}, bf16[4,32,1536]{2,1,0:T(8,128)(2,1)S(1)}, u32[]{:S(2)}, u32[]{:S(2)}) collective-permute-start(bf16[4,32,1536]{2,1,0:T(8,128)(2,1)S(1)} %pad_maximum_fusion.2), channel_id=1, source_target_pairs={{0,4},{4,0},{8,12},{12,8},{16,20},{20,16},{24,28},{28,24},{1,5},{5... | collective-permute-start | bytes 1179656 | tf_op jit(solution)/shard_map/ppermute | solution.py:504
  133.3 9.7 %collective-permute-start.36 = (bf16[1536,128]{1,0:T(8,128)(2,1)S(1)}, bf16[1536,128]{1,0:T(8,128)(2,1)S(1)}, u32[]{:S(2)}, u32[]{:S(2)}) collective-permute-start(bf16[1536,128]{1,0:T(8,128)(2,1)S(1)} %bitcast.234), channel_id=1, source_target_pairs={{0,2},{1,3},{2,0},{3,1},{4,6},{5,7},{6,4},{7,5},{8,10},{9,11},{10,... | collective-permute-start | bytes 1179656 | tf_op jit(solution)/shard_map/ppermute | solution.py:372
  136.0 10.8 %collective-permute-start.35 = (bf16[4,32,1536]{2,1,0:T(8,128)(2,1)S(1)}, bf16[4,32,1536]{2,1,0:T(8,128)(2,1)S(1)}, u32[]{:S(2)}, u32[]{:S(2)}) collective-permute-start(bf16[4,32,1536]{2,1,0:T(8,128)(2,1)S(1)} %pad_maximum_fusion.4), channel_id=1, source_target_pairs={{0,4},{4,0},{8,12},{12,8},{16,20},{20,16},{24,28},{28,24},{1,5},{5... | collective-permute-start | bytes 1179656 | tf_op jit(solution)/shard_map/ppermute | solution.py:504
  143.2 4.8 %collective-permute-start.37 = (bf16[2,1536,128]{2,1,0:T(8,128)(2,1)S(1)}, bf16[2,1536,128]{2,1,0:T(8,128)(2,1)}, u32[]{:S(2)}, u32[]{:S(2)}) collective-permute-start(bf16[2,1536,128]{2,1,0:T(8,128)(2,1)S(1)} %pad_maximum_fusion), channel_id=1, source_target_pairs={{0,1},{1,0},{2,3},{3,2},{4,5},{5,4},{6,7},{7,6},{8,9},{9,8},{10,11... | collective-permute-start | bytes 2359304 | tf_op jit(solution)/shard_map/ppermute | solution.py:372
  (5 other events, 7.3 us)

commit v5 on v4

--- a/solution.py
+++ b/solution.py
@@ -410,7 +410,7 @@
             found.append(piece)
         return found
 
-    filters = along(packed[:, 0], up3, down3, *pieces[:m])
+    filters = along(packed[:, 0], up2, down2)
 
     whole = jnp.zeros((pairs, rows, depth), features.dtype)
     for shift, value in enumerate([features] + behind):
@@ -420,7 +420,7 @@
             jnp.concatenate([value[:, block_depth:], value[:, :block_depth]], axis=1),
         )
         whole = lax.dynamic_update_slice(whole, value[None], ((line - shift) % pairs, 0, 0))
-    whole = after(whole.reshape(pairs * rows, depth), *filters)
+    whole = whole.reshape(pairs * rows, depth)
 
     count = m // 2
     spot = 3 * 2 * sub

time: 153 us -> 151 us (0.987)
  waiting for transfers between devices: 37.8 us -> 27.7 us
  starting transfers between devices: 69.4 us -> 78.4 us
    ppermute x1, waiting for transfers between devices: 12.4 us -> 3.18 us  [special(): down2 = lax.ppermute(down1, 'ctx', down)]
    ppermute x1, starting transfers between devices: 11.6 us -> 19 us  [special(): up3 = lax.ppermute(after(up2, packed), 'ctx', up)]
    ppermute x4, waiting for transfers between devices: 0.01 us -> 4.06 us  [special(): pieces.append(lax.ppermute(piece, BOTH, hops))]
    ppermute x1, waiting for transfers between devices: 4.96 us -> 2.06 us  [special(): down3 = lax.ppermute(after(down2, packed), 'ctx', down)]
    ppermute x4, starting transfers between devices: 9.92 us -> 7.64 us  [special(): pieces.append(lax.ppermute(piece, BOTH, hops))]
    ppermute x6, waiting for transfers between devices: 2.24 us -> 0.05 us  [along(): piece = lax.ppermute(after(piece, *others), 'ctx', back)]
    ppermute x2, starting transfers between devices: 1.08 us -> 3.11 us  [beside(): return (mine, lax.ppermute(give, 'ctx', flips))]
    ppermute x6, starting transfers between devices: 3 us -> 4.74 us  [trade(): return lax.ppermute(value, 'ch', [(j, j ^ 1 << bit) for j in range(m)])]
where the time goes in v5:
time: 151 us; the launch traced here: 150 us
  starting transfers between devices  78.4 us (52%)
  waiting for transfers between devices  27.7 us (18%)
  local copies, waits for them, and re-layouts  15.3 us (10%)
  other arithmetic  11.2 us (7%)
  Pallas kernels  8.91 us (6%)
  matrix products  7.4 us (5%)
    ppermute x1, starting transfers between devices, special(): up3 = lax.ppermute(after(up2, packed), 'ctx', up)  19 us
    ppermute x6, starting transfers between devices, along(): piece = lax.ppermute(after(piece, *others), 'ctx', back)  12 us
    ppermute x6, starting transfers between devices, special(): lax.ppermute(gated[part], 'ctx', shifts[s])  9.28 us
    ppermute x2, waiting for transfers between devices, special(): other = lax.ppermute(near, 'ctx', flips)  8.29 us
    ppermute x4, starting transfers between devices, special(): pieces.append(lax.ppermute(piece, BOTH, hops))  7.64 us
    pallas_call x2, Pallas kernels, convolve(): pl.pallas_call(convolve_kernel, out_shape=jax.ShapeDtypeStruct((own, tota...  6.36 us
    ppermute x1, starting transfers between devices, special(): up1 = lax.ppermute(features, 'ctx', up)  5.67 us
    ppermute x1, starting transfers between devices, special(): up2 = lax.ppermute(up1, 'ctx', up)  5.46 us
  transfers between devices with their start and end apart: 38, of which 9 were waited for; matrix products, arithmetic and copies ran while one was open for 18% of the time, Pallas kernels for 6%

profile of v5, /device:TPU:0, one launch (start us, length us, event | category | flops | bytes accessed | tf_op | source)
XLA Modules:
  0.0 150.3 jit_solution(2345257163541069753)
XLA Ops:
  0.6 5.7 %collective-permute-start.3 = (bf16[192,1024]{1,0:T(8,128)(2,1)}, bf16[192,1024]{1,0:T(8,128)(2,1)}, u32[]{:S(2)}, u32[]{:S(2)}) collective-permute-start(bf16[192,1024]{1,0:T(8,128)(2,1)} %param.10), channel_id=1, source_target_pairs={{0,8},{4,12},{8,16},{12,20},{16,24},{20,28},{1,9},{5,13},{9,17},{1... | collective-permute-start | bytes 1179656 | tf_op jit(solution)/shard_map/ppermute | solution.py:374
  6.3 1.3 collective-permute-start.4
  7.6 1.4 copy-done.1
  9.0 1.6 %shard_map.113 = (bf16[384,512]{1,0:T(8,128)(2,1)}, bf16[384,512]{1,0:T(8,128)(2,1)}, bf16[384,512]{1,0:T(8,128)(2,1)S(1)}, bf16[384,512]{1,0:T(8,128)(2,1)S(1)}) custom-call(s32[4]{0:T(128)S(1)} %and_select_fusion.which_ref, bf16[3,512,512]{2,1,0:T(8,128)(2,1)S(1)} %bitcast.220), custom_call_target="tpu_custom_call" | custom-call | bytes 3145728 | tf_op jit(solution)/shard_map/pallas_call | solution.py:332
  10.6 4.5 %collective-permute-start = (bf16[384,512]{1,0:T(8,128)(2,1)}, bf16[384,512]{1,0:T(8,128)(2,1)}, u32[]{:S(2)}, u32[]{:S(2)}) collective-permute-start(bf16[384,512]{1,0:T(8,128)(2,1)} %get-tuple-element.32), channel_id=1, source_target_pairs={{0,0},{1,8},{2,16},{3,24},{4,4},{5,12},{6,20},{7,28},{8,1},{9,9},{... | collective-permute-start | bytes 1179656 | tf_op jit(solution)/shard_map/ppermute | solution.py:387
  15.3 2.4 %collective-permute-start.2 = (bf16[384,512]{1,0:T(8,128)(2,1)S(1)}, bf16[384,512]{1,0:T(8,128)(2,1)}, u32[]{:S(2)}, u32[]{:S(2)}) collective-permute-start(bf16[384,512]{1,0:T(8,128)(2,1)S(1)} %get-tuple-element.34), channel_id=1, source_target_pairs={{0,16},{1,24},{2,0},{3,8},{4,20},{5,28},{6,4},{7,12},{8,17},{9,25}... | collective-permute-start | bytes 1179656 | tf_op jit(solution)/shard_map/ppermute | solution.py:387
  17.7 1.7 %fusion.55 = (bf16[192,512]{1,0:T(8,128)(2,1)S(1)}, bf16[192,512]{1,0:T(8,128)(2,1)}) fusion(bf16[192,1024]{1,0:T(8,128)(2,1)} %param.10), kind=kLoop, calls=%fused_computation.137 | loop fusion | bytes 786432 | tf_op jit(solution)/shard_map/slice | solution.py:420
  21.5 1.0 fusion.24
  22.7 1.7 %dynamic-slice_bitcast_fusion.10 = (bf16[2,192,128]{2,1,0:T(8,128)(2,1)S(1)}, bf16[2,192,128]{2,1,0:T(8,128)(2,1)S(1)}, bf16[2,192,128]{2,1,0:T(8,128)(2,1)}, bf16[2,192,128]{2,1,0:T(8,128)(2,1)}) fusion(bf16[4,2,192,128]{3,2,1,0:T(8,128)(2,1)} %bitcast.232, s32[]{:T(128)S(6)} %select_n.349, s32[]{:T(128)S(6)} %select_n.361, s32[]{:T(128)S(6)} %select_n.357, ...), kind=kLoop, calls=%fused_computation.99 | loop fusion | bytes 786448 | tf_op jit(solution)/shard_map/jit(dynamic_index_in_dim)/squeeze | solution.py:406
  25.1 1.3 collective-permute-start.10
  26.4 5.5 %collective-permute-start.12 = (bf16[192,1024]{1,0:T(8,128)(2,1)}, bf16[192,1024]{1,0:T(8,128)(2,1)}, u32[]{:S(2)}, u32[]{:S(2)}) collective-permute-start(bf16[192,1024]{1,0:T(8,128)(2,1)} %collective-permute-done.3), channel_id=1, source_target_pairs={{0,8},{4,12},{8,16},{12,20},{16,24},{20,28},{1,9},{5,13},{9,17},{1... | collective-permute-start | bytes 1179656 | tf_op jit(solution)/shard_map/ppermute | solution.py:393
  34.2 1.6 %collective-permute-start.6 = (bf16[384,512]{1,0:T(8,128)(2,1)}, bf16[384,512]{1,0:T(8,128)(2,1)S(1)}, u32[]{:S(2)}, u32[]{:S(2)}) collective-permute-start(bf16[384,512]{1,0:T(8,128)(2,1)} %collective-permute-done), channel_id=1, source_target_pairs={{0,4},{4,0},{8,12},{12,8},{16,20},{20,16},{24,28},{28,24},{1,5},{5... | collective-permute-start | bytes 1179656 | tf_op jit(solution)/shard_map/ppermute | solution.py:388
  38.5 3.2 %collective-permute-done.10 = bf16[192,1024]{1,0:T(8,128)(2,1)} collective-permute-done((bf16[192,1024]{1,0:T(8,128)(2,1)}, bf16[192,1024]{1,0:T(8,128)(2,1)}, u32[]{:S(2)}, u32[]{:S(2)}) %collective-permute-start.10) | collective-permute-done | bytes 393248 | tf_op jit(solution)/shard_map/ppermute | solution.py:394
  41.7 1.5 %collective-permute-start.8 = (bf16[384,512]{1,0:T(8,128)(2,1)}, bf16[384,512]{1,0:T(8,128)(2,1)S(1)}, u32[]{:S(2)}, u32[]{:S(2)}) collective-permute-start(bf16[384,512]{1,0:T(8,128)(2,1)} %collective-permute-done.2), channel_id=1, source_target_pairs={{0,4},{4,0},{8,12},{12,8},{16,20},{20,16},{24,28},{28,24},{1,5},{5... | collective-permute-start | bytes 1179656 | tf_op jit(solution)/shard_map/ppermute | solution.py:388
  43.2 1.3 collective-permute-start.11
  44.5 1.1 broadcast_select_fusion.3
  45.6 4.0 %collective-permute-done.5 = bf16[384,512]{1,0:T(8,128)(2,1)S(1)} collective-permute-done((bf16[384,512]{1,0:T(8,128)(2,1)S(1)}, bf16[384,512]{1,0:T(8,128)(2,1)S(1)}, u32[]{:S(2)}, u32[]{:S(2)}) %collective-permute-start.5) | collective-permute-done | bytes 393248 | tf_op jit(solution)/shard_map/ppermute | solution.py:387
  49.6 19.0 %collective-permute-start.13 = (bf16[192,1024]{1,0:T(8,128)(2,1)}, bf16[192,1024]{1,0:T(8,128)(2,1)S(1)}, u32[]{:S(2)}, u32[]{:S(2)}) collective-permute-start(bf16[192,1024]{1,0:T(8,128)(2,1)} %collective-permute-done.12), channel_id=1, source_target_pairs={{0,8},{4,12},{8,16},{12,20},{16,24},{20,28},{1,9},{5,13},{9,17},{1... | collective-permute-start | bytes 1179656 | tf_op jit(solution)/shard_map/ppermute | solution.py:395
  69.4 2.1 %collective-permute-done.11 = bf16[192,1024]{1,0:T(8,128)(2,1)S(1)} collective-permute-done((bf16[192,1024]{1,0:T(8,128)(2,1)}, bf16[192,1024]{1,0:T(8,128)(2,1)S(1)}, u32[]{:S(2)}, u32[]{:S(2)}) %collective-permute-start.11) | collective-permute-done | bytes 393248 | tf_op jit(solution)/shard_map/ppermute | solution.py:396
  71.5 2.6 %collective-permute-done.13 = bf16[192,1024]{1,0:T(8,128)(2,1)S(1)} collective-permute-done((bf16[192,1024]{1,0:T(8,128)(2,1)}, bf16[192,1024]{1,0:T(8,128)(2,1)S(1)}, u32[]{:S(2)}, u32[]{:S(2)}) %collective-permute-start.13) | collective-permute-done | bytes 393248 | tf_op jit(solution)/shard_map/ppermute | solution.py:395
  75.3 1.3 collective-permute-done.9
  77.0 1.9 %fusion.9 = f32[2,192,768]{2,1,0:T(8,128)} fusion(bf16[768,1024,1]{1,0,2:T(8,128)(2,1)S(1)} %bitcast.227, bf16[2,2,2,192,1024]{4,3,2,1,0:T(8,128)(2,1)S(1)} %constant_dynamic-update-slice_fusion), kind=kOutput, calls=%fused_computation.11 | convolution fusion | flops 603979776 | bytes 3538944 | tf_op jit(solution)/shard_map/dot_general | solution.py:439
  79.0 1.8 %fusion.8 = f32[2,192,768]{2,1,0:T(8,128)} fusion(bf16[768,1024,1]{1,0,2:T(8,128)(2,1)S(1)} %bitcast.228, bf16[2,2,2,192,1024]{4,3,2,1,0:T(8,128)(2,1)S(1)} %constant_dynamic-update-slice_fusion), kind=kOutput, calls=%fused_computation.9 | convolution fusion | flops 603979776 | bytes 3538944 | tf_op jit(solution)/shard_map/dot_general | solution.py:439
  81.4 3.3 %collective-permute-start.17 = (bf16[2,192,128]{2,1,0:T(8,128)(2,1)S(1)}, bf16[2,192,128]{2,1,0:T(8,128)(2,1)S(1)}, u32[]{:S(2)}, u32[]{:S(2)}) collective-permute-start(bf16[2,192,128]{2,1,0:T(8,128)(2,1)S(1)} %copy-done.12), channel_id=1, source_target_pairs={{0,24},{4,28},{8,0},{12,4},{16,8},{20,12},{24,16},{28,20},{1,25},{... | collective-permute-start | bytes 294920 | tf_op jit(solution)/shard_map/ppermute | solution.py:409
  84.7 3.1 %collective-permute-start.18 = (bf16[2,192,128]{2,1,0:T(8,128)(2,1)S(1)}, bf16[2,192,128]{2,1,0:T(8,128)(2,1)S(1)}, u32[]{:S(2)}, u32[]{:S(2)}) collective-permute-start(bf16[2,192,128]{2,1,0:T(8,128)(2,1)S(1)} %copy-done.11), channel_id=1, source_target_pairs={{0,16},{4,20},{8,24},{12,28},{16,0},{20,4},{24,8},{28,12},{1,17},{... | collective-permute-start | bytes 294920 | tf_op jit(solution)/shard_map/ppermute | solution.py:409
  87.8 1.9 %collective-permute-start.19 = (bf16[2,192,128]{2,1,0:T(8,128)(2,1)S(1)}, bf16[2,192,128]{2,1,0:T(8,128)(2,1)S(1)}, u32[]{:S(2)}, u32[]{:S(2)}) collective-permute-start(bf16[2,192,128]{2,1,0:T(8,128)(2,1)S(1)} %copy-done.10), channel_id=1, source_target_pairs={{0,8},{4,12},{8,16},{12,20},{16,24},{20,28},{24,0},{28,4},{1,9},{5... | collective-permute-start | bytes 294920 | tf_op jit(solution)/shard_map/ppermute | solution.py:409
  89.7 1.5 fusion.46
  92.9 1.2 fusion.16
  94.1 1.2 collective-permute-start.15
  97.8 1.5 %collective-permute-start.20 = (bf16[4,192,128]{2,1,0:T(8,128)(2,1)}, bf16[4,192,128]{2,1,0:T(8,128)(2,1)}, u32[]{:S(2)}, u32[]{:S(2)}) collective-permute-start(bf16[4,192,128]{2,1,0:T(8,128)(2,1)} %get-tuple-element.106), channel_id=1, source_target_pairs={{0,4},{4,0},{8,12},{12,8},{16,20},{20,16},{24,28},{28,24},{1,5},{5... | collective-permute-start | bytes 589832 | tf_op jit(solution)/shard_map/ppermute | solution.py:448
  99.3 4.8 %collective-permute-done.15 = bf16[192,768]{1,0:T(8,128)(2,1)S(1)} collective-permute-done((bf16[192,768]{1,0:T(8,128)(2,1)S(1)}, bf16[192,768]{1,0:T(8,128)(2,1)S(1)}, u32[]{:S(2)}, u32[]{:S(2)}) %collective-permute-start.15) | collective-permute-done | bytes 294944 | tf_op jit(solution)/shard_map/ppermute | solution.py:372
  104.1 1.2 fusion.19
  105.9 1.5 %collective-permute-start.16 = (bf16[96,768]{1,0:T(8,128)(2,1)}, bf16[96,768]{1,0:T(8,128)(2,1)S(1)}, u32[]{:S(2)}, u32[]{:S(2)}) collective-permute-start(bf16[96,768]{1,0:T(8,128)(2,1)} %get-tuple-element.122), channel_id=1, source_target_pairs={{0,4},{4,0},{8,12},{12,8},{16,20},{20,16},{24,28},{28,24},{1,5},{5... | collective-permute-start | bytes 442376 | tf_op jit(solution)/shard_map/ppermute | solution.py:471
  107.9 3.0 %collective-permute-start.28 = (bf16[2,192,128]{2,1,0:T(8,128)(2,1)}, bf16[2,192,128]{2,1,0:T(8,128)(2,1)S(1)}, u32[]{:S(2)}, u32[]{:S(2)}) collective-permute-start(bf16[2,192,128]{2,1,0:T(8,128)(2,1)} %get-tuple-element.52), channel_id=1, source_target_pairs={{0,24},{4,28},{8,0},{12,4},{16,8},{20,12},{24,16},{28,20},{1,25},{... | collective-permute-start | bytes 294920 | tf_op jit(solution)/shard_map/ppermute | solution.py:409
  112.6 1.1 fusion.14
  114.3 3.2 %shard_map.115 = bf16[32,1536]{1,0:T(8,128)(2,1)S(1)} custom-call(s32[9]{0:T(128)S(1)} %pad_add_fusion.odd_ref, bf16[96,768]{1,0:T(8,128)(2,1)S(1)} %get-tuple-element.123.mine_ref, bf16[96,768]{1,0:T(8,128)(2,1)S(1)} %collective-permute-done.16.other_ref, f32[3,96,1]{2,1,0:T(8,128)S(1)} %squeeze.108.taps_ref, ...), custom_call_target="tpu_custom_call" | custom-call | flops 1000000000 | bytes 4000000 | tf_op jit(solution)/shard_map/pallas_call | solution.py:262
  117.5 2.9 %collective-permute-start.24 = (bf16[32,1536]{1,0:T(8,128)(2,1)S(1)}, bf16[32,1536]{1,0:T(8,128)(2,1)S(1)}, u32[]{:S(2)}, u32[]{:S(2)}) collective-permute-start(bf16[32,1536]{1,0:T(8,128)(2,1)S(1)} %shard_map.115), channel_id=1, source_target_pairs={{0,8},{4,12},{8,16},{12,20},{16,24},{20,28},{24,0},{28,4},{1,9},{5... | collective-permute-start | bytes 294920 | tf_op jit(solution)/shard_map/ppermute | solution.py:501
  121.3 1.5 %collective-permute-start.26 = (bf16[32,1536]{1,0:T(8,128)(2,1)S(1)}, bf16[32,1536]{1,0:T(8,128)(2,1)S(1)}, u32[]{:S(2)}, u32[]{:S(2)}) collective-permute-start(bf16[32,1536]{1,0:T(8,128)(2,1)S(1)} %shard_map.115), channel_id=1, source_target_pairs={{0,24},{4,28},{8,0},{12,4},{16,8},{20,12},{24,16},{28,20},{1,25},{... | collective-permute-start | bytes 294920 | tf_op jit(solution)/shard_map/ppermute | solution.py:501
  122.9 1.6 %collective-permute-start.31 = (bf16[4,192,128]{2,1,0:T(8,128)(2,1)S(1)}, bf16[4,192,128]{2,1,0:T(8,128)(2,1)S(1)}, u32[]{:S(2)}, u32[]{:S(2)}) collective-permute-start(bf16[4,192,128]{2,1,0:T(8,128)(2,1)S(1)} %dynamic-slice_bitcast_fusion.1), channel_id=1, source_target_pairs={{0,4},{4,0},{8,12},{12,8},{16,20},{20,16},{24,28},{28,24},{1,5},{5... | collective-permute-start | bytes 589832 | tf_op jit(solution)/shard_map/ppermute | solution.py:448
  124.5 3.2 %shard_map.116 = bf16[32,1536]{1,0:T(8,128)(2,1)S(1)} custom-call(s32[9]{0:T(128)S(1)} %pad_add_fusion.odd_ref, bf16[96,768]{1,0:T(8,128)(2,1)S(1)} %get-tuple-element.120.mine_ref, bf16[96,768]{1,0:T(8,128)(2,1)S(1)} %collective-permute-done.23.other_ref, f32[3,96,1]{2,1,0:T(8,128)S(1)} %squeeze.109.taps_ref, ...), custom_call_target="tpu_custom_call" | custom-call | flops 1000000000 | bytes 4000000 | tf_op jit(solution)/shard_map/pallas_call | solution.py:262
  128.3 2.0 %collective-permute-start.33 = (bf16[32,1536]{1,0:T(8,128)(2,1)S(1)}, bf16[32,1536]{1,0:T(8,128)(2,1)S(1)}, u32[]{:S(2)}, u32[]{:S(2)}) collective-permute-start(bf16[32,1536]{1,0:T(8,128)(2,1)S(1)} %shard_map.116), channel_id=1, source_target_pairs={{0,16},{4,20},{8,24},{12,28},{16,0},{20,4},{24,8},{28,12},{1,17},{... | collective-permute-start | bytes 294920 | tf_op jit(solution)/shard_map/ppermute | solution.py:501
  130.3 1.4 collective-permute-start.34
  132.5 2.1 %collective-permute-start.36 = (bf16[1536,128]{1,0:T(8,128)(2,1)S(1)}, bf16[1536,128]{1,0:T(8,128)(2,1)S(1)}, u32[]{:S(2)}, u32[]{:S(2)}) collective-permute-start(bf16[1536,128]{1,0:T(8,128)(2,1)S(1)} %bitcast.233), channel_id=1, source_target_pairs={{0,2},{1,3},{2,0},{3,1},{4,6},{5,7},{6,4},{7,5},{8,10},{9,11},{10,... | collective-permute-start | bytes 1179656 | tf_op jit(solution)/shard_map/ppermute | solution.py:372
  134.6 1.3 collective-permute-done.33
  136.7 4.8 %collective-permute-done.27 = bf16[4,32,1536]{2,1,0:T(8,128)(2,1)S(1)} collective-permute-done((bf16[4,32,1536]{2,1,0:T(8,128)(2,1)S(1)}, bf16[4,32,1536]{2,1,0:T(8,128)(2,1)S(1)}, u32[]{:S(2)}, u32[]{:S(2)}) %collective-permute-start.27) | collective-permute-done | bytes 393248 | tf_op jit(solution)/shard_map/ppermute | solution.py:504
  142.2 3.5 %collective-permute-done.35 = bf16[4,32,1536]{2,1,0:T(8,128)(2,1)S(1)} collective-permute-done((bf16[4,32,1536]{2,1,0:T(8,128)(2,1)S(1)}, bf16[4,32,1536]{2,1,0:T(8,128)(2,1)S(1)}, u32[]{:S(2)}, u32[]{:S(2)}) %collective-permute-start.35) | collective-permute-done | bytes 393248 | tf_op jit(solution)/shard_map/ppermute | solution.py:504
  146.9 1.3 broadcast_select_fusion.1
  148.3 2.0 %fusion = f32[512,512]{1,0:T(8,128)} fusion(bf16[512,1536]{1,0:T(8,128)(2,1)S(1)} %bitcast.226, bf16[1536,128]{1,0:T(8,128)(2,1)S(1)} %get-tuple-element.73, bf16[1536,128]{1,0:T(8,128)(2,1)S(1)} %get-tuple-element.132, bf16[1536,128]{1,0:T(8,128)(2,1)S(1)} %get-tuple-element.72, bf16[1536,128]{1,0:T(8,128)(2,1)S(1)} %get-tuple-element.133), kind=kOutput, calls=%fused_computation | convolution fusion | flops 811597824 | bytes 4194304 | tf_op jit(solution)/shard_map/dot_general | solution.py:514
  (135 shorter events, 23.3 us)
Async XLA Ops:
  0.6 31.3 %copy-start = (f32[3,3,512]{2,1,0:T(4,128)S(1)}, f32[3,3,512]{2,1,0:T(4,128)}, u32[]{:S(2)}) copy-start(f32[3,3,512]{2,1,0:T(4,128)} %param.12) | copy-start | bytes 55300
  0.6 25.8 %collective-permute-start.3 = (bf16[192,1024]{1,0:T(8,128)(2,1)}, bf16[192,1024]{1,0:T(8,128)(2,1)}, u32[]{:S(2)}, u32[]{:S(2)}) collective-permute-start(bf16[192,1024]{1,0:T(8,128)(2,1)} %param.10), channel_id=1, source_target_pairs={{0,8},{4,12},{8,16},{12,20},{16,24},{20,28},{1,9},{5,13},{9,17},{1... | collective-permute-start | bytes 1179656 | tf_op jit(solution)/shard_map/ppermute | solution.py:374
  6.3 18.8 %collective-permute-start.4 = (bf16[192,1024]{1,0:T(8,128)(2,1)}, bf16[192,1024]{1,0:T(8,128)(2,1)}, u32[]{:S(2)}, u32[]{:S(2)}) collective-permute-start(bf16[192,1024]{1,0:T(8,128)(2,1)} %param.10), channel_id=1, source_target_pairs={{8,0},{12,4},{16,8},{20,12},{24,16},{28,20},{9,1},{13,5},{17,9},{2... | collective-permute-start | bytes 1179656 | tf_op jit(solution)/shard_map/ppermute | solution.py:375
  9.0 10.4 %copy-start.2 = (bf16[192,4096]{1,0:T(8,128)(2,1)S(1)}, bf16[192,4096]{1,0:T(8,128)(2,1)}, u32[]{:S(2)}) copy-start(bf16[192,4096]{1,0:T(8,128)(2,1)} %grad_ref.1) | copy-start | bytes 4718596
  9.0 10.4 %copy-start.3 = (f32[2,192,512]{2,1,0:T(8,128)S(1)}, f32[2,192,512]{2,1,0:T(8,128)}, u32[]{:S(2)}) copy-start(f32[2,192,512]{2,1,0:T(8,128)} %value_ref.1) | copy-start | bytes 2359300
  10.6 21.5 %collective-permute-start = (bf16[384,512]{1,0:T(8,128)(2,1)}, bf16[384,512]{1,0:T(8,128)(2,1)}, u32[]{:S(2)}, u32[]{:S(2)}) collective-permute-start(bf16[384,512]{1,0:T(8,128)(2,1)} %get-tuple-element.32), channel_id=1, source_target_pairs={{0,0},{1,8},{2,16},{3,24},{4,4},{5,12},{6,20},{7,28},{8,1},{9,9},{... | collective-permute-start | bytes 1179656 | tf_op jit(solution)/shard_map/ppermute | solution.py:387
  15.1 19.1 %collective-permute-start.1 = (bf16[384,512]{1,0:T(8,128)(2,1)}, bf16[384,512]{1,0:T(8,128)(2,1)}, u32[]{:S(2)}, u32[]{:S(2)}) collective-permute-start(bf16[384,512]{1,0:T(8,128)(2,1)} %get-tuple-element.33), channel_id=1, source_target_pairs={{0,8},{1,16},{2,24},{3,0},{4,12},{5,20},{6,28},{7,4},{8,9},{9,17},... | collective-permute-start | bytes 1179656 | tf_op jit(solution)/shard_map/ppermute | solution.py:387
  15.3 21.6 %collective-permute-start.2 = (bf16[384,512]{1,0:T(8,128)(2,1)S(1)}, bf16[384,512]{1,0:T(8,128)(2,1)}, u32[]{:S(2)}, u32[]{:S(2)}) collective-permute-start(bf16[384,512]{1,0:T(8,128)(2,1)S(1)} %get-tuple-element.34), channel_id=1, source_target_pairs={{0,16},{1,24},{2,0},{3,8},{4,20},{5,28},{6,4},{7,12},{8,17},{9,25}... | collective-permute-start | bytes 1179656 | tf_op jit(solution)/shard_map/ppermute | solution.py:387
  25.1 16.5 %collective-permute-start.10 = (bf16[192,1024]{1,0:T(8,128)(2,1)}, bf16[192,1024]{1,0:T(8,128)(2,1)}, u32[]{:S(2)}, u32[]{:S(2)}) collective-permute-start(bf16[192,1024]{1,0:T(8,128)(2,1)} %collective-permute-done.4), channel_id=1, source_target_pairs={{8,0},{12,4},{16,8},{20,12},{24,16},{28,20},{9,1},{13,5},{17,9},{2... | collective-permute-start | bytes 1179656 | tf_op jit(solution)/shard_map/ppermute | solution.py:394
  26.4 16.8 %collective-permute-start.12 = (bf16[192,1024]{1,0:T(8,128)(2,1)}, bf16[192,1024]{1,0:T(8,128)(2,1)}, u32[]{:S(2)}, u32[]{:S(2)}) collective-permute-start(bf16[192,1024]{1,0:T(8,128)(2,1)} %collective-permute-done.3), channel_id=1, source_target_pairs={{0,8},{4,12},{8,16},{12,20},{16,24},{20,28},{1,9},{5,13},{9,17},{1... | collective-permute-start | bytes 1179656 | tf_op jit(solution)/shard_map/ppermute | solution.py:393
  32.2 17.5 %collective-permute-start.5 = (bf16[384,512]{1,0:T(8,128)(2,1)S(1)}, bf16[384,512]{1,0:T(8,128)(2,1)S(1)}, u32[]{:S(2)}, u32[]{:S(2)}) collective-permute-start(bf16[384,512]{1,0:T(8,128)(2,1)S(1)} %get-tuple-element.36), channel_id=1, source_target_pairs={{0,24},{1,0},{2,8},{3,16},{4,28},{5,4},{6,12},{7,20},{8,25},{9,1},... | collective-permute-start | bytes 1179656 | tf_op jit(solution)/shard_map/ppermute | solution.py:387
  34.2 34.4 %collective-permute-start.6 = (bf16[384,512]{1,0:T(8,128)(2,1)}, bf16[384,512]{1,0:T(8,128)(2,1)S(1)}, u32[]{:S(2)}, u32[]{:S(2)}) collective-permute-start(bf16[384,512]{1,0:T(8,128)(2,1)} %collective-permute-done), channel_id=1, source_target_pairs={{0,4},{4,0},{8,12},{12,8},{16,20},{20,16},{24,28},{28,24},{1,5},{5... | collective-permute-start | bytes 1179656 | tf_op jit(solution)/shard_map/ppermute | solution.py:388
  36.9 31.8 %collective-permute-start.7 = (bf16[384,512]{1,0:T(8,128)(2,1)}, bf16[384,512]{1,0:T(8,128)(2,1)S(1)}, u32[]{:S(2)}, u32[]{:S(2)}) collective-permute-start(bf16[384,512]{1,0:T(8,128)(2,1)} %collective-permute-done.1), channel_id=1, source_target_pairs={{0,4},{4,0},{8,12},{12,8},{16,20},{20,16},{24,28},{28,24},{1,5},{5... | collective-permute-start | bytes 1179656 | tf_op jit(solution)/shard_map/ppermute | solution.py:388
  41.7 27.7 %collective-permute-start.8 = (bf16[384,512]{1,0:T(8,128)(2,1)}, bf16[384,512]{1,0:T(8,128)(2,1)S(1)}, u32[]{:S(2)}, u32[]{:S(2)}) collective-permute-start(bf16[384,512]{1,0:T(8,128)(2,1)} %collective-permute-done.2), channel_id=1, source_target_pairs={{0,4},{4,0},{8,12},{12,8},{16,20},{20,16},{24,28},{28,24},{1,5},{5... | collective-permute-start | bytes 1179656 | tf_op jit(solution)/shard_map/ppermute | solution.py:388
  43.2 28.3 %collective-permute-start.11 = (bf16[192,1024]{1,0:T(8,128)(2,1)}, bf16[192,1024]{1,0:T(8,128)(2,1)S(1)}, u32[]{:S(2)}, u32[]{:S(2)}) collective-permute-start(bf16[192,1024]{1,0:T(8,128)(2,1)} %collective-permute-done.10), channel_id=1, source_target_pairs={{8,0},{12,4},{16,8},{20,12},{24,16},{28,20},{9,1},{13,5},{17,9},{2... | collective-permute-start | bytes 1179656 | tf_op jit(solution)/shard_map/ppermute | solution.py:396
  49.6 24.5 %collective-permute-start.13 = (bf16[192,1024]{1,0:T(8,128)(2,1)}, bf16[192,1024]{1,0:T(8,128)(2,1)S(1)}, u32[]{:S(2)}, u32[]{:S(2)}) collective-permute-start(bf16[192,1024]{1,0:T(8,128)(2,1)} %collective-permute-done.12), channel_id=1, source_target_pairs={{0,8},{4,12},{8,16},{12,20},{16,24},{20,28},{1,9},{5,13},{9,17},{1... | collective-permute-start | bytes 1179656 | tf_op jit(solution)/shard_map/ppermute | solution.py:395
  68.8 7.8 %collective-permute-start.9 = (bf16[384,512]{1,0:T(8,128)(2,1)S(1)}, bf16[384,512]{1,0:T(8,128)(2,1)S(1)}, u32[]{:S(2)}, u32[]{:S(2)}) collective-permute-start(bf16[384,512]{1,0:T(8,128)(2,1)S(1)} %collective-permute-done.5), channel_id=1, source_target_pairs={{0,4},{4,0},{8,12},{12,8},{16,20},{20,16},{24,28},{28,24},{1,5},{5... | collective-permute-start | bytes 1179656 | tf_op jit(solution)/shard_map/ppermute | solution.py:388
  78.9 2.4 %copy-start.12 = (bf16[2,192,128]{2,1,0:T(8,128)(2,1)S(1)}, bf16[2,192,128]{2,1,0:T(8,128)(2,1)}, u32[]{:S(2)}) copy-start(bf16[2,192,128]{2,1,0:T(8,128)(2,1)} %get-tuple-element.40) | copy-start | bytes 294916
  78.9 5.7 %copy-start.11 = (bf16[2,192,128]{2,1,0:T(8,128)(2,1)S(1)}, bf16[2,192,128]{2,1,0:T(8,128)(2,1)}, u32[]{:S(2)}) copy-start(bf16[2,192,128]{2,1,0:T(8,128)(2,1)} %get-tuple-element.42) | copy-start | bytes 294916
  78.9 8.8 %copy-start.10 = (bf16[2,192,128]{2,1,0:T(8,128)(2,1)S(1)}, bf16[2,192,128]{2,1,0:T(8,128)(2,1)}, u32[]{:S(2)}) copy-start(bf16[2,192,128]{2,1,0:T(8,128)(2,1)} %get-tuple-element.44) | copy-start | bytes 294916
  78.9 14.0 %collective-permute-start.14 = (f32[2,192,768]{2,1,0:T(8,128)}, f32[2,192,768]{2,1,0:T(8,128)}, u32[]{:S(2)}, u32[]{:S(2)}) collective-permute-start(f32[2,192,768]{2,1,0:T(8,128)} %fusion.9), channel_id=1, source_target_pairs={{0,1},{1,0},{2,3},{3,2},{4,5},{5,4},{6,7},{7,6},{8,9},{9,8},{10,11... | collective-permute-start | bytes 3538952 | tf_op jit(solution)/shard_map/ppermute | solution.py:372
  80.8 14.5 %collective-permute-start.21 = (f32[2,192,768]{2,1,0:T(8,128)}, f32[2,192,768]{2,1,0:T(8,128)S(1)}, u32[]{:S(2)}, u32[]{:S(2)}) collective-permute-start(f32[2,192,768]{2,1,0:T(8,128)} %fusion.8), channel_id=1, source_target_pairs={{0,1},{1,0},{2,3},{3,2},{4,5},{5,4},{6,7},{7,6},{8,9},{9,8},{10,11... | collective-permute-start | bytes 3538952 | tf_op jit(solution)/shard_map/ppermute | solution.py:372
  81.4 15.6 %collective-permute-start.17 = (bf16[2,192,128]{2,1,0:T(8,128)(2,1)S(1)}, bf16[2,192,128]{2,1,0:T(8,128)(2,1)S(1)}, u32[]{:S(2)}, u32[]{:S(2)}) collective-permute-start(bf16[2,192,128]{2,1,0:T(8,128)(2,1)S(1)} %copy-done.12), channel_id=1, source_target_pairs={{0,24},{4,28},{8,0},{12,4},{16,8},{20,12},{24,16},{28,20},{1,25},{... | collective-permute-start | bytes 294920 | tf_op jit(solution)/shard_map/ppermute | solution.py:409
  84.7 12.3 %collective-permute-start.18 = (bf16[2,192,128]{2,1,0:T(8,128)(2,1)S(1)}, bf16[2,192,128]{2,1,0:T(8,128)(2,1)S(1)}, u32[]{:S(2)}, u32[]{:S(2)}) collective-permute-start(bf16[2,192,128]{2,1,0:T(8,128)(2,1)S(1)} %copy-done.11), channel_id=1, source_target_pairs={{0,16},{4,20},{8,24},{12,28},{16,0},{20,4},{24,8},{28,12},{1,17},{... | collective-permute-start | bytes 294920 | tf_op jit(solution)/shard_map/ppermute | solution.py:409
  87.8 9.2 %collective-permute-start.19 = (bf16[2,192,128]{2,1,0:T(8,128)(2,1)S(1)}, bf16[2,192,128]{2,1,0:T(8,128)(2,1)S(1)}, u32[]{:S(2)}, u32[]{:S(2)}) collective-permute-start(bf16[2,192,128]{2,1,0:T(8,128)(2,1)S(1)} %copy-done.10), channel_id=1, source_target_pairs={{0,8},{4,12},{8,16},{12,20},{16,24},{20,28},{24,0},{28,4},{1,9},{5... | collective-permute-start | bytes 294920 | tf_op jit(solution)/shard_map/ppermute | solution.py:409
  92.1 3.3 %copy-start.8 = (f32[384,768]{1,0:T(8,128)}, f32[384,768]{1,0:T(8,128)S(1)}, u32[]{:S(2)}) copy-start(f32[384,768]{1,0:T(8,128)S(1)} %fusion.57) | copy-start | bytes 3538948
  94.1 10.0 %collective-permute-start.15 = (bf16[192,768]{1,0:T(8,128)(2,1)S(1)}, bf16[192,768]{1,0:T(8,128)(2,1)S(1)}, u32[]{:S(2)}, u32[]{:S(2)}) collective-permute-start(bf16[192,768]{1,0:T(8,128)(2,1)S(1)} %fusion.16), channel_id=1, source_target_pairs={{0,2},{1,3},{2,0},{3,1},{4,6},{5,7},{6,4},{7,5},{8,10},{9,11},{10,... | collective-permute-start | bytes 884744 | tf_op jit(solution)/shard_map/ppermute | solution.py:372
  96.1 16.5 %collective-permute-start.22 = (bf16[192,768]{1,0:T(8,128)(2,1)}, bf16[192,768]{1,0:T(8,128)(2,1)}, u32[]{:S(2)}, u32[]{:S(2)}) collective-permute-start(bf16[192,768]{1,0:T(8,128)(2,1)} %fusion.11), channel_id=1, source_target_pairs={{0,2},{1,3},{2,0},{3,1},{4,6},{5,7},{6,4},{7,5},{8,10},{9,11},{10,... | collective-permute-start | bytes 884744 | tf_op jit(solution)/shard_map/ppermute | solution.py:372
  97.8 14.8 %copy-start.9 = (f32[384,768]{1,0:T(8,128)S(1)}, f32[384,768]{1,0:T(8,128)}, u32[]{:S(2)}) copy-start(f32[384,768]{1,0:T(8,128)} %copy-done.8) | copy-start | bytes 3538948
  97.8 13.2 %collective-permute-start.20 = (bf16[4,192,128]{2,1,0:T(8,128)(2,1)}, bf16[4,192,128]{2,1,0:T(8,128)(2,1)}, u32[]{:S(2)}, u32[]{:S(2)}) collective-permute-start(bf16[4,192,128]{2,1,0:T(8,128)(2,1)} %get-tuple-element.106), channel_id=1, source_target_pairs={{0,4},{4,0},{8,12},{12,8},{16,20},{20,16},{24,28},{28,24},{1,5},{5... | collective-permute-start | bytes 589832 | tf_op jit(solution)/shard_map/ppermute | solution.py:448
  105.9 6.7 %collective-permute-start.16 = (bf16[96,768]{1,0:T(8,128)(2,1)}, bf16[96,768]{1,0:T(8,128)(2,1)S(1)}, u32[]{:S(2)}, u32[]{:S(2)}) collective-permute-start(bf16[96,768]{1,0:T(8,128)(2,1)} %get-tuple-element.122), channel_id=1, source_target_pairs={{0,4},{4,0},{8,12},{12,8},{16,20},{20,16},{24,28},{28,24},{1,5},{5... | collective-permute-start | bytes 442376 | tf_op jit(solution)/shard_map/ppermute | solution.py:471
  107.9 12.5 %collective-permute-start.28 = (bf16[2,192,128]{2,1,0:T(8,128)(2,1)}, bf16[2,192,128]{2,1,0:T(8,128)(2,1)S(1)}, u32[]{:S(2)}, u32[]{:S(2)}) collective-permute-start(bf16[2,192,128]{2,1,0:T(8,128)(2,1)} %get-tuple-element.52), channel_id=1, source_target_pairs={{0,24},{4,28},{8,0},{12,4},{16,8},{20,12},{24,16},{28,20},{1,25},{... | collective-permute-start | bytes 294920 | tf_op jit(solution)/shard_map/ppermute | solution.py:409
  110.9 10.4 %collective-permute-start.29 = (bf16[2,192,128]{2,1,0:T(8,128)(2,1)}, bf16[2,192,128]{2,1,0:T(8,128)(2,1)S(1)}, u32[]{:S(2)}, u32[]{:S(2)}) collective-permute-start(bf16[2,192,128]{2,1,0:T(8,128)(2,1)} %get-tuple-element.54), channel_id=1, source_target_pairs={{0,16},{4,20},{8,24},{12,28},{16,0},{20,4},{24,8},{28,12},{1,17},{... | collective-permute-start | bytes 294920 | tf_op jit(solution)/shard_map/ppermute | solution.py:409
  110.9 11.9 %collective-permute-start.30 = (bf16[2,192,128]{2,1,0:T(8,128)(2,1)S(1)}, bf16[2,192,128]{2,1,0:T(8,128)(2,1)S(1)}, u32[]{:S(2)}, u32[]{:S(2)}) collective-permute-start(bf16[2,192,128]{2,1,0:T(8,128)(2,1)S(1)} %get-tuple-element.56), channel_id=1, source_target_pairs={{0,8},{4,12},{8,16},{12,20},{16,24},{20,28},{24,0},{28,4},{1,9},{5... | collective-permute-start | bytes 294920 | tf_op jit(solution)/shard_map/ppermute | solution.py:409
  111.6 2.7 %copy-start.4 = (f32[192,512]{1,0:T(8,128)S(1)}, f32[192,512]{1,0:T(8,128)}, u32[]{:S(2)}) copy-start(f32[192,512]{1,0:T(8,128)} %constant.269.clone.table_ref) | copy-start | bytes 1179652
  111.6 2.7 %copy-start.5 = (f32[2,5,192]{2,1,0:T(8,128)S(1)}, f32[2,5,192]{2,1,0:T(8,128)}, u32[]{:S(2)}) copy-start(f32[2,5,192]{2,1,0:T(8,128)} %constant.270.clone.turn_ref) | copy-start | bytes 23044
  113.7 10.8 %collective-permute-start.23 = (bf16[96,768]{1,0:T(8,128)(2,1)S(1)}, bf16[96,768]{1,0:T(8,128)(2,1)S(1)}, u32[]{:S(2)}, u32[]{:S(2)}) collective-permute-start(bf16[96,768]{1,0:T(8,128)(2,1)S(1)} %get-tuple-element.121), channel_id=1, source_target_pairs={{0,4},{4,0},{8,12},{12,8},{16,20},{20,16},{24,28},{28,24},{1,5},{5... | collective-permute-start | bytes 442376 | tf_op jit(solution)/shard_map/ppermute | solution.py:471
  117.5 10.8 %collective-permute-start.24 = (bf16[32,1536]{1,0:T(8,128)(2,1)S(1)}, bf16[32,1536]{1,0:T(8,128)(2,1)S(1)}, u32[]{:S(2)}, u32[]{:S(2)}) collective-permute-start(bf16[32,1536]{1,0:T(8,128)(2,1)S(1)} %shard_map.115), channel_id=1, source_target_pairs={{0,8},{4,12},{8,16},{12,20},{16,24},{20,28},{24,0},{28,4},{1,9},{5... | collective-permute-start | bytes 294920 | tf_op jit(solution)/shard_map/ppermute | solution.py:501
  120.4 9.9 %collective-permute-start.25 = (bf16[32,1536]{1,0:T(8,128)(2,1)S(1)}, bf16[32,1536]{1,0:T(8,128)(2,1)S(1)}, u32[]{:S(2)}, u32[]{:S(2)}) collective-permute-start(bf16[32,1536]{1,0:T(8,128)(2,1)S(1)} %shard_map.115), channel_id=1, source_target_pairs={{0,16},{4,20},{8,24},{12,28},{16,0},{20,4},{24,8},{28,12},{1,17},{... | collective-permute-start | bytes 294920 | tf_op jit(solution)/shard_map/ppermute | solution.py:501
  121.3 10.4 %collective-permute-start.26 = (bf16[32,1536]{1,0:T(8,128)(2,1)S(1)}, bf16[32,1536]{1,0:T(8,128)(2,1)S(1)}, u32[]{:S(2)}, u32[]{:S(2)}) collective-permute-start(bf16[32,1536]{1,0:T(8,128)(2,1)S(1)} %shard_map.115), channel_id=1, source_target_pairs={{0,24},{4,28},{8,0},{12,4},{16,8},{20,12},{24,16},{28,20},{1,25},{... | collective-permute-start | bytes 294920 | tf_op jit(solution)/shard_map/ppermute | solution.py:501
  122.9 9.4 %collective-permute-start.31 = (bf16[4,192,128]{2,1,0:T(8,128)(2,1)S(1)}, bf16[4,192,128]{2,1,0:T(8,128)(2,1)S(1)}, u32[]{:S(2)}, u32[]{:S(2)}) collective-permute-start(bf16[4,192,128]{2,1,0:T(8,128)(2,1)S(1)} %dynamic-slice_bitcast_fusion.1), channel_id=1, source_target_pairs={{0,4},{4,0},{8,12},{12,8},{16,20},{20,16},{24,28},{28,24},{1,5},{5... | collective-permute-start | bytes 589832 | tf_op jit(solution)/shard_map/ppermute | solution.py:448
  127.7 6.9 %collective-permute-start.32 = (bf16[32,1536]{1,0:T(8,128)(2,1)S(1)}, bf16[32,1536]{1,0:T(8,128)(2,1)S(1)}, u32[]{:S(2)}, u32[]{:S(2)}) collective-permute-start(bf16[32,1536]{1,0:T(8,128)(2,1)S(1)} %shard_map.116), channel_id=1, source_target_pairs={{0,8},{4,12},{8,16},{12,20},{16,24},{20,28},{24,0},{28,4},{1,9},{5... | collective-permute-start | bytes 294920 | tf_op jit(solution)/shard_map/ppermute | solution.py:501
  128.3 7.6 %collective-permute-start.33 = (bf16[32,1536]{1,0:T(8,128)(2,1)S(1)}, bf16[32,1536]{1,0:T(8,128)(2,1)S(1)}, u32[]{:S(2)}, u32[]{:S(2)}) collective-permute-start(bf16[32,1536]{1,0:T(8,128)(2,1)S(1)} %shard_map.116), channel_id=1, source_target_pairs={{0,16},{4,20},{8,24},{12,28},{16,0},{20,4},{24,8},{28,12},{1,17},{... | collective-permute-start | bytes 294920 | tf_op jit(solution)/shard_map/ppermute | solution.py:501
  130.3 5.6 %collective-permute-start.34 = (bf16[32,1536]{1,0:T(8,128)(2,1)S(1)}, bf16[32,1536]{1,0:T(8,128)(2,1)S(1)}, u32[]{:S(2)}, u32[]{:S(2)}) collective-permute-start(bf16[32,1536]{1,0:T(8,128)(2,1)S(1)} %shard_map.116), channel_id=1, source_target_pairs={{0,24},{4,28},{8,0},{12,4},{16,8},{20,12},{24,16},{28,20},{1,25},{... | collective-permute-start | bytes 294920 | tf_op jit(solution)/shard_map/ppermute | solution.py:501
  131.7 9.7 %collective-permute-start.27 = (bf16[4,32,1536]{2,1,0:T(8,128)(2,1)S(1)}, bf16[4,32,1536]{2,1,0:T(8,128)(2,1)S(1)}, u32[]{:S(2)}, u32[]{:S(2)}) collective-permute-start(bf16[4,32,1536]{2,1,0:T(8,128)(2,1)S(1)} %pad_maximum_fusion.2), channel_id=1, source_target_pairs={{0,4},{4,0},{8,12},{12,8},{16,20},{20,16},{24,28},{28,24},{1,5},{5... | collective-permute-start | bytes 1179656 | tf_op jit(solution)/shard_map/ppermute | solution.py:504
  132.5 9.3 %collective-permute-start.36 = (bf16[1536,128]{1,0:T(8,128)(2,1)S(1)}, bf16[1536,128]{1,0:T(8,128)(2,1)S(1)}, u32[]{:S(2)}, u32[]{:S(2)}) collective-permute-start(bf16[1536,128]{1,0:T(8,128)(2,1)S(1)} %bitcast.233), channel_id=1, source_target_pairs={{0,2},{1,3},{2,0},{3,1},{4,6},{5,7},{6,4},{7,5},{8,10},{9,11},{10,... | collective-permute-start | bytes 1179656 | tf_op jit(solution)/shard_map/ppermute | solution.py:372
  135.9 9.7 %collective-permute-start.35 = (bf16[4,32,1536]{2,1,0:T(8,128)(2,1)S(1)}, bf16[4,32,1536]{2,1,0:T(8,128)(2,1)S(1)}, u32[]{:S(2)}, u32[]{:S(2)}) collective-permute-start(bf16[4,32,1536]{2,1,0:T(8,128)(2,1)S(1)} %pad_maximum_fusion.4), channel_id=1, source_target_pairs={{0,4},{4,0},{8,12},{12,8},{16,20},{20,16},{24,28},{28,24},{1,5},{5... | collective-permute-start | bytes 1179656 | tf_op jit(solution)/shard_map/ppermute | solution.py:504
  142.1 4.8 %collective-permute-start.37 = (bf16[2,1536,128]{2,1,0:T(8,128)(2,1)S(1)}, bf16[2,1536,128]{2,1,0:T(8,128)(2,1)}, u32[]{:S(2)}, u32[]{:S(2)}) collective-permute-start(bf16[2,1536,128]{2,1,0:T(8,128)(2,1)S(1)} %pad_maximum_fusion), channel_id=1, source_target_pairs={{0,1},{1,0},{2,3},{3,2},{4,5},{5,4},{6,7},{7,6},{8,9},{9,8},{10,11... | collective-permute-start | bytes 2359304 | tf_op jit(solution)/shard_map/ppermute | solution.py:372
  (5 other events, 7.4 us)

commit v6 on v5

--- a/solution.py
+++ b/solution.py
@@ -410,7 +410,6 @@
             found.append(piece)
         return found
 
-    filters = along(packed[:, 0], up2, down2)
 
     whole = jnp.zeros((pairs, rows, depth), features.dtype)
     for shift, value in enumerate([features] + behind):
@@ -458,6 +457,7 @@
     gots = [trade(send, 0) for send in sends]
     onwards = [(keep[1] + got[1]).astype(jnp.bfloat16) for keep, got in zip(keeps, gots)]
     across = [trade(onward, 1) for onward in onwards]
+    filters = along(packed[:, 0], *keeps)
     mine, other = beside(filters, onwards[0])
     response = jnp.concatenate([mine, other]).reshape(n, rows // own, own, -1)
     gated = []

time: 151 us -> 150 us (level)
    ppermute x6, waiting for transfers between devices: 0.05 us -> 2.79 us  [along(): piece = lax.ppermute(after(piece, *others), 'ctx', back)]
    ppermute x6, waiting for transfers between devices: 4.81 us -> 2.22 us  [trade(): return lax.ppermute(value, 'ch', [(j, j ^ 1 << bit) for j in range(m)])]
  transfers between devices with their start and end apart: 38 -> 38, of which waited for: 9 -> 10; matrix products, arithmetic and copies ran while one was open for 18% -> 17% of each run, Pallas kernels for 6% -> 6%
where the time goes in v6:
time: 150 us; the launch traced here: 149 us
  starting transfers between devices  78.5 us (52%)
  waiting for transfers between devices  28 us (19%)
  local copies, waits for them, and re-layouts  14.1 us (9%)
  other arithmetic  10.7 us (7%)
  Pallas kernels  8.91 us (6%)
  matrix products  7.46 us (5%)
    ppermute x1, starting transfers between devices, special(): up3 = lax.ppermute(after(up2, packed), 'ctx', up)  18.9 us
    ppermute x6, starting transfers between devices, along(): piece = lax.ppermute(after(piece, *others), 'ctx', back)  12 us
    ppermute x6, starting transfers between devices, special(): lax.ppermute(gated[part], 'ctx', shifts[s])  8.86 us
    ppermute x2, waiting for transfers between devices, special(): other = lax.ppermute(near, 'ctx', flips)  8.38 us
    ppermute x4, starting transfers between devices, special(): pieces.append(lax.ppermute(piece, BOTH, hops))  8.36 us
    pallas_call x2, Pallas kernels, convolve(): pl.pallas_call(convolve_kernel, out_shape=jax.ShapeDtypeStruct((own, tota...  6.36 us
    ppermute x1, starting transfers between devices, special(): up1 = lax.ppermute(features, 'ctx', up)  5.7 us
    dot_general x4, matrix products, multiply(): lax.dot_general(left, whole, (((1,), (1,)), ((), ())), preferred_element_...  5.45 us
  transfers between devices with their start and end apart: 38, of which 10 were waited for; matrix products, arithmetic and copies ran while one was open for 17% of the time, Pallas kernels for 6%

profile of v6, /device:TPU:0, one launch (start us, length us, event | category | flops | bytes accessed | tf_op | source)
XLA Modules:
  0.0 149.2 jit_solution(6505238489437141053)
XLA Ops:
  0.6 5.7 %collective-permute-start.3 = (bf16[192,1024]{1,0:T(8,128)(2,1)}, bf16[192,1024]{1,0:T(8,128)(2,1)}, u32[]{:S(2)}, u32[]{:S(2)}) collective-permute-start(bf16[192,1024]{1,0:T(8,128)(2,1)} %param.10), channel_id=1, source_target_pairs={{0,8},{4,12},{8,16},{12,20},{16,24},{20,28},{1,9},{5,13},{9,17},{1... | collective-permute-start | bytes 1179656 | tf_op jit(solution)/shard_map/ppermute | solution.py:374
  6.3 1.3 collective-permute-start.4
  7.7 1.4 copy-done.1
  9.1 1.6 %shard_map.113 = (bf16[384,512]{1,0:T(8,128)(2,1)}, bf16[384,512]{1,0:T(8,128)(2,1)}, bf16[384,512]{1,0:T(8,128)(2,1)S(1)}, bf16[384,512]{1,0:T(8,128)(2,1)S(1)}) custom-call(s32[4]{0:T(128)S(1)} %and_select_fusion.which_ref, bf16[3,512,512]{2,1,0:T(8,128)(2,1)S(1)} %bitcast.222), custom_call_target="tpu_custom_call" | custom-call | bytes 3145728 | tf_op jit(solution)/shard_map/pallas_call | solution.py:332
  10.7 4.5 %collective-permute-start = (bf16[384,512]{1,0:T(8,128)(2,1)}, bf16[384,512]{1,0:T(8,128)(2,1)}, u32[]{:S(2)}, u32[]{:S(2)}) collective-permute-start(bf16[384,512]{1,0:T(8,128)(2,1)} %get-tuple-element.32), channel_id=1, source_target_pairs={{0,0},{1,8},{2,16},{3,24},{4,4},{5,12},{6,20},{7,28},{8,1},{9,9},{... | collective-permute-start | bytes 1179656 | tf_op jit(solution)/shard_map/ppermute | solution.py:387
  15.3 2.4 %collective-permute-start.2 = (bf16[384,512]{1,0:T(8,128)(2,1)S(1)}, bf16[384,512]{1,0:T(8,128)(2,1)}, u32[]{:S(2)}, u32[]{:S(2)}) collective-permute-start(bf16[384,512]{1,0:T(8,128)(2,1)S(1)} %get-tuple-element.34), channel_id=1, source_target_pairs={{0,16},{1,24},{2,0},{3,8},{4,20},{5,28},{6,4},{7,12},{8,17},{9,25}... | collective-permute-start | bytes 1179656 | tf_op jit(solution)/shard_map/ppermute | solution.py:387
  17.7 1.7 %fusion.55 = (bf16[192,512]{1,0:T(8,128)(2,1)S(1)}, bf16[192,512]{1,0:T(8,128)(2,1)}) fusion(bf16[192,1024]{1,0:T(8,128)(2,1)} %param.10), kind=kLoop, calls=%fused_computation.137 | loop fusion | bytes 786432 | tf_op jit(solution)/shard_map/slice | solution.py:419
  22.7 1.8 %dynamic-slice_bitcast_fusion.10 = (bf16[2,192,128]{2,1,0:T(8,128)(2,1)S(1)}, bf16[2,192,128]{2,1,0:T(8,128)(2,1)S(1)}, bf16[2,192,128]{2,1,0:T(8,128)(2,1)}, bf16[2,192,128]{2,1,0:T(8,128)(2,1)}) fusion(bf16[4,2,192,128]{3,2,1,0:T(8,128)(2,1)} %bitcast.234, s32[]{:T(128)S(6)} %select_n.349, s32[]{:T(128)S(6)} %select_n.361, s32[]{:T(128)S(6)} %select_n.357, ...), kind=kLoop, calls=%fused_computation.99 | loop fusion | bytes 786448 | tf_op jit(solution)/shard_map/jit(dynamic_index_in_dim)/squeeze | solution.py:406
  25.2 1.3 collective-permute-start.10
  26.5 4.7 %collective-permute-start.12 = (bf16[192,1024]{1,0:T(8,128)(2,1)}, bf16[192,1024]{1,0:T(8,128)(2,1)S(1)}, u32[]{:S(2)}, u32[]{:S(2)}) collective-permute-start(bf16[192,1024]{1,0:T(8,128)(2,1)} %collective-permute-done.3), channel_id=1, source_target_pairs={{0,8},{4,12},{8,16},{12,20},{16,24},{20,28},{1,9},{5,13},{9,17},{1... | collective-permute-start | bytes 1179656 | tf_op jit(solution)/shard_map/ppermute | solution.py:393
  31.5 1.3 collective-permute-start.5
  34.3 1.6 %collective-permute-start.6 = (bf16[384,512]{1,0:T(8,128)(2,1)}, bf16[384,512]{1,0:T(8,128)(2,1)S(1)}, u32[]{:S(2)}, u32[]{:S(2)}) collective-permute-start(bf16[384,512]{1,0:T(8,128)(2,1)} %collective-permute-done), channel_id=1, source_target_pairs={{0,4},{4,0},{8,12},{12,8},{16,20},{20,16},{24,28},{28,24},{1,5},{5... | collective-permute-start | bytes 1179656 | tf_op jit(solution)/shard_map/ppermute | solution.py:388
  38.5 3.2 %collective-permute-done.10 = bf16[192,1024]{1,0:T(8,128)(2,1)} collective-permute-done((bf16[192,1024]{1,0:T(8,128)(2,1)}, bf16[192,1024]{1,0:T(8,128)(2,1)}, u32[]{:S(2)}, u32[]{:S(2)}) %collective-permute-start.10) | collective-permute-done | bytes 393248 | tf_op jit(solution)/shard_map/ppermute | solution.py:394
  41.7 1.5 %collective-permute-start.8 = (bf16[384,512]{1,0:T(8,128)(2,1)}, bf16[384,512]{1,0:T(8,128)(2,1)S(1)}, u32[]{:S(2)}, u32[]{:S(2)}) collective-permute-start(bf16[384,512]{1,0:T(8,128)(2,1)} %collective-permute-done.2), channel_id=1, source_target_pairs={{0,4},{4,0},{8,12},{12,8},{16,20},{20,16},{24,28},{28,24},{1,5},{5... | collective-permute-start | bytes 1179656 | tf_op jit(solution)/shard_map/ppermute | solution.py:388
  43.3 1.3 collective-permute-start.11
  45.7 4.0 %collective-permute-done.5 = bf16[384,512]{1,0:T(8,128)(2,1)S(1)} collective-permute-done((bf16[384,512]{1,0:T(8,128)(2,1)S(1)}, bf16[384,512]{1,0:T(8,128)(2,1)S(1)}, u32[]{:S(2)}, u32[]{:S(2)}) %collective-permute-start.5) | collective-permute-done | bytes 393248 | tf_op jit(solution)/shard_map/ppermute | solution.py:387
  49.7 18.9 %collective-permute-start.13 = (bf16[192,1024]{1,0:T(8,128)(2,1)S(1)}, bf16[192,1024]{1,0:T(8,128)(2,1)S(1)}, u32[]{:S(2)}, u32[]{:S(2)}) collective-permute-start(bf16[192,1024]{1,0:T(8,128)(2,1)S(1)} %collective-permute-done.12), channel_id=1, source_target_pairs={{0,8},{4,12},{8,16},{12,20},{16,24},{20,28},{1,9},{5,13},{9,17},{1... | collective-permute-start | bytes 1179656 | tf_op jit(solution)/shard_map/ppermute | solution.py:395
  69.4 2.1 %collective-permute-done.11 = bf16[192,1024]{1,0:T(8,128)(2,1)S(1)} collective-permute-done((bf16[192,1024]{1,0:T(8,128)(2,1)}, bf16[192,1024]{1,0:T(8,128)(2,1)S(1)}, u32[]{:S(2)}, u32[]{:S(2)}) %collective-permute-start.11) | collective-permute-done | bytes 393248 | tf_op jit(solution)/shard_map/ppermute | solution.py:396
  71.5 2.3 %collective-permute-done.13 = bf16[192,1024]{1,0:T(8,128)(2,1)S(1)} collective-permute-done((bf16[192,1024]{1,0:T(8,128)(2,1)S(1)}, bf16[192,1024]{1,0:T(8,128)(2,1)S(1)}, u32[]{:S(2)}, u32[]{:S(2)}) %collective-permute-start.13) | collective-permute-done | bytes 393248 | tf_op jit(solution)/shard_map/ppermute | solution.py:395
  74.9 1.7 %collective-permute-done.9 = bf16[384,512]{1,0:T(8,128)(2,1)S(1)} collective-permute-done((bf16[384,512]{1,0:T(8,128)(2,1)S(1)}, bf16[384,512]{1,0:T(8,128)(2,1)S(1)}, u32[]{:S(2)}, u32[]{:S(2)}) %collective-permute-start.9) | collective-permute-done | bytes 393248 | tf_op jit(solution)/shard_map/ppermute | solution.py:388
  77.0 1.8 %fusion.9 = f32[2,192,768]{2,1,0:T(8,128)} fusion(bf16[768,1024,1]{1,0,2:T(8,128)(2,1)S(1)} %bitcast.229, bf16[2,2,2,192,1024]{4,3,2,1,0:T(8,128)(2,1)S(1)} %constant_dynamic-update-slice_fusion), kind=kOutput, calls=%fused_computation.11 | convolution fusion | flops 603979776 | bytes 3538944 | tf_op jit(solution)/shard_map/dot_general | solution.py:438
  78.9 1.9 %fusion.8 = f32[2,192,768]{2,1,0:T(8,128)} fusion(bf16[768,1024,1]{1,0,2:T(8,128)(2,1)S(1)} %bitcast.230, bf16[2,2,2,192,1024]{4,3,2,1,0:T(8,128)(2,1)S(1)} %constant_dynamic-update-slice_fusion), kind=kOutput, calls=%fused_computation.9 | convolution fusion | flops 603979776 | bytes 3538944 | tf_op jit(solution)/shard_map/dot_general | solution.py:438
  81.4 1.5 fusion.46
  84.7 3.1 %collective-permute-start.17 = (bf16[2,192,128]{2,1,0:T(8,128)(2,1)S(1)}, bf16[2,192,128]{2,1,0:T(8,128)(2,1)S(1)}, u32[]{:S(2)}, u32[]{:S(2)}) collective-permute-start(bf16[2,192,128]{2,1,0:T(8,128)(2,1)S(1)} %copy-done.13), channel_id=1, source_target_pairs={{0,24},{4,28},{8,0},{12,4},{16,8},{20,12},{24,16},{28,20},{1,25},{... | collective-permute-start | bytes 294920 | tf_op jit(solution)/shard_map/ppermute | solution.py:409
  87.8 3.3 %collective-permute-start.18 = (bf16[2,192,128]{2,1,0:T(8,128)(2,1)S(1)}, bf16[2,192,128]{2,1,0:T(8,128)(2,1)S(1)}, u32[]{:S(2)}, u32[]{:S(2)}) collective-permute-start(bf16[2,192,128]{2,1,0:T(8,128)(2,1)S(1)} %copy-done.12), channel_id=1, source_target_pairs={{0,16},{4,20},{8,24},{12,28},{16,0},{20,4},{24,8},{28,12},{1,17},{... | collective-permute-start | bytes 294920 | tf_op jit(solution)/shard_map/ppermute | solution.py:409
  91.2 1.9 %collective-permute-start.19 = (bf16[2,192,128]{2,1,0:T(8,128)(2,1)S(1)}, bf16[2,192,128]{2,1,0:T(8,128)(2,1)S(1)}, u32[]{:S(2)}, u32[]{:S(2)}) collective-permute-start(bf16[2,192,128]{2,1,0:T(8,128)(2,1)S(1)} %copy-done.11), channel_id=1, source_target_pairs={{0,8},{4,12},{8,16},{12,20},{16,24},{20,28},{24,0},{28,4},{1,9},{5... | collective-permute-start | bytes 294920 | tf_op jit(solution)/shard_map/ppermute | solution.py:409
  94.2 1.3 collective-permute-start.15
  95.5 1.1 fusion.11
  97.5 2.8 %collective-permute-done.18 = bf16[2,192,128]{2,1,0:T(8,128)(2,1)S(1)} collective-permute-done((bf16[2,192,128]{2,1,0:T(8,128)(2,1)S(1)}, bf16[2,192,128]{2,1,0:T(8,128)(2,1)S(1)}, u32[]{:S(2)}, u32[]{:S(2)}) %collective-permute-start.18) | collective-permute-done | bytes 98336 | tf_op jit(solution)/shard_map/ppermute | solution.py:409
  100.4 1.6 %collective-permute-start.20 = (bf16[4,192,128]{2,1,0:T(8,128)(2,1)S(1)}, bf16[4,192,128]{2,1,0:T(8,128)(2,1)S(1)}, u32[]{:S(2)}, u32[]{:S(2)}) collective-permute-start(bf16[4,192,128]{2,1,0:T(8,128)(2,1)S(1)} %get-tuple-element.106), channel_id=1, source_target_pairs={{0,4},{4,0},{8,12},{12,8},{16,20},{20,16},{24,28},{28,24},{1,5},{5... | collective-permute-start | bytes 589832 | tf_op jit(solution)/shard_map/ppermute | solution.py:447
  102.0 2.2 %collective-permute-done.15 = bf16[192,768]{1,0:T(8,128)(2,1)S(1)} collective-permute-done((bf16[192,768]{1,0:T(8,128)(2,1)S(1)}, bf16[192,768]{1,0:T(8,128)(2,1)S(1)}, u32[]{:S(2)}, u32[]{:S(2)}) %collective-permute-start.15) | collective-permute-done | bytes 294944 | tf_op jit(solution)/shard_map/ppermute | solution.py:372
  104.2 1.2 fusion.19
  105.4 1.6 %collective-permute-start.16 = (bf16[96,768]{1,0:T(8,128)(2,1)S(1)}, bf16[96,768]{1,0:T(8,128)(2,1)S(1)}, u32[]{:S(2)}, u32[]{:S(2)}) collective-permute-start(bf16[96,768]{1,0:T(8,128)(2,1)S(1)} %get-tuple-element.122), channel_id=1, source_target_pairs={{0,4},{4,0},{8,12},{12,8},{16,20},{20,16},{24,28},{28,24},{1,5},{5... | collective-permute-start | bytes 442376 | tf_op jit(solution)/shard_map/ppermute | solution.py:471
  107.4 3.0 %collective-permute-start.28 = (bf16[2,192,128]{2,1,0:T(8,128)(2,1)}, bf16[2,192,128]{2,1,0:T(8,128)(2,1)S(1)}, u32[]{:S(2)}, u32[]{:S(2)}) collective-permute-start(bf16[2,192,128]{2,1,0:T(8,128)(2,1)} %get-tuple-element.52), channel_id=1, source_target_pairs={{0,24},{4,28},{8,0},{12,4},{16,8},{20,12},{24,16},{28,20},{1,25},{... | collective-permute-start | bytes 294920 | tf_op jit(solution)/shard_map/ppermute | solution.py:409
  111.2 1.2 fusion.14
  113.4 3.2 %shard_map.115 = bf16[32,1536]{1,0:T(8,128)(2,1)S(1)} custom-call(s32[9]{0:T(128)S(1)} %pad_add_fusion.odd_ref, bf16[96,768]{1,0:T(8,128)(2,1)S(1)} %get-tuple-element.123.mine_ref, bf16[96,768]{1,0:T(8,128)(2,1)S(1)} %collective-permute-done.16.other_ref, f32[3,96,1]{2,1,0:T(8,128)S(1)} %squeeze.108.taps_ref, ...), custom_call_target="tpu_custom_call" | custom-call | flops 1000000000 | bytes 4000000 | tf_op jit(solution)/shard_map/pallas_call | solution.py:262
  116.6 2.5 %collective-permute-start.24 = (bf16[32,1536]{1,0:T(8,128)(2,1)S(1)}, bf16[32,1536]{1,0:T(8,128)(2,1)S(1)}, u32[]{:S(2)}, u32[]{:S(2)}) collective-permute-start(bf16[32,1536]{1,0:T(8,128)(2,1)S(1)} %shard_map.115), channel_id=1, source_target_pairs={{0,8},{4,12},{8,16},{12,20},{16,24},{20,28},{24,0},{28,4},{1,9},{5... | collective-permute-start | bytes 294920 | tf_op jit(solution)/shard_map/ppermute | solution.py:501
  120.2 1.3 collective-permute-start.26
  121.6 1.6 %collective-permute-start.31 = (bf16[4,192,128]{2,1,0:T(8,128)(2,1)S(1)}, bf16[4,192,128]{2,1,0:T(8,128)(2,1)S(1)}, u32[]{:S(2)}, u32[]{:S(2)}) collective-permute-start(bf16[4,192,128]{2,1,0:T(8,128)(2,1)S(1)} %dynamic-slice_bitcast_fusion.1), channel_id=1, source_target_pairs={{0,4},{4,0},{8,12},{12,8},{16,20},{20,16},{24,28},{28,24},{1,5},{5... | collective-permute-start | bytes 589832 | tf_op jit(solution)/shard_map/ppermute | solution.py:447
  123.2 3.2 %shard_map.116 = bf16[32,1536]{1,0:T(8,128)(2,1)S(1)} custom-call(s32[9]{0:T(128)S(1)} %pad_add_fusion.odd_ref, bf16[96,768]{1,0:T(8,128)(2,1)S(1)} %get-tuple-element.120.mine_ref, bf16[96,768]{1,0:T(8,128)(2,1)S(1)} %collective-permute-done.23.other_ref, f32[3,96,1]{2,1,0:T(8,128)S(1)} %squeeze.109.taps_ref, ...), custom_call_target="tpu_custom_call" | custom-call | flops 1000000000 | bytes 4000000 | tf_op jit(solution)/shard_map/pallas_call | solution.py:262
  127.0 2.0 %collective-permute-start.33 = (bf16[32,1536]{1,0:T(8,128)(2,1)S(1)}, bf16[32,1536]{1,0:T(8,128)(2,1)S(1)}, u32[]{:S(2)}, u32[]{:S(2)}) collective-permute-start(bf16[32,1536]{1,0:T(8,128)(2,1)S(1)} %shard_map.116), channel_id=1, source_target_pairs={{0,16},{4,20},{8,24},{12,28},{16,0},{20,4},{24,8},{28,12},{1,17},{... | collective-permute-start | bytes 294920 | tf_op jit(solution)/shard_map/ppermute | solution.py:501
  129.0 1.4 collective-permute-start.34
  131.2 2.1 %collective-permute-start.36 = (bf16[1536,128]{1,0:T(8,128)(2,1)S(1)}, bf16[1536,128]{1,0:T(8,128)(2,1)S(1)}, u32[]{:S(2)}, u32[]{:S(2)}) collective-permute-start(bf16[1536,128]{1,0:T(8,128)(2,1)S(1)} %bitcast.235), channel_id=1, source_target_pairs={{0,2},{1,3},{2,0},{3,1},{4,6},{5,7},{6,4},{7,5},{8,10},{9,11},{10,... | collective-permute-start | bytes 1179656 | tf_op jit(solution)/shard_map/ppermute | solution.py:372
  133.3 1.3 collective-permute-done.33
  135.4 4.9 %collective-permute-done.27 = bf16[4,32,1536]{2,1,0:T(8,128)(2,1)S(1)} collective-permute-done((bf16[4,32,1536]{2,1,0:T(8,128)(2,1)S(1)}, bf16[4,32,1536]{2,1,0:T(8,128)(2,1)S(1)}, u32[]{:S(2)}, u32[]{:S(2)}) %collective-permute-start.27) | collective-permute-done | bytes 393248 | tf_op jit(solution)/shard_map/ppermute | solution.py:504
  141.0 3.5 %collective-permute-done.35 = bf16[4,32,1536]{2,1,0:T(8,128)(2,1)S(1)} collective-permute-done((bf16[4,32,1536]{2,1,0:T(8,128)(2,1)S(1)}, bf16[4,32,1536]{2,1,0:T(8,128)(2,1)S(1)}, u32[]{:S(2)}, u32[]{:S(2)}) %collective-permute-start.35) | collective-permute-done | bytes 393248 | tf_op jit(solution)/shard_map/ppermute | solution.py:504
  145.7 1.3 broadcast_select_fusion.1
  147.2 2.0 %fusion = f32[512,512]{1,0:T(8,128)} fusion(bf16[512,1536]{1,0:T(8,128)(2,1)S(1)} %bitcast.228, bf16[1536,128]{1,0:T(8,128)(2,1)S(1)} %get-tuple-element.73, bf16[1536,128]{1,0:T(8,128)(2,1)S(1)} %get-tuple-element.132, bf16[1536,128]{1,0:T(8,128)(2,1)S(1)} %get-tuple-element.72, bf16[1536,128]{1,0:T(8,128)(2,1)S(1)} %get-tuple-element.133), kind=kOutput, calls=%fused_computation | convolution fusion | flops 811597824 | bytes 4194304 | tf_op jit(solution)/shard_map/dot_general | solution.py:514
  (137 shorter events, 23.7 us)
Async XLA Ops:
  0.6 30.6 %copy-start = (f32[3,3,512]{2,1,0:T(4,128)S(1)}, f32[3,3,512]{2,1,0:T(4,128)}, u32[]{:S(2)}) copy-start(f32[3,3,512]{2,1,0:T(4,128)} %param.12) | copy-start | bytes 55300
  0.6 25.8 %collective-permute-start.3 = (bf16[192,1024]{1,0:T(8,128)(2,1)}, bf16[192,1024]{1,0:T(8,128)(2,1)}, u32[]{:S(2)}, u32[]{:S(2)}) collective-permute-start(bf16[192,1024]{1,0:T(8,128)(2,1)} %param.10), channel_id=1, source_target_pairs={{0,8},{4,12},{8,16},{12,20},{16,24},{20,28},{1,9},{5,13},{9,17},{1... | collective-permute-start | bytes 1179656 | tf_op jit(solution)/shard_map/ppermute | solution.py:374
  6.3 18.9 %collective-permute-start.4 = (bf16[192,1024]{1,0:T(8,128)(2,1)}, bf16[192,1024]{1,0:T(8,128)(2,1)}, u32[]{:S(2)}, u32[]{:S(2)}) collective-permute-start(bf16[192,1024]{1,0:T(8,128)(2,1)} %param.10), channel_id=1, source_target_pairs={{8,0},{12,4},{16,8},{20,12},{24,16},{28,20},{9,1},{13,5},{17,9},{2... | collective-permute-start | bytes 1179656 | tf_op jit(solution)/shard_map/ppermute | solution.py:375
  9.1 10.4 %copy-start.2 = (bf16[192,4096]{1,0:T(8,128)(2,1)S(1)}, bf16[192,4096]{1,0:T(8,128)(2,1)}, u32[]{:S(2)}) copy-start(bf16[192,4096]{1,0:T(8,128)(2,1)} %grad_ref.1) | copy-start | bytes 4718596
  9.1 10.4 %copy-start.3 = (f32[2,192,512]{2,1,0:T(8,128)S(1)}, f32[2,192,512]{2,1,0:T(8,128)}, u32[]{:S(2)}) copy-start(f32[2,192,512]{2,1,0:T(8,128)} %value_ref.1) | copy-start | bytes 2359300
  10.7 20.8 %collective-permute-start = (bf16[384,512]{1,0:T(8,128)(2,1)}, bf16[384,512]{1,0:T(8,128)(2,1)}, u32[]{:S(2)}, u32[]{:S(2)}) collective-permute-start(bf16[384,512]{1,0:T(8,128)(2,1)} %get-tuple-element.32), channel_id=1, source_target_pairs={{0,0},{1,8},{2,16},{3,24},{4,4},{5,12},{6,20},{7,28},{8,1},{9,9},{... | collective-permute-start | bytes 1179656 | tf_op jit(solution)/shard_map/ppermute | solution.py:387
  15.1 19.1 %collective-permute-start.1 = (bf16[384,512]{1,0:T(8,128)(2,1)}, bf16[384,512]{1,0:T(8,128)(2,1)}, u32[]{:S(2)}, u32[]{:S(2)}) collective-permute-start(bf16[384,512]{1,0:T(8,128)(2,1)} %get-tuple-element.33), channel_id=1, source_target_pairs={{0,8},{1,16},{2,24},{3,0},{4,12},{5,20},{6,28},{7,4},{8,9},{9,17},... | collective-permute-start | bytes 1179656 | tf_op jit(solution)/shard_map/ppermute | solution.py:387
  15.3 21.6 %collective-permute-start.2 = (bf16[384,512]{1,0:T(8,128)(2,1)S(1)}, bf16[384,512]{1,0:T(8,128)(2,1)}, u32[]{:S(2)}, u32[]{:S(2)}) collective-permute-start(bf16[384,512]{1,0:T(8,128)(2,1)S(1)} %get-tuple-element.34), channel_id=1, source_target_pairs={{0,16},{1,24},{2,0},{3,8},{4,20},{5,28},{6,4},{7,12},{8,17},{9,25}... | collective-permute-start | bytes 1179656 | tf_op jit(solution)/shard_map/ppermute | solution.py:387
  25.2 16.5 %collective-permute-start.10 = (bf16[192,1024]{1,0:T(8,128)(2,1)}, bf16[192,1024]{1,0:T(8,128)(2,1)}, u32[]{:S(2)}, u32[]{:S(2)}) collective-permute-start(bf16[192,1024]{1,0:T(8,128)(2,1)} %collective-permute-done.4), channel_id=1, source_target_pairs={{8,0},{12,4},{16,8},{20,12},{24,16},{28,20},{9,1},{13,5},{17,9},{2... | collective-permute-start | bytes 1179656 | tf_op jit(solution)/shard_map/ppermute | solution.py:394
  26.5 16.8 %collective-permute-start.12 = (bf16[192,1024]{1,0:T(8,128)(2,1)}, bf16[192,1024]{1,0:T(8,128)(2,1)S(1)}, u32[]{:S(2)}, u32[]{:S(2)}) collective-permute-start(bf16[192,1024]{1,0:T(8,128)(2,1)} %collective-permute-done.3), channel_id=1, source_target_pairs={{0,8},{4,12},{8,16},{12,20},{16,24},{20,28},{1,9},{5,13},{9,17},{1... | collective-permute-start | bytes 1179656 | tf_op jit(solution)/shard_map/ppermute | solution.py:393
  31.5 18.2 %collective-permute-start.5 = (bf16[384,512]{1,0:T(8,128)(2,1)S(1)}, bf16[384,512]{1,0:T(8,128)(2,1)S(1)}, u32[]{:S(2)}, u32[]{:S(2)}) collective-permute-start(bf16[384,512]{1,0:T(8,128)(2,1)S(1)} %get-tuple-element.36), channel_id=1, source_target_pairs={{0,24},{1,0},{2,8},{3,16},{4,28},{5,4},{6,12},{7,20},{8,25},{9,1},... | collective-permute-start | bytes 1179656 | tf_op jit(solution)/shard_map/ppermute | solution.py:387
  34.3 34.3 %collective-permute-start.6 = (bf16[384,512]{1,0:T(8,128)(2,1)}, bf16[384,512]{1,0:T(8,128)(2,1)S(1)}, u32[]{:S(2)}, u32[]{:S(2)}) collective-permute-start(bf16[384,512]{1,0:T(8,128)(2,1)} %collective-permute-done), channel_id=1, source_target_pairs={{0,4},{4,0},{8,12},{12,8},{16,20},{20,16},{24,28},{28,24},{1,5},{5... | collective-permute-start | bytes 1179656 | tf_op jit(solution)/shard_map/ppermute | solution.py:388
  36.9 31.8 %collective-permute-start.7 = (bf16[384,512]{1,0:T(8,128)(2,1)}, bf16[384,512]{1,0:T(8,128)(2,1)S(1)}, u32[]{:S(2)}, u32[]{:S(2)}) collective-permute-start(bf16[384,512]{1,0:T(8,128)(2,1)} %collective-permute-done.1), channel_id=1, source_target_pairs={{0,4},{4,0},{8,12},{12,8},{16,20},{20,16},{24,28},{28,24},{1,5},{5... | collective-permute-start | bytes 1179656 | tf_op jit(solution)/shard_map/ppermute | solution.py:388
  41.7 27.6 %collective-permute-start.8 = (bf16[384,512]{1,0:T(8,128)(2,1)}, bf16[384,512]{1,0:T(8,128)(2,1)S(1)}, u32[]{:S(2)}, u32[]{:S(2)}) collective-permute-start(bf16[384,512]{1,0:T(8,128)(2,1)} %collective-permute-done.2), channel_id=1, source_target_pairs={{0,4},{4,0},{8,12},{12,8},{16,20},{20,16},{24,28},{28,24},{1,5},{5... | collective-permute-start | bytes 1179656 | tf_op jit(solution)/shard_map/ppermute | solution.py:388
  43.3 28.2 %collective-permute-start.11 = (bf16[192,1024]{1,0:T(8,128)(2,1)}, bf16[192,1024]{1,0:T(8,128)(2,1)S(1)}, u32[]{:S(2)}, u32[]{:S(2)}) collective-permute-start(bf16[192,1024]{1,0:T(8,128)(2,1)} %collective-permute-done.10), channel_id=1, source_target_pairs={{8,0},{12,4},{16,8},{20,12},{24,16},{28,20},{9,1},{13,5},{17,9},{2... | collective-permute-start | bytes 1179656 | tf_op jit(solution)/shard_map/ppermute | solution.py:396
  49.7 24.2 %collective-permute-start.13 = (bf16[192,1024]{1,0:T(8,128)(2,1)S(1)}, bf16[192,1024]{1,0:T(8,128)(2,1)S(1)}, u32[]{:S(2)}, u32[]{:S(2)}) collective-permute-start(bf16[192,1024]{1,0:T(8,128)(2,1)S(1)} %collective-permute-done.12), channel_id=1, source_target_pairs={{0,8},{4,12},{8,16},{12,20},{16,24},{20,28},{1,9},{5,13},{9,17},{1... | collective-permute-start | bytes 1179656 | tf_op jit(solution)/shard_map/ppermute | solution.py:395
  68.8 7.8 %collective-permute-start.9 = (bf16[384,512]{1,0:T(8,128)(2,1)S(1)}, bf16[384,512]{1,0:T(8,128)(2,1)S(1)}, u32[]{:S(2)}, u32[]{:S(2)}) collective-permute-start(bf16[384,512]{1,0:T(8,128)(2,1)S(1)} %collective-permute-done.5), channel_id=1, source_target_pairs={{0,4},{4,0},{8,12},{12,8},{16,20},{20,16},{24,28},{28,24},{1,5},{5... | collective-permute-start | bytes 1179656 | tf_op jit(solution)/shard_map/ppermute | solution.py:388
  78.9 14.2 %collective-permute-start.14 = (f32[2,192,768]{2,1,0:T(8,128)}, f32[2,192,768]{2,1,0:T(8,128)}, u32[]{:S(2)}, u32[]{:S(2)}) collective-permute-start(f32[2,192,768]{2,1,0:T(8,128)} %fusion.9), channel_id=1, source_target_pairs={{0,1},{1,0},{2,3},{3,2},{4,5},{5,4},{6,7},{7,6},{8,9},{9,8},{10,11... | collective-permute-start | bytes 3538952 | tf_op jit(solution)/shard_map/ppermute | solution.py:372
  80.8 14.6 %collective-permute-start.21 = (f32[2,192,768]{2,1,0:T(8,128)}, f32[2,192,768]{2,1,0:T(8,128)}, u32[]{:S(2)}, u32[]{:S(2)}) collective-permute-start(f32[2,192,768]{2,1,0:T(8,128)} %fusion.8), channel_id=1, source_target_pairs={{0,1},{1,0},{2,3},{3,2},{4,5},{5,4},{6,7},{7,6},{8,9},{9,8},{10,11... | collective-permute-start | bytes 3538952 | tf_op jit(solution)/shard_map/ppermute | solution.py:372
  83.7 11.7 %copy-start.8 = (f32[384,768]{1,0:T(8,128)}, f32[384,768]{1,0:T(8,128)S(1)}, u32[]{:S(2)}) copy-start(f32[384,768]{1,0:T(8,128)S(1)} %fusion.57) | copy-start | bytes 3538948
  83.7 4.1 %copy-start.12 = (bf16[2,192,128]{2,1,0:T(8,128)(2,1)S(1)}, bf16[2,192,128]{2,1,0:T(8,128)(2,1)}, u32[]{:S(2)}) copy-start(bf16[2,192,128]{2,1,0:T(8,128)(2,1)} %get-tuple-element.42) | copy-start | bytes 294916
  83.7 7.4 %copy-start.11 = (bf16[2,192,128]{2,1,0:T(8,128)(2,1)S(1)}, bf16[2,192,128]{2,1,0:T(8,128)(2,1)}, u32[]{:S(2)}) copy-start(bf16[2,192,128]{2,1,0:T(8,128)(2,1)} %get-tuple-element.44) | copy-start | bytes 294916
  84.7 12.8 %collective-permute-start.17 = (bf16[2,192,128]{2,1,0:T(8,128)(2,1)S(1)}, bf16[2,192,128]{2,1,0:T(8,128)(2,1)S(1)}, u32[]{:S(2)}, u32[]{:S(2)}) collective-permute-start(bf16[2,192,128]{2,1,0:T(8,128)(2,1)S(1)} %copy-done.13), channel_id=1, source_target_pairs={{0,24},{4,28},{8,0},{12,4},{16,8},{20,12},{24,16},{28,20},{1,25},{... | collective-permute-start | bytes 294920 | tf_op jit(solution)/shard_map/ppermute | solution.py:409
  87.8 12.5 %collective-permute-start.18 = (bf16[2,192,128]{2,1,0:T(8,128)(2,1)S(1)}, bf16[2,192,128]{2,1,0:T(8,128)(2,1)S(1)}, u32[]{:S(2)}, u32[]{:S(2)}) collective-permute-start(bf16[2,192,128]{2,1,0:T(8,128)(2,1)S(1)} %copy-done.12), channel_id=1, source_target_pairs={{0,16},{4,20},{8,24},{12,28},{16,0},{20,4},{24,8},{28,12},{1,17},{... | collective-permute-start | bytes 294920 | tf_op jit(solution)/shard_map/ppermute | solution.py:409
  91.2 9.1 %collective-permute-start.19 = (bf16[2,192,128]{2,1,0:T(8,128)(2,1)S(1)}, bf16[2,192,128]{2,1,0:T(8,128)(2,1)S(1)}, u32[]{:S(2)}, u32[]{:S(2)}) collective-permute-start(bf16[2,192,128]{2,1,0:T(8,128)(2,1)S(1)} %copy-done.11), channel_id=1, source_target_pairs={{0,8},{4,12},{8,16},{12,20},{16,24},{20,28},{24,0},{28,4},{1,9},{5... | collective-permute-start | bytes 294920 | tf_op jit(solution)/shard_map/ppermute | solution.py:409
  94.2 10.0 %collective-permute-start.15 = (bf16[192,768]{1,0:T(8,128)(2,1)S(1)}, bf16[192,768]{1,0:T(8,128)(2,1)S(1)}, u32[]{:S(2)}, u32[]{:S(2)}) collective-permute-start(bf16[192,768]{1,0:T(8,128)(2,1)S(1)} %fusion.16), channel_id=1, source_target_pairs={{0,2},{1,3},{2,0},{3,1},{4,6},{5,7},{6,4},{7,5},{8,10},{9,11},{10,... | collective-permute-start | bytes 884744 | tf_op jit(solution)/shard_map/ppermute | solution.py:372
  96.6 14.5 %collective-permute-start.22 = (bf16[192,768]{1,0:T(8,128)(2,1)S(1)}, bf16[192,768]{1,0:T(8,128)(2,1)S(1)}, u32[]{:S(2)}, u32[]{:S(2)}) collective-permute-start(bf16[192,768]{1,0:T(8,128)(2,1)S(1)} %fusion.11), channel_id=1, source_target_pairs={{0,2},{1,3},{2,0},{3,1},{4,6},{5,7},{6,4},{7,5},{8,10},{9,11},{10,... | collective-permute-start | bytes 884744 | tf_op jit(solution)/shard_map/ppermute | solution.py:372
  100.3 10.1 %copy-start.10 = (bf16[2,192,128]{2,1,0:T(8,128)(2,1)S(1)}, bf16[2,192,128]{2,1,0:T(8,128)(2,1)}, u32[]{:S(2)}) copy-start(bf16[2,192,128]{2,1,0:T(8,128)(2,1)} %get-tuple-element.54) | copy-start | bytes 294916
  100.4 10.8 %copy-start.9 = (f32[384,768]{1,0:T(8,128)S(1)}, f32[384,768]{1,0:T(8,128)}, u32[]{:S(2)}) copy-start(f32[384,768]{1,0:T(8,128)} %copy-done.8) | copy-start | bytes 3538948
  100.4 10.1 %collective-permute-start.20 = (bf16[4,192,128]{2,1,0:T(8,128)(2,1)S(1)}, bf16[4,192,128]{2,1,0:T(8,128)(2,1)S(1)}, u32[]{:S(2)}, u32[]{:S(2)}) collective-permute-start(bf16[4,192,128]{2,1,0:T(8,128)(2,1)S(1)} %get-tuple-element.106), channel_id=1, source_target_pairs={{0,4},{4,0},{8,12},{12,8},{16,20},{20,16},{24,28},{28,24},{1,5},{5... | collective-permute-start | bytes 589832 | tf_op jit(solution)/shard_map/ppermute | solution.py:447
  105.4 5.8 %collective-permute-start.16 = (bf16[96,768]{1,0:T(8,128)(2,1)S(1)}, bf16[96,768]{1,0:T(8,128)(2,1)S(1)}, u32[]{:S(2)}, u32[]{:S(2)}) collective-permute-start(bf16[96,768]{1,0:T(8,128)(2,1)S(1)} %get-tuple-element.122), channel_id=1, source_target_pairs={{0,4},{4,0},{8,12},{12,8},{16,20},{20,16},{24,28},{28,24},{1,5},{5... | collective-permute-start | bytes 442376 | tf_op jit(solution)/shard_map/ppermute | solution.py:471
  107.4 11.7 %collective-permute-start.28 = (bf16[2,192,128]{2,1,0:T(8,128)(2,1)}, bf16[2,192,128]{2,1,0:T(8,128)(2,1)S(1)}, u32[]{:S(2)}, u32[]{:S(2)}) collective-permute-start(bf16[2,192,128]{2,1,0:T(8,128)(2,1)} %get-tuple-element.52), channel_id=1, source_target_pairs={{0,24},{4,28},{8,0},{12,4},{16,8},{20,12},{24,16},{28,20},{1,25},{... | collective-permute-start | bytes 294920 | tf_op jit(solution)/shard_map/ppermute | solution.py:409
  110.5 9.8 %collective-permute-start.29 = (bf16[2,192,128]{2,1,0:T(8,128)(2,1)S(1)}, bf16[2,192,128]{2,1,0:T(8,128)(2,1)S(1)}, u32[]{:S(2)}, u32[]{:S(2)}) collective-permute-start(bf16[2,192,128]{2,1,0:T(8,128)(2,1)S(1)} %copy-done.10), channel_id=1, source_target_pairs={{0,16},{4,20},{8,24},{12,28},{16,0},{20,4},{24,8},{28,12},{1,17},{... | collective-permute-start | bytes 294920 | tf_op jit(solution)/shard_map/ppermute | solution.py:409
  110.5 11.1 %collective-permute-start.30 = (bf16[2,192,128]{2,1,0:T(8,128)(2,1)S(1)}, bf16[2,192,128]{2,1,0:T(8,128)(2,1)S(1)}, u32[]{:S(2)}, u32[]{:S(2)}) collective-permute-start(bf16[2,192,128]{2,1,0:T(8,128)(2,1)S(1)} %get-tuple-element.56), channel_id=1, source_target_pairs={{0,8},{4,12},{8,16},{12,20},{16,24},{20,28},{24,0},{28,4},{1,9},{5... | collective-permute-start | bytes 294920 | tf_op jit(solution)/shard_map/ppermute | solution.py:409
  111.1 2.3 %copy-start.4 = (f32[192,512]{1,0:T(8,128)S(1)}, f32[192,512]{1,0:T(8,128)}, u32[]{:S(2)}) copy-start(f32[192,512]{1,0:T(8,128)} %constant.269.clone.table_ref) | copy-start | bytes 1179652
  111.1 2.3 %copy-start.5 = (f32[2,5,192]{2,1,0:T(8,128)S(1)}, f32[2,5,192]{2,1,0:T(8,128)}, u32[]{:S(2)}) copy-start(f32[2,5,192]{2,1,0:T(8,128)} %constant.270.clone.turn_ref) | copy-start | bytes 23044
  112.4 10.8 %collective-permute-start.23 = (bf16[96,768]{1,0:T(8,128)(2,1)S(1)}, bf16[96,768]{1,0:T(8,128)(2,1)S(1)}, u32[]{:S(2)}, u32[]{:S(2)}) collective-permute-start(bf16[96,768]{1,0:T(8,128)(2,1)S(1)} %get-tuple-element.121), channel_id=1, source_target_pairs={{0,4},{4,0},{8,12},{12,8},{16,20},{20,16},{24,28},{28,24},{1,5},{5... | collective-permute-start | bytes 442376 | tf_op jit(solution)/shard_map/ppermute | solution.py:471
  116.6 10.4 %collective-permute-start.24 = (bf16[32,1536]{1,0:T(8,128)(2,1)S(1)}, bf16[32,1536]{1,0:T(8,128)(2,1)S(1)}, u32[]{:S(2)}, u32[]{:S(2)}) collective-permute-start(bf16[32,1536]{1,0:T(8,128)(2,1)S(1)} %shard_map.115), channel_id=1, source_target_pairs={{0,8},{4,12},{8,16},{12,20},{16,24},{20,28},{24,0},{28,4},{1,9},{5... | collective-permute-start | bytes 294920 | tf_op jit(solution)/shard_map/ppermute | solution.py:501
  119.1 9.9 %collective-permute-start.25 = (bf16[32,1536]{1,0:T(8,128)(2,1)S(1)}, bf16[32,1536]{1,0:T(8,128)(2,1)S(1)}, u32[]{:S(2)}, u32[]{:S(2)}) collective-permute-start(bf16[32,1536]{1,0:T(8,128)(2,1)S(1)} %shard_map.115), channel_id=1, source_target_pairs={{0,16},{4,20},{8,24},{12,28},{16,0},{20,4},{24,8},{28,12},{1,17},{... | collective-permute-start | bytes 294920 | tf_op jit(solution)/shard_map/ppermute | solution.py:501
  120.2 10.1 %collective-permute-start.26 = (bf16[32,1536]{1,0:T(8,128)(2,1)S(1)}, bf16[32,1536]{1,0:T(8,128)(2,1)S(1)}, u32[]{:S(2)}, u32[]{:S(2)}) collective-permute-start(bf16[32,1536]{1,0:T(8,128)(2,1)S(1)} %shard_map.115), channel_id=1, source_target_pairs={{0,24},{4,28},{8,0},{12,4},{16,8},{20,12},{24,16},{28,20},{1,25},{... | collective-permute-start | bytes 294920 | tf_op jit(solution)/shard_map/ppermute | solution.py:501
  121.6 9.4 %collective-permute-start.31 = (bf16[4,192,128]{2,1,0:T(8,128)(2,1)S(1)}, bf16[4,192,128]{2,1,0:T(8,128)(2,1)S(1)}, u32[]{:S(2)}, u32[]{:S(2)}) collective-permute-start(bf16[4,192,128]{2,1,0:T(8,128)(2,1)S(1)} %dynamic-slice_bitcast_fusion.1), channel_id=1, source_target_pairs={{0,4},{4,0},{8,12},{12,8},{16,20},{20,16},{24,28},{28,24},{1,5},{5... | collective-permute-start | bytes 589832 | tf_op jit(solution)/shard_map/ppermute | solution.py:447
  126.4 6.9 %collective-permute-start.32 = (bf16[32,1536]{1,0:T(8,128)(2,1)S(1)}, bf16[32,1536]{1,0:T(8,128)(2,1)S(1)}, u32[]{:S(2)}, u32[]{:S(2)}) collective-permute-start(bf16[32,1536]{1,0:T(8,128)(2,1)S(1)} %shard_map.116), channel_id=1, source_target_pairs={{0,8},{4,12},{8,16},{12,20},{16,24},{20,28},{24,0},{28,4},{1,9},{5... | collective-permute-start | bytes 294920 | tf_op jit(solution)/shard_map/ppermute | solution.py:501
  127.0 7.6 %collective-permute-start.33 = (bf16[32,1536]{1,0:T(8,128)(2,1)S(1)}, bf16[32,1536]{1,0:T(8,128)(2,1)S(1)}, u32[]{:S(2)}, u32[]{:S(2)}) collective-permute-start(bf16[32,1536]{1,0:T(8,128)(2,1)S(1)} %shard_map.116), channel_id=1, source_target_pairs={{0,16},{4,20},{8,24},{12,28},{16,0},{20,4},{24,8},{28,12},{1,17},{... | collective-permute-start | bytes 294920 | tf_op jit(solution)/shard_map/ppermute | solution.py:501
  129.0 5.7 %collective-permute-start.34 = (bf16[32,1536]{1,0:T(8,128)(2,1)S(1)}, bf16[32,1536]{1,0:T(8,128)(2,1)S(1)}, u32[]{:S(2)}, u32[]{:S(2)}) collective-permute-start(bf16[32,1536]{1,0:T(8,128)(2,1)S(1)} %shard_map.116), channel_id=1, source_target_pairs={{0,24},{4,28},{8,0},{12,4},{16,8},{20,12},{24,16},{28,20},{1,25},{... | collective-permute-start | bytes 294920 | tf_op jit(solution)/shard_map/ppermute | solution.py:501
  130.4 9.9 %collective-permute-start.27 = (bf16[4,32,1536]{2,1,0:T(8,128)(2,1)S(1)}, bf16[4,32,1536]{2,1,0:T(8,128)(2,1)S(1)}, u32[]{:S(2)}, u32[]{:S(2)}) collective-permute-start(bf16[4,32,1536]{2,1,0:T(8,128)(2,1)S(1)} %pad_maximum_fusion.2), channel_id=1, source_target_pairs={{0,4},{4,0},{8,12},{12,8},{16,20},{20,16},{24,28},{28,24},{1,5},{5... | collective-permute-start | bytes 1179656 | tf_op jit(solution)/shard_map/ppermute | solution.py:504
  131.2 9.5 %collective-permute-start.36 = (bf16[1536,128]{1,0:T(8,128)(2,1)S(1)}, bf16[1536,128]{1,0:T(8,128)(2,1)S(1)}, u32[]{:S(2)}, u32[]{:S(2)}) collective-permute-start(bf16[1536,128]{1,0:T(8,128)(2,1)S(1)} %bitcast.235), channel_id=1, source_target_pairs={{0,2},{1,3},{2,0},{3,1},{4,6},{5,7},{6,4},{7,5},{8,10},{9,11},{10,... | collective-permute-start | bytes 1179656 | tf_op jit(solution)/shard_map/ppermute | solution.py:372
  134.7 9.8 %collective-permute-start.35 = (bf16[4,32,1536]{2,1,0:T(8,128)(2,1)S(1)}, bf16[4,32,1536]{2,1,0:T(8,128)(2,1)S(1)}, u32[]{:S(2)}, u32[]{:S(2)}) collective-permute-start(bf16[4,32,1536]{2,1,0:T(8,128)(2,1)S(1)} %pad_maximum_fusion.4), channel_id=1, source_target_pairs={{0,4},{4,0},{8,12},{12,8},{16,20},{20,16},{24,28},{28,24},{1,5},{5... | collective-permute-start | bytes 1179656 | tf_op jit(solution)/shard_map/ppermute | solution.py:504
  140.9 4.8 %collective-permute-start.37 = (bf16[2,1536,128]{2,1,0:T(8,128)(2,1)S(1)}, bf16[2,1536,128]{2,1,0:T(8,128)(2,1)}, u32[]{:S(2)}, u32[]{:S(2)}) collective-permute-start(bf16[2,1536,128]{2,1,0:T(8,128)(2,1)S(1)} %pad_maximum_fusion), channel_id=1, source_target_pairs={{0,1},{1,0},{2,3},{3,2},{4,5},{5,4},{6,7},{7,6},{8,9},{9,8},{10,11... | collective-permute-start | bytes 2359304 | tf_op jit(solution)/shard_map/ppermute | solution.py:372
  (6 other events, 8.4 us)
